TPU v7x, 32 devices: a whole 2x2x4 slice. The times are simulated.
32 devices in a mesh: batch: 8 (over z, x), lat: 4 (over y, core).
Axes of the slice: x: 2, y: 2, z: 4, core: 2. Of those that a mesh axis runs over, the one named last changes fastest.
Arguments:
- observations: bfloat16 [6144, 4, 39], P(('batch', 'lat')), may hold values from -6 to 6
- actions: bfloat16 [6144, 3, 6], P(('batch', 'lat')), may hold values from -1 to 1
- task_ids: int32 [6144], P(('batch', 'lat')), may hold values from 0 to 79
- counts: int32 [80], replicated, may hold values from 1 to 8192, as said below
- reward_bins: int32 [6144, 3], P(('batch', 'lat')), may hold values from 0 to 100
- value_bins: int32 [6144, 3], P(('batch', 'lat')), may hold values from 0 to 100
- encoder_in: bfloat16 [39, 1024], P(None, 'lat'), may hold values from -1 to 1
- latent_out: bfloat16 [2, 1024, 768], P(None, 'batch', 'lat'), may hold values from -0.375 to 0.375
- head_latent: bfloat16 [8, 768, 1024], P(None, 'batch', 'lat'), may hold values from -0.875 to 0.875
- head_action: bfloat16 [7, 6, 1024], P(None, None, 'lat'), may hold values from -2.5 to 2.5
- head_task: bfloat16 [8, 96, 1024], P(None, 'batch', 'lat'), may hold values from -0.625 to 0.625
- head_middle: bfloat16 [8, 1024, 1024], P(None, 'batch', 'lat'), may hold values from -0.1875 to 0.1875
- value_out: bfloat16 [6, 1024, 101], P(None, 'batch'), may hold values from -0.375 to 0.375
- policy_out: bfloat16 [1024, 12], P('batch'), may hold values from -0.1875 to 0.1875
- task_table: bfloat16 [80, 96], P('batch', 'lat'), may hold values from -6 to 6
- norm_gain: bfloat16 [17, 1024], P(None, 'lat'), may hold values from 0.5 to 1.5
- norm_shift: bfloat16 [17, 1024], P(None, 'lat'), may hold values from -3 to 3
- latent_bias: bfloat16 [2, 768], P(None, 'lat'), may hold values from -3 to 3
- value_bias: bfloat16 [6, 101], replicated, may hold values from -3 to 3
- policy_bias: bfloat16 [12], replicated, may hold values from -3 to 3
Outputs:
- grad_observations: float32 [6144, 4, 39], P(('batch', 'lat'))
- grad_encoder_in: float32 [39, 1024], P(None, 'lat')
- grad_latent_out: float32 [2, 1024, 768], P(None, 'batch', 'lat')
- grad_head_latent: float32 [8, 768, 1024], P(None, 'batch', 'lat')
- grad_head_action: float32 [7, 6, 1024], P(None, None, 'lat')
- grad_head_task: float32 [8, 96, 1024], P(None, 'batch', 'lat')
- grad_head_middle: float32 [8, 1024, 1024], P(None, 'batch', 'lat')
- grad_value_out: float32 [6, 1024, 101], P(None, 'batch')
- grad_policy_out: float32 [1024, 12], P('batch')
- grad_task_table: float32 [80, 96], P('batch', 'lat')
- grad_norm_gain: float32 [17, 1024], P(None, 'lat')
- grad_norm_shift: float32 [17, 1024], P(None, 'lat')
- grad_latent_bias: float32 [2, 768], P(None, 'lat')
- grad_value_bias: float32 [6, 101], replicated
- grad_policy_bias: float32 [12], replicated
Inputs may be any that keep to these rules, and one draw needn't show every extreme that they name: `counts`: each count is a power of two or twice one; some task has exactly 8192.
All inputs are finite; a program needn't handle non-finite values.
Results may differ from a plain program's by a relative error of at most 0.015.
Values may be sent and summed in bfloat16 or wider, within the bound.
A program may use at most 384 MiB of HBM per device.

v0:
```python
from functools import reduce
import math

import jax
import jax.numpy as jnp
from jax import lax
from jax.sharding import PartitionSpec as P

SIMNORM = 8


LOG_STD_LO = -2.0
LOG_STD_HI = 2.0
HIGHEST = lax.Precision.HIGHEST


def product32(left, right):
    return jnp.dot(left, right, preferred_element_type=jnp.float32)


def contract(form, left, right):
    return jnp.einsum(form, left, right, preferred_element_type=jnp.float32)


def mish_act(values):
    return values * jnp.tanh(jax.nn.softplus(values))


def norm_act(preact, gain, shift):
    centered = preact - jnp.mean(preact, -1, keepdims=True)
    variance = jnp.mean(centered * centered, -1, keepdims=True)
    return mish_act(centered * lax.rsqrt(variance + 1e-05) * gain + shift)


def simnorm(values):
    groups = values.reshape(values.shape[:-1] + (values.shape[-1] // SIMNORM, SIMNORM))
    return jax.nn.softmax(groups, -1).reshape(values.shape)


def heads_loss(
    logits, policy_lin, predicted, targets, action_rows, row_weight, reward_hot, value_hot
):
    seq_count = predicted.shape[0]
    horizon = predicted.shape[1]
    act_dim = action_rows.shape[1]
    log_total = jax.nn.logsumexp(logits, -1)
    reward_ce = log_total[0] - jnp.sum(logits[0] * reward_hot, -1)
    value_ce = jnp.mean(log_total[1:] - jnp.sum(logits[1:] * value_hot[None], -1), 0)
    pi_mean = jnp.tanh(policy_lin[:, :act_dim])
    log_std = LOG_STD_LO + 0.5 * (LOG_STD_HI - LOG_STD_LO) * (
        jnp.tanh(policy_lin[:, act_dim:]) + 1.0
    )
    neg_loglik = jnp.sum(
        0.5 * jnp.square((action_rows - pi_mean) * jnp.exp(-log_std)) + log_std, -1
    )
    per_row = (0.1 * (reward_ce + value_ce + neg_loglik)).reshape(seq_count, horizon)
    consistency = 20.0 * jnp.mean(jnp.square(predicted - targets), -1)
    discount = jnp.power(0.5, jnp.arange(horizon).astype(jnp.float32))
    return jnp.sum(jnp.sum((per_row + consistency) * discount, -1) * row_weight)


def through_lat(members):
    (
        encoder_in,
        latent_out,
        head_latent,
        head_action,
        head_task,
        head_middle,
        value_out,
        policy_out,
        task_table,
        norm_gain,
        norm_shift,
        latent_bias,
        value_bias,
        policy_bias,
    ) = members
    (
        encoder_in,
        latent_out,
        head_latent,
        head_action,
        head_task,
        head_middle,
        task_table,
        norm_gain,
        norm_shift,
        latent_bias,
    ) = (
        lax.all_gather(encoder_in, "lat", axis=1, tiled=True),
        lax.all_gather(latent_out, "lat", axis=2, tiled=True),
        lax.all_gather(head_latent, "lat", axis=2, tiled=True),
        lax.all_gather(head_action, "lat", axis=2, tiled=True),
        lax.all_gather(head_task, "lat", axis=2, tiled=True),
        lax.all_gather(head_middle, "lat", axis=2, tiled=True),
        lax.all_gather(task_table, "lat", axis=1, tiled=True),
        lax.all_gather(norm_gain, "lat", axis=1, tiled=True),
        lax.all_gather(norm_shift, "lat", axis=1, tiled=True),
        lax.all_gather(latent_bias, "lat", axis=1, tiled=True),
    )
    return (
        encoder_in,
        latent_out,
        head_latent,
        head_action,
        head_task,
        head_middle,
        value_out,
        policy_out,
        task_table,
        norm_gain,
        norm_shift,
        latent_bias,
        value_bias,
        policy_bias,
    )


def through_batch(members):
    (
        encoder_in,
        latent_out,
        head_latent,
        head_action,
        head_task,
        head_middle,
        value_out,
        policy_out,
        task_table,
        norm_gain,
        norm_shift,
        latent_bias,
        value_bias,
        policy_bias,
    ) = members
    latent_out, head_latent, head_task, head_middle, value_out, policy_out, task_table = (
        lax.all_gather(latent_out, "batch", axis=1, tiled=True),
        lax.all_gather(head_latent, "batch", axis=1, tiled=True),
        lax.all_gather(head_task, "batch", axis=1, tiled=True),
        lax.all_gather(head_middle, "batch", axis=1, tiled=True),
        lax.all_gather(value_out, "batch", axis=1, tiled=True),
        lax.all_gather(policy_out, "batch", axis=0, tiled=True),
        lax.all_gather(task_table, "batch", axis=0, tiled=True),
    )
    return (
        encoder_in,
        latent_out,
        head_latent,
        head_action,
        head_task,
        head_middle,
        value_out,
        policy_out,
        task_table,
        norm_gain,
        norm_shift,
        latent_bias,
        value_bias,
        policy_bias,
    )


def reduce_batch(grads):
    (
        encoder_in,
        latent_out,
        head_latent,
        head_action,
        head_task,
        head_middle,
        value_out,
        policy_out,
        task_table,
        norm_gain,
        norm_shift,
        latent_bias,
        value_bias,
        policy_bias,
    ) = grads
    latent_out, head_latent, head_task, head_middle, value_out, policy_out, task_table = (
        lax.psum_scatter(
            latent_out.astype(jnp.bfloat16), "batch", scatter_dimension=1, tiled=True
        ).astype(jnp.float32),
        lax.psum_scatter(
            head_latent.astype(jnp.bfloat16), "batch", scatter_dimension=1, tiled=True
        ).astype(jnp.float32),
        lax.psum_scatter(
            head_task.astype(jnp.bfloat16), "batch", scatter_dimension=1, tiled=True
        ).astype(jnp.float32),
        lax.psum_scatter(
            head_middle.astype(jnp.bfloat16), "batch", scatter_dimension=1, tiled=True
        ).astype(jnp.float32),
        lax.psum_scatter(
            value_out.astype(jnp.bfloat16), "batch", scatter_dimension=1, tiled=True
        ).astype(jnp.float32),
        lax.psum_scatter(
            policy_out.astype(jnp.bfloat16), "batch", scatter_dimension=0, tiled=True
        ).astype(jnp.float32),
        lax.psum_scatter(
            task_table.astype(jnp.bfloat16), "batch", scatter_dimension=0, tiled=True
        ).astype(jnp.float32),
    )
    encoder_in, head_action, norm_gain, norm_shift, latent_bias, value_bias, policy_bias = (
        lax.psum(encoder_in.astype(jnp.bfloat16), "batch").astype(jnp.float32),
        lax.psum(head_action.astype(jnp.bfloat16), "batch").astype(jnp.float32),
        lax.psum(norm_gain.astype(jnp.bfloat16), "batch").astype(jnp.float32),
        lax.psum(norm_shift.astype(jnp.bfloat16), "batch").astype(jnp.float32),
        lax.psum(latent_bias.astype(jnp.bfloat16), "batch").astype(jnp.float32),
        lax.psum(value_bias.astype(jnp.bfloat16), "batch").astype(jnp.float32),
        lax.psum(policy_bias.astype(jnp.bfloat16), "batch").astype(jnp.float32),
    )
    return (
        encoder_in,
        latent_out,
        head_latent,
        head_action,
        head_task,
        head_middle,
        value_out,
        policy_out,
        task_table,
        norm_gain,
        norm_shift,
        latent_bias,
        value_bias,
        policy_bias,
    )


def reduce_lat(grads):
    (
        encoder_in,
        latent_out,
        head_latent,
        head_action,
        head_task,
        head_middle,
        value_out,
        policy_out,
        task_table,
        norm_gain,
        norm_shift,
        latent_bias,
        value_bias,
        policy_bias,
    ) = grads
    (
        encoder_in,
        latent_out,
        head_latent,
        head_action,
        head_task,
        head_middle,
        task_table,
        norm_gain,
        norm_shift,
        latent_bias,
    ) = (
        lax.psum_scatter(
            encoder_in.astype(jnp.bfloat16), "lat", scatter_dimension=1, tiled=True
        ).astype(jnp.float32),
        lax.psum_scatter(
            latent_out.astype(jnp.bfloat16), "lat", scatter_dimension=2, tiled=True
        ).astype(jnp.float32),
        lax.psum_scatter(
            head_latent.astype(jnp.bfloat16), "lat", scatter_dimension=2, tiled=True
        ).astype(jnp.float32),
        lax.psum_scatter(
            head_action.astype(jnp.bfloat16), "lat", scatter_dimension=2, tiled=True
        ).astype(jnp.float32),
        lax.psum_scatter(
            head_task.astype(jnp.bfloat16), "lat", scatter_dimension=2, tiled=True
        ).astype(jnp.float32),
        lax.psum_scatter(
            head_middle.astype(jnp.bfloat16), "lat", scatter_dimension=2, tiled=True
        ).astype(jnp.float32),
        lax.psum_scatter(
            task_table.astype(jnp.bfloat16), "lat", scatter_dimension=1, tiled=True
        ).astype(jnp.float32),
        lax.psum_scatter(
            norm_gain.astype(jnp.bfloat16), "lat", scatter_dimension=1, tiled=True
        ).astype(jnp.float32),
        lax.psum_scatter(
            norm_shift.astype(jnp.bfloat16), "lat", scatter_dimension=1, tiled=True
        ).astype(jnp.float32),
        lax.psum_scatter(
            latent_bias.astype(jnp.bfloat16), "lat", scatter_dimension=1, tiled=True
        ).astype(jnp.float32),
    )
    value_out, policy_out, value_bias, policy_bias = (
        lax.psum(value_out.astype(jnp.bfloat16), "lat").astype(jnp.float32),
        lax.psum(policy_out.astype(jnp.bfloat16), "lat").astype(jnp.float32),
        lax.psum(value_bias.astype(jnp.bfloat16), "lat").astype(jnp.float32),
        lax.psum(policy_bias.astype(jnp.bfloat16), "lat").astype(jnp.float32),
    )
    return (
        encoder_in,
        latent_out,
        head_latent,
        head_action,
        head_task,
        head_middle,
        value_out,
        policy_out,
        task_table,
        norm_gain,
        norm_shift,
        latent_bias,
        value_bias,
        policy_bias,
    )


def gather_all(members):
    return through_batch(through_lat(members))


def reduce_all(grads):
    return reduce_lat(reduce_batch(grads))


def local(
    observations,
    actions,
    task_ids,
    counts,
    reward_bins,
    value_bins,
    encoder_in,
    latent_out,
    head_latent,
    head_action,
    head_task,
    head_middle,
    value_out,
    policy_out,
    task_table,
    norm_gain,
    norm_shift,
    latent_bias,
    value_bias,
    policy_bias,
):
    (
        encoder_in,
        latent_out,
        head_latent,
        head_action,
        head_task,
        head_middle,
        value_out,
        policy_out,
        task_table,
        norm_gain,
        norm_shift,
        latent_bias,
        value_bias,
        policy_bias,
    ) = gather_all(
        (
            encoder_in,
            latent_out,
            head_latent,
            head_action,
            head_task,
            head_middle,
            value_out,
            policy_out,
            task_table,
            norm_gain,
            norm_shift,
            latent_bias,
            value_bias,
            policy_bias,
        )
    )
    bf16 = jnp.bfloat16
    seq_count = observations.shape[0]
    horizon = actions.shape[1]
    obs_dim = observations.shape[2]
    act_dim = actions.shape[2]
    latent_dim = head_latent.shape[1]
    hidden_dim = head_latent.shape[2]
    num_tasks = task_table.shape[0]
    num_bins = value_out.shape[2]
    extra_heads = head_latent.shape[0] - 1
    row_count = seq_count * horizon
    gain_full = norm_gain.astype(jnp.float32)
    shift_full = norm_shift.astype(jnp.float32)
    all_seqs = seq_count * lax.axis_size("batch") * lax.axis_size("lat")
    task_hot = (task_ids[:, None] == jnp.arange(num_tasks)[None, :]).astype(jnp.float32)
    task_counts = jnp.sum(task_hot * counts.astype(jnp.float32)[None, :], 1)
    row_weight = 64.0 * lax.rsqrt(task_counts) * (1.0 / math.sqrt(all_seqs))
    flat_obs = observations.reshape(seq_count * (horizon + 1), obs_dim)
    enc_pre = product32(flat_obs, encoder_in)
    enc_hidden = norm_act(enc_pre, gain_full[0], shift_full[0]).astype(bf16)
    enc_lin = product32(enc_hidden, latent_out[0]) + latent_bias[0].astype(jnp.float32)
    encoded, enc_soft_back = jax.vjp(simnorm, enc_lin)
    encoded = encoded.reshape(seq_count, horizon + 1, latent_dim)
    embedded = product32(task_hot.astype(bf16), task_table).astype(bf16)
    task_terms = contract("se,kef->ksf", embedded, head_task)
    state_low = [encoded[:, 0].astype(bf16)]
    predicted = []
    dyn_saved = []
    for moment in range(horizon):
        first_pre = (
            product32(state_low[moment], head_latent[0])
            + product32(actions[:, moment], head_action[0])
            + task_terms[0]
        )
        first_hidden = norm_act(first_pre, gain_full[1], shift_full[1]).astype(bf16)
        second_pre = product32(first_hidden, head_middle[0])
        second_hidden = norm_act(second_pre, gain_full[2], shift_full[2]).astype(bf16)
        dyn_lin = product32(second_hidden, latent_out[1]) + latent_bias[1].astype(jnp.float32)
        next_state = simnorm(dyn_lin)
        predicted.append(next_state)
        dyn_saved.append((first_pre, first_hidden, second_pre, second_hidden, dyn_lin))
        if moment + 1 < horizon:
            state_low.append(next_state.astype(bf16))
    state_rows = jnp.stack(state_low, 1).reshape(row_count, latent_dim)
    action_rows = actions.reshape(row_count, act_dim)
    action_terms = contract("ra,kaf->krf", action_rows, head_action[1:])
    action_terms = jnp.concatenate(
        [action_terms, jnp.zeros((1, row_count, hidden_dim), jnp.float32)], 0
    )
    task_rows = jnp.repeat(task_terms[1:], horizon, axis=1)
    first_gain = gain_full[3::2][:, None]
    first_shift = shift_full[3::2][:, None]
    second_gain = gain_full[4::2][:, None]
    second_shift = shift_full[4::2][:, None]
    head_pre = contract("rl,klf->krf", state_rows, head_latent[1:]) + action_terms + task_rows
    head_hidden = norm_act(head_pre, first_gain, first_shift).astype(bf16)
    head_pre2 = contract("krf,kfg->krg", head_hidden, head_middle[1:])
    head_hidden2 = norm_act(head_pre2, second_gain, second_shift).astype(bf16)
    value_logits = (
        contract("krf,kfc->krc", head_hidden2[:-1], value_out)
        + value_bias.astype(jnp.float32)[:, None]
    )
    policy_lin = product32(head_hidden2[-1], policy_out) + policy_bias.astype(jnp.float32)
    reward_hot = (reward_bins.reshape(row_count)[:, None] == jnp.arange(num_bins)[None, :]).astype(
        jnp.float32
    )
    value_hot = (value_bins.reshape(row_count)[:, None] == jnp.arange(num_bins)[None, :]).astype(
        jnp.float32
    )
    action_float = action_rows.astype(jnp.float32)

    def local_loss(logits, lin_values, pred_values, target_values):
        return heads_loss(
            logits,
            lin_values,
            pred_values,
            target_values,
            action_float,
            row_weight,
            reward_hot,
            value_hot,
        )

    _, loss_backward = jax.vjp(
        local_loss, value_logits, policy_lin, jnp.stack(predicted, 1), encoded[:, 1:]
    )
    d_logits, d_policy, d_predicted, d_targets = loss_backward(jnp.ones((), jnp.float32))
    d_logits_low = d_logits.astype(bf16)
    grad_value_out = contract("krf,krc->kfc", head_hidden2[:-1], d_logits_low)
    grad_value_bias = jnp.sum(d_logits_low.astype(jnp.float32), 1)
    d_policy_low = d_policy.astype(bf16)
    grad_policy_out = contract("rf,rc->fc", head_hidden2[-1], d_policy_low)
    grad_policy_bias = jnp.sum(d_policy_low.astype(jnp.float32), 0)
    d_hidden2 = jnp.concatenate(
        [
            contract("krc,kfc->krf", d_logits_low, value_out),
            contract("rc,fc->rf", d_policy_low, policy_out)[None],
        ],
        0,
    )
    _, second_back = jax.vjp(norm_act, head_pre2, second_gain, second_shift)
    d_pre2, d_gain2, d_shift2 = second_back(d_hidden2)
    d_pre2_low = d_pre2.astype(bf16)
    grad_middle_heads = contract("krf,krg->kfg", head_hidden, d_pre2_low)
    d_hidden1 = contract("krg,kfg->krf", d_pre2_low, head_middle[1:])
    _, first_back = jax.vjp(norm_act, head_pre, first_gain, first_shift)
    d_pre1, d_gain1, d_shift1 = first_back(d_hidden1)
    d_pre1_low = d_pre1.astype(bf16)
    grad_latent_heads = contract("rl,krf->klf", state_rows, d_pre1_low)
    grad_action_heads = contract("ra,krf->kaf", action_rows, d_pre1_low[:-1])
    d_task_heads = jnp.sum(
        d_pre1_low.astype(jnp.float32).reshape(extra_heads, seq_count, horizon, hidden_dim), 2
    )
    d_state_heads = contract("krf,klf->rl", d_pre1_low, head_latent[1:]).reshape(
        seq_count, horizon, latent_dim
    )
    carry = jnp.zeros((seq_count, latent_dim), jnp.float32)
    dyn_terms = []
    for moment in reversed(range(horizon)):
        first_pre, first_hidden, second_pre, second_hidden, dyn_lin = dyn_saved[moment]
        d_next = d_predicted[:, moment]
        if moment + 1 < horizon:
            d_next = d_next + d_state_heads[:, moment + 1] + carry
        _, soft_back = jax.vjp(simnorm, dyn_lin)
        (d_lin,) = soft_back(d_next)
        d_lin_low = d_lin.astype(bf16)
        d_second = contract("rl,fl->rf", d_lin_low, latent_out[1])
        _, dyn_second_back = jax.vjp(norm_act, second_pre, gain_full[2], shift_full[2])
        d_spre, d_sgain, d_sshift = dyn_second_back(d_second)
        d_spre_low = d_spre.astype(bf16)
        d_first = contract("rg,fg->rf", d_spre_low, head_middle[0])
        _, dyn_first_back = jax.vjp(norm_act, first_pre, gain_full[1], shift_full[1])
        d_fpre, d_fgain, d_fshift = dyn_first_back(d_first)
        d_fpre_low = d_fpre.astype(bf16)
        carry = contract("rf,lf->rl", d_fpre_low, head_latent[0])
        dyn_terms.append(
            (
                contract("rf,rl->fl", second_hidden, d_lin_low),
                jnp.sum(d_lin_low.astype(jnp.float32), 0),
                contract("rf,rg->fg", first_hidden, d_spre_low),
                contract("rl,rf->lf", state_low[moment], d_fpre_low),
                contract("ra,rf->af", actions[:, moment], d_fpre_low),
                d_fpre_low.astype(jnp.float32),
                d_fgain,
                d_fshift,
                d_sgain,
                d_sshift,
            )
        )
    dyn_grads = [reduce(jnp.add, [terms[place] for terms in dyn_terms]) for place in range(10)]
    (
        grad_latent_dyn,
        grad_bias_dyn,
        grad_middle_dyn,
        grad_latent_in_dyn,
        grad_action_dyn,
        d_task_dyn,
        gain_dyn1,
        shift_dyn1,
        gain_dyn2,
        shift_dyn2,
    ) = dyn_grads
    d_state0 = d_state_heads[:, 0] + carry
    d_encoded = jnp.concatenate([d_state0[:, None], d_targets], 1).reshape(
        seq_count * (horizon + 1), latent_dim
    )
    (d_enc_lin,) = enc_soft_back(d_encoded)
    d_enc_lin_low = d_enc_lin.astype(bf16)
    grad_latent_enc = contract("rf,rl->fl", enc_hidden, d_enc_lin_low)
    grad_bias_enc = jnp.sum(d_enc_lin_low.astype(jnp.float32), 0)
    d_enc_hidden = contract("rl,fl->rf", d_enc_lin_low, latent_out[0])
    _, enc_back = jax.vjp(norm_act, enc_pre, gain_full[0], shift_full[0])
    d_enc_pre, gain_enc, shift_enc = enc_back(d_enc_hidden)
    d_enc_pre_low = d_enc_pre.astype(bf16)
    grad_encoder_in = contract("ro,rf->of", flat_obs, d_enc_pre_low)
    grad_observations = contract("rf,of->ro", d_enc_pre_low, encoder_in).reshape(
        seq_count, horizon + 1, obs_dim
    )
    d_task_all = jnp.concatenate([d_task_dyn[None], d_task_heads], 0)
    grad_head_task = jnp.einsum(
        "se,ksf->kef", embedded.astype(jnp.float32), d_task_all, precision=HIGHEST
    )
    d_embedded = jnp.einsum(
        "ksf,kef->se", d_task_all, head_task.astype(jnp.float32), precision=HIGHEST
    )
    grad_task_table = jnp.einsum("sn,se->ne", task_hot, d_embedded, precision=HIGHEST)
    head_gains = jnp.stack(
        [d_gain1.reshape(extra_heads, hidden_dim), d_gain2.reshape(extra_heads, hidden_dim)], 1
    ).reshape(2 * extra_heads, hidden_dim)
    head_shifts = jnp.stack(
        [d_shift1.reshape(extra_heads, hidden_dim), d_shift2.reshape(extra_heads, hidden_dim)], 1
    ).reshape(2 * extra_heads, hidden_dim)
    grad_norm_gain = jnp.concatenate(
        [gain_enc[None], gain_dyn1[None], gain_dyn2[None], head_gains], 0
    )
    grad_norm_shift = jnp.concatenate(
        [shift_enc[None], shift_dyn1[None], shift_dyn2[None], head_shifts], 0
    )
    reduced = reduce_all(
        (
            grad_encoder_in,
            jnp.stack([grad_latent_enc, grad_latent_dyn], 0),
            jnp.concatenate([grad_latent_in_dyn[None], grad_latent_heads], 0),
            jnp.concatenate([grad_action_dyn[None], grad_action_heads], 0),
            grad_head_task,
            jnp.concatenate([grad_middle_dyn[None], grad_middle_heads], 0),
            grad_value_out,
            grad_policy_out,
            grad_task_table,
            grad_norm_gain,
            grad_norm_shift,
            jnp.stack([grad_bias_enc, grad_bias_dyn], 0),
            grad_value_bias,
            grad_policy_bias,
        )
    )
    return (
        grad_observations,
        reduced[0],
        reduced[1],
        reduced[2],
        reduced[3],
        reduced[4],
        reduced[5],
        reduced[6],
        reduced[7],
        reduced[8],
        reduced[9],
        reduced[10],
        reduced[11],
        reduced[12],
        reduced[13],
    )


def solution(mesh):
    placed = (
        P(("batch", "lat"), None, None),
        P(("batch", "lat"), None, None),
        P(("batch", "lat")),
        P(),
        P(("batch", "lat"), None),
        P(("batch", "lat"), None),
        P(None, "lat"),
        P(None, "batch", "lat"),
        P(None, "batch", "lat"),
        P(None, None, "lat"),
        P(None, "batch", "lat"),
        P(None, "batch", "lat"),
        P(None, "batch", None),
        P("batch", None),
        P("batch", "lat"),
        P(None, "lat"),
        P(None, "lat"),
        P(None, "lat"),
        P(),
        P(),
    )
    return jax.shard_map(
        local,
        mesh=mesh,
        in_specs=placed,
        out_specs=(
            P(("batch", "lat"), None, None),
            P(None, "lat"),
            P(None, "batch", "lat"),
            P(None, "batch", "lat"),
            P(None, None, "lat"),
            P(None, "batch", "lat"),
            P(None, "batch", "lat"),
            P(None, "batch", None),
            P("batch", None),
            P("batch", "lat"),
            P(None, "lat"),
            P(None, "lat"),
            P(None, "lat"),
            P(),
            P(),
        ),
        check_vma=False,
    )
```

profile of v0, /device:TPU:0, one launch (start us, length us, event | category | flops | bytes accessed | tf_op | source)
XLA Modules:
  0.0 2103.0 jit_solution(2793790598853476314)
XLA Ops:
  34.0 24.7 %all-gather.19.cloned.1.call-done = bf16[8,128,1024]{2,1,0:T(8,128)(2,1)} async-done(((bf16[8,128,256]{2,1,0:T(8,128)(2,1)}), bf16[8,128,1024]{2,1,0:T(8,128)(2,1)}) %all-gather.19.cloned.1.call-update) | async-done | bytes 2097168 | tf_op jit(solution)/shard_map/all_gather | solution.py:96
  106.0 30.6 %all-gather.2 = bf16[8,10,96]{2,1,0:T(8,128)(2,1)S(1)} all-gather(bf16[1,10,96]{2,1,0:T(8,128)(2,1)S(1)} %bitcast.414), channel_id=1, replica_groups=mesh['batch'=8,'lat'=4] {'batch'}, dimensions={0}, use_global_device_ids=true | all-gather | bytes 17280 | tf_op jit(solution)/shard_map/all_gather | solution.py:144
  144.8 27.3 %all_gather.67 = bf16[1024,12]{0,1:T(8,128)(2,1)} all-gather(bf16[128,12]{0,1:T(8,128)(2,1)S(1)} %copy-done.239), channel_id=1, replica_groups=mesh['batch'=8,'lat'=4] {'batch'}, dimensions={0}, use_global_device_ids=true | all-gather | bytes 27648 | tf_op jit(solution)/shard_map/all_gather | solution.py:143
  210.3 12.6 div.315.clone
  222.9 27.3 %div.316 = f32[192,4,768]{2,1,0:T(4,128)} reshape(f32[768,96,8]{2,1,0:T(8,128)} %div.315.clone) | data formatting | bytes 4718592 | tf_op jit(solution)/shard_map/jvp()/div | solution.py:37
  250.2 12.6 sub.248.clone
  262.8 26.8 %sub.249 = f32[192,4,768]{2,1,0:T(4,128)} reshape(f32[768,96,8]{2,1,0:T(8,128)} %sub.248.clone) | data formatting | bytes 4718592 | tf_op jit(solution)/shard_map/jvp()/sub | solution.py:37
  306.3 40.0 %all-gather.15.cloned.1.call-done = bf16[8,768,1024]{2,1,0:T(8,128)(2,1)} async-done(((bf16[8,96,1024]{2,1,0:T(8,128)(2,1)}), bf16[8,768,1024]{2,1,0:T(8,128)(2,1)}) %all-gather.15.cloned.1.call-update) | async-done | bytes 12582928 | tf_op jit(solution)/shard_map/all_gather | solution.py:139
  349.0 225.1 %all-gather.21.cloned.1.call-done = bf16[8,1024,1024]{2,1,0:T(8,128)(2,1)} async-done(((bf16[8,128,1024]{2,1,0:T(8,128)(2,1)}), bf16[8,1024,1024]{2,1,0:T(8,128)(2,1)}) %all-gather.21.cloned.1.call-update) | async-done | bytes 16777232 | tf_op jit(solution)/shard_map/all_gather | solution.py:141
  615.2 12.4 broadcast_in_dim.88
  627.6 22.7 %fusion.206 = (f32[7,576]{1,0:T(8,128)S(1)}, f32[7,576,1024]{2,1,0:T(8,128)}) fusion(f32[7,576,1024]{2,0,1:T(8,128)} %bitcast.353, f32[6,576,1024]{2,1,0:T(8,128)} %convolution_bitcast_fusion, bf16[576,768,1]{1,0,2:T(8,128)(2,1)S(1)} %reshape.734, bf16[8,768,1024]{2,1,0:T(8,128)(2,1)} %all-gather.15.cloned.1.call-done), kind=kOutput, calls=%fused_computation.459 | convolution fusion | flops 6354169856 | bytes 61456128 | tf_op jit(solution)/shard_map/rl,klf->krf/dot_general | solution.py:22
  658.0 25.9 %fusion.207 = (f32[7,576]{1,0:T(8,128)S(1)}, f32[7,576,1024]{2,1,0:T(8,128)}) fusion(bf16[8,1024,1024]{2,1,0:T(8,128)(2,1)} %all-gather.21.cloned.1.call-done, f32[7,576,1024]{2,1,0:T(8,128)} %get-tuple-element.240, f32[7,1024]{1,0:T(8,128)S(1)} %copy-done.164, f32[7,1024]{1,0:T(8,128)S(1)} %copy-done.121, f32[7,576]{1,0:T(8,128)S(1)} %fusion.124, ...), kind=kOutput, calls=%fused_computation.460 | convolution fusion | flops 8509386752 | bytes 47815936 | tf_op jit(solution)/shard_map/krf,kfg->krg/dot_general | solution.py:22
  691.5 38.5 %fusion.10 = bf16[7,576,1024]{2,1,0:T(8,128)(2,1)} fusion(f32[7,576,1024]{2,1,0:T(8,128)} %get-tuple-element.242, f32[7,1024]{1,0:T(8,128)S(1)} %copy-done.120, f32[7,1024]{1,0:T(8,128)S(1)} %copy-done.111, f32[7,576]{1,0:T(8,128)S(1)} %fusion.125, f32[7,576]{1,0:T(8,128)S(1)} %broadcast_multiply_fusion.1), kind=kLoop, calls=%fused_computation.31 | loop fusion | flops 49545216 | bytes 24862208 | tf_op jit(solution)/shard_map/convert_element_type | solution.py:435
  745.3 28.6 %multiply_reduce_fusion = (bf16[7,1024]{1,0:T(8,128)(2,1)}, f32[7,576]{1,0:T(8,128)S(1)}, bf16[7,1024]{1,0:T(8,128)(2,1)}, f32[7,576,1024]{2,1,0:T(8,128)}) fusion(f32[7,576,1024]{2,1,0:T(8,128)S(1)} %bitcast.349, f32[7,576]{1,0:T(8,128)S(1)} %fusion.125, f32[7,576]{1,0:T(8,128)S(1)} %broadcast_multiply_fusion.1, f32[7,1024]{1,0:T(8,128)S(1)} %copy-done.111, ...), kind=kLoop, calls=%fused_computation.20 | loop fusion | flops 123844672 | bytes 49679616 | tf_op jit(solution)/shard_map/transpose(jvp())/reduce_sum | solution.py:32
  773.9 14.4 fusion.188
  788.4 39.5 %fusion.179 = (bf16[7,1024]{1,0:T(8,128)(2,1)}, f32[7,576]{1,0:T(8,128)S(1)}, f32[7,576,1024]{2,1,0:T(8,128)}) fusion(f32[7,1024]{1,0:T(8,128)S(1)} %copy-done.121, f32[7,576,1024]{2,1,0:T(8,128)} %get-tuple-element.240, f32[7,576]{1,0:T(8,128)S(1)} %broadcast_multiply_fusion.2, f32[7,1024]{1,0:T(8,128)S(1)} %copy-done.164, f32[7,576]{1,0:T(8,128)S(1)} %fusion.124, ...), kind=kOutput, calls=%fused_computation.437 | convolution fusion | flops 8575439872 | bytes 64361472 | tf_op jit(solution)/shard_map/krg,kfg->krf/dot_general | solution.py:22
  828.0 17.5 multiply_reduce_fusion.1
  942.9 23.4 %reshape_reshape.6 = f32[768,96,8]{2,1,0:T(8,128)} reshape(f32[192,4,768]{2,1,0:T(4,128)S(1)} %copy.256) | data formatting | bytes 4718592 | tf_op jit(solution)/shard_map/transpose(jvp())/reshape;reshape | solution.py:37
  973.4 26.8 %copy.259 = f32[768,96,8]{0,2,1:T(8,128)} copy(f32[768,96,8]{2,1,0:T(8,128)} %reshape_reshape.6) | data formatting | bytes 4718592 | tf_op jit(solution)/shard_map/transpose(jvp())/reshape;reshape | solution.py:37
  1036.7 14.6 copy.266
  1119.0 16.9 copy.265
  1141.4 30.5 %convolution_convert_fusion = bf16[7,1024,1024]{2,1,0:T(8,128)(2,1)} fusion(f32[7,576,1024]{2,1,0:T(8,128)} %get-tuple-element.189, f32[7,576]{1,0:T(8,128)S(1)} %copy-done.168, f32[7,576,1024]{2,1,0:T(8,128)} %get-tuple-element.240, f32[7,1024]{1,0:T(8,128)S(1)} %copy-done.165, f32[7,1024]{1,0:T(8,128)S(1)} %copy-done.122, f32[7,576]{1,0:T(8,128)S(1)} %copy-done.130, ...), kind=kOutput, calls=%fused_computation.44 | convolution fusion | flops 8520859648 | bytes 47815936 | tf_op jit(solution)/shard_map/krf,krg->kfg/dot_general | solution.py:22
  1171.9 13.2 pad_maximum_fusion
  1200.6 58.7 %reduce-scatter.44.cloned.1.call-done = bf16[128,606]{1,0:T(8,128)(2,1)} async-done(((bf16[1024,606]{1,0:T(8,128)(2,1)}), bf16[128,606]{1,0:T(8,128)(2,1)}) %reduce-scatter.44.cloned.1.call-update) | async-done | bytes 155152
  1261.4 74.8 %reduce-scatter.22.cloned.1.call-done = bf16[2,128,768]{2,1,0:T(8,128)(2,1)} async-done(((bf16[2,1024,768]{2,1,0:T(8,128)(2,1)}), bf16[2,128,768]{2,1,0:T(8,128)(2,1)}) %reduce-scatter.22.cloned.1.call-update) | async-done | bytes 393232 | tf_op jit(solution)/shard_map/reduce_scatter | solution.py:182
  1338.2 207.8 %reduce-scatter.24.cloned.1.call-done = bf16[8,96,1024]{2,0,1:T(8,128)(2,1)} async-done(((bf16[8,768,1024]{2,0,1:T(8,128)(2,1)}), bf16[8,96,1024]{2,0,1:T(8,128)(2,1)}) %reduce-scatter.24.cloned.1.call-update) | async-done | bytes 1572880 | tf_op jit(solution)/shard_map/reduce_scatter | solution.py:185
  1546.1 284.7 %reduce-scatter.32.cloned.1.call-done = bf16[8,128,1024]{2,1,0:T(8,128)(2,1)} async-done(((bf16[8,1024,1024]{2,1,0:T(8,128)(2,1)}), bf16[8,128,1024]{2,1,0:T(8,128)(2,1)}) %reduce-scatter.32.cloned.1.call-update) | async-done | bytes 2097168 | tf_op jit(solution)/shard_map/reduce_scatter | solution.py:191
  1836.4 58.9 %reduce-scatter.46.cloned.1.call-done = bf16[128,12]{1,0:T(8,128)(2,1)} async-done(((bf16[1024,12]{1,0:T(8,128)(2,1)}), bf16[128,12]{1,0:T(8,128)(2,1)}) %reduce-scatter.46.cloned.1.call-update) | async-done | bytes 3088
  1896.1 74.8 %all-reduce.16.cloned.1.call-done = (bf16[7,6,256]{2,1,0:T(8,128)(2,1)}, bf16[39,256]{1,0:T(8,128)(2,1)}, bf16[80,96]{1,0:T(8,128)(2,1)}, bf16[17,256]{1,0:T(8,1...) async-done(((bf16[7,6,256]{2,1,0:T(8,128)(2,1)}, bf16[39,256]{1,0:T(8,128)(2,1)}, ...) | async-done | bytes 76260 | tf_op jit(solution)/shard_map/psum | solution.py:206
  1993.7 35.1 %all-reduce.18.cloned.1.call-done = (bf16[2,128,768]{1,0,2:T(2,128)(2,1)}, bf16[6,128,101]{1,2,0:T(8,128)(2,1)}) async-done(((bf16[2,128,768]{1,0,2:T(2,128)(2,1)}, bf16[6,128,101]{1,2,0:T(8,128)(2,1)}), (bf16[2,128,768]{1,0,2:T(2,128)(2,1)}, bf16[6,128,101]{1,2,0:T(8,128)(2,1)})) %all-reduce.18.cloned.1.call-update) | async-done | bytes 548368
  2032.1 27.7 %reduce-scatter.26.cloned.1.call-done = bf16[8,96,256]{2,0,1:T(8,128)(2,1)} async-done(((bf16[8,96,1024]{2,0,1:T(8,128)(2,1)}), bf16[8,96,256]{2,0,1:T(8,128)(2,1)}) %reduce-scatter.26.cloned.1.call-update) | async-done | bytes 393232 | tf_op jit(solution)/shard_map/reduce_scatter | solution.py:266
  2061.7 32.2 %reduce-scatter.34.cloned.1.call-done = bf16[8,128,256]{2,1,0:T(8,128)(2,1)} async-done(((bf16[8,128,1024]{2,1,0:T(8,128)(2,1)}), bf16[8,128,256]{2,1,0:T(8,128)(2,1)}) %reduce-scatter.34.cloned.1.call-update) | async-done | bytes 524304 | tf_op jit(solution)/shard_map/reduce_scatter | solution.py:275
  (905 shorter events, 476.1 us)
Async XLA Ops:
  7.2 26.7 %all-gather.13.cloned.1.call-start = ((), (), s32[]{:S(2)}) async-start(), calls=%async_computation.15 | async-start | bytes 1966080 | tf_op jit(solution)/shard_map/all_gather | solution.py:93
  7.9 50.7 %all-gather.19.cloned.1.call-start = ((), (), s32[]{:S(2)}) async-start(), calls=%async_computation.18 | async-start | bytes 2621440 | tf_op jit(solution)/shard_map/all_gather | solution.py:96
  8.7 173.5 %all-gather.17.cloned.1.call-start = ((), (), s32[]{:S(2)}) async-start(), calls=%async_computation.17 | async-start | bytes 1769472 | tf_op jit(solution)/shard_map/all_gather | solution.py:140
  17.4 178.0 %all-gather.11.cloned.1.call-start = ((), (), s32[]{:S(2)}) async-start(), calls=%async_computation.14 | async-start | bytes 3538944 | tf_op jit(solution)/shard_map/all_gather | solution.py:138
  27.4 318.9 %all-gather.15.cloned.1.call-start = ((), (), s32[]{:S(2)}) async-start(), calls=%async_computation.16 | async-start | bytes 14155776 | tf_op jit(solution)/shard_map/all_gather | solution.py:139
  33.9 540.2 %all-gather.21.cloned.1.call-start = ((), (), s32[]{:S(2)}) async-start(), calls=%async_computation.19 | async-start | bytes 18874368 | tf_op jit(solution)/shard_map/all_gather | solution.py:141
  58.7 671.3 %all-gather.23.cloned.1.call-start = ((), (), s32[]{:S(2)}) async-start(), calls=%async_computation.20 | async-start | bytes 1437696 | tf_op jit(solution)/shard_map/all_gather | solution.py:142
  59.5 1138.9 %reduce-scatter.48.cloned.1.call-start = ((), (), s32[]{:S(2)}) async-start(), calls=%async_computation.34 | async-start | bytes 245760
  73.4 529.7 %copy-start.123 = (f32[1,1024]{1,0:T(1,128)}, f32[1,1024]{1,0:T(1,128)S(1)}, u32[]{:S(2)}) copy-start(f32[1,1024]{1,0:T(1,128)S(1)} %get-tuple-element.215) | copy-start | bytes 12292
  73.4 533.6 %copy-start.125 = (f32[1,1024]{1,0:T(1,128)}, f32[1,1024]{1,0:T(1,128)S(1)}, u32[]{:S(2)}) copy-start(f32[1,1024]{1,0:T(1,128)S(1)} %get-tuple-element.214) | copy-start | bytes 12292
  79.8 523.3 %copy-start.145 = (f32[1,1024]{1,0:T(1,128)}, f32[1,1024]{1,0:T(1,128)S(1)}, u32[]{:S(2)}) copy-start(f32[1,1024]{1,0:T(1,128)S(1)} %get-tuple-element.218) | copy-start | bytes 12292
  348.7 228.3 %copy-start.9 = (f32[192,1024]{1,0:T(8,128)}, f32[192,1024]{1,0:T(8,128)S(1)}, u32[]{:S(2)}) copy-start(f32[192,1024]{1,0:T(8,128)S(1)} %get-tuple-element.226) | copy-start | bytes 2359300
  348.8 228.3 %copy-start.170 = (f32[192]{0:T(256)}, f32[192]{0:T(256)S(1)}, u32[]{:S(2)}) copy-start(f32[192]{0:T(256)S(1)} %broadcast_multiply_fusion.9) | copy-start | bytes 2308
  1016.7 183.3 %reduce-scatter.42.cloned.1.call-start = ((), (), s32[]{:S(2)}) async-start(), calls=%async_computation.31 | async-start | bytes 61440 | tf_op jit(solution)/shard_map/reduce_scatter | solution.py:284
  1032.0 167.9 %reduce-scatter.40.cloned.1.call-start = ((), (), s32[]{:S(2)}) async-start(), calls=%async_computation.30 | async-start | bytes 61440 | tf_op jit(solution)/shard_map/reduce_scatter | solution.py:281
  1032.8 167.2 %reduce-scatter.36.cloned.1.call-start = ((), (), s32[]{:S(2)}) async-start(), calls=%async_computation.28 | async-start | bytes 102400 | tf_op jit(solution)/shard_map/reduce_scatter | solution.py:260
  1036.1 163.9 %reduce-scatter.38.cloned.1.call-start = ((), (), s32[]{:S(2)}) async-start(), calls=%async_computation.29 | async-start | bytes 143360 | tf_op jit(solution)/shard_map/reduce_scatter | solution.py:269
  1073.0 127.0 %reduce-scatter.28.cloned.1.call-start = ((), (), s32[]{:S(2)}) async-start(), calls=%async_computation.24 | async-start | bytes 1769472 | tf_op jit(solution)/shard_map/reduce_scatter | solution.py:188
  1080.5 178.9 %reduce-scatter.44.cloned.1.call-start = ((), (), s32[]{:S(2)}) async-start(), calls=%async_computation.32 | async-start | bytes 1474560
  1089.4 246.8 %reduce-scatter.22.cloned.1.call-start = ((), (), s32[]{:S(2)}) async-start(), calls=%async_computation.21 | async-start | bytes 3538944 | tf_op jit(solution)/shard_map/reduce_scatter | solution.py:182
  1097.1 448.9 %reduce-scatter.24.cloned.1.call-start = ((), (), s32[]{:S(2)}) async-start(), calls=%async_computation.22 | async-start | bytes 14155776 | tf_op jit(solution)/shard_map/reduce_scatter | solution.py:185
  1136.1 694.7 %reduce-scatter.32.cloned.1.call-start = ((), (), s32[]{:S(2)}) async-start(), calls=%async_computation.26 | async-start | bytes 18874368 | tf_op jit(solution)/shard_map/reduce_scatter | solution.py:191
  1185.1 710.2 %reduce-scatter.46.cloned.1.call-start = ((), (), s32[]{:S(2)}) async-start(), calls=%async_computation.33 | async-start | bytes 294912
  1188.3 782.6 %all-reduce.16.cloned.1.call-start = ((), (), s32[]{:S(2)}) async-start(), calls=%async_computation.35 | async-start | bytes 195584 | tf_op jit(solution)/shard_map/psum | solution.py:206
  1197.7 633.1 %copy-start.268 = (u32[32]{0:T(128)S(1)}, u32[32]{0:T(128)}, u32[]{:S(2)}) copy-start(u32[32]{0:T(128)} %constant.143) | copy-start | bytes 388
  1197.7 633.7 %copy-start.267 = (u32[32]{0:T(128)S(1)}, u32[32]{0:T(128)}, u32[]{:S(2)}) copy-start(u32[32]{0:T(128)} %constant.139) | copy-start | bytes 388
  1198.3 635.6 %copy-start.6 = (f32[768,1024]{1,0:T(8,128)S(1)}, f32[768,1024]{1,0:T(8,128)}, u32[]{:S(2)}) copy-start(f32[768,1024]{1,0:T(8,128)} %get-tuple-element.179) | copy-start | bytes 9437188
  1198.3 635.6 %copy-start.163 = (f32[768]{0:T(1024)S(1)}, f32[768]{0:T(1024)}, u32[]{:S(2)}) copy-start(f32[768]{0:T(1024)} %copy-done.162) | copy-start | bytes 9220
  1200.0 792.2 %reduce-scatter.30.cloned.1.call-start = ((), (), s32[]{:S(2)}) async-start(), calls=%async_computation.25 | async-start | bytes 245760 | tf_op jit(solution)/shard_map/reduce_scatter | solution.py:272
  1200.6 828.2 %all-reduce.18.cloned.1.call-start = ((), (), s32[]{:S(2)}) async-start(), calls=%async_computation.36 | async-start | bytes 1105920
  1338.2 721.6 %reduce-scatter.26.cloned.1.call-start = ((), (), s32[]{:S(2)}) async-start(), calls=%async_computation.23 | async-start | bytes 1966080 | tf_op jit(solution)/shard_map/reduce_scatter | solution.py:266
  1546.0 547.9 %reduce-scatter.34.cloned.1.call-start = ((), (), s32[]{:S(2)}) async-start(), calls=%async_computation.27 | async-start | bytes 2621440 | tf_op jit(solution)/shard_map/reduce_scatter | solution.py:275
  (269 other events, 3042.3 us)
Sparse Core Ops, SparseCore 0:
  9.6 24.2 all-gather.12
  35.5 23.1 all-gather.18
  60.9 44.1 all-gather.16
  107.0 62.3 all-gather.10
  171.4 174.8 all-gather.14
  348.3 225.7 all-gather.20
  576.2 40.2 all-gather.22
  1016.8 17.8 reduce-scatter.47
  1037.1 19.3 reduce-scatter.41
  1059.6 19.4 reduce-scatter.39
  1082.0 19.5 reduce-scatter.35
  1104.4 19.5 reduce-scatter.37
  1127.8 64.9 reduce-scatter.27
  1196.0 63.2 reduce-scatter.43
  1262.7 73.3 reduce-scatter.21
  1339.6 206.3 reduce-scatter.23
  1549.6 281.1 reduce-scatter.31
  1834.9 60.3 reduce-scatter.45
  1900.6 70.2 all-reduce.15
  1973.4 18.8 reduce-scatter.29
  1995.4 33.3 all-reduce.17
  2031.3 28.3 reduce-scatter.25
  2062.4 31.4 reduce-scatter.33
where the time goes:
time: 2110 us; the launch traced here: 2100 us
  waiting for transfers between devices  1150 us (55%)
  local copies, waits for them, and re-layouts  309 us (15%)
  matrix products  267 us (13%)
  other arithmetic  232 us (11%)
  blocking collectives  118 us (6%)
    reduce_scatter x1, waiting for transfers between devices, reduce_batch(): lax.psum_scatter(head_middle.astype(jnp.bfloat16), 'batch', scatter_dimen...  285 us
    all_gather x1, waiting for transfers between devices, through_batch(): lax.all_gather(head_middle, 'batch', axis=1, tiled=True)  225 us
    dot_general x39, matrix products, contract(): return jnp.einsum(form, left, right, preferred_element_type=jnp.float32)  222 us
    reduce_scatter x1, waiting for transfers between devices, reduce_batch(): lax.psum_scatter(head_latent.astype(jnp.bfloat16), 'batch', scatter_dimen...  208 us
    unnamed x27, waiting for transfers between devices  156 us
    psum x1, waiting for transfers between devices, reduce_batch(): lax.psum(head_action.astype(jnp.bfloat16), 'batch').astype(jnp.float32)  74.8 us
    reduce_scatter x1, waiting for transfers between devices, reduce_batch(): lax.psum_scatter(latent_out.astype(jnp.bfloat16), 'batch', scatter_dimens...  74.8 us
    div x10, local copies, waits for them, and re-layouts, simnorm(): return jax.nn.softmax(groups, -1).reshape(values.shape)  60.6 us
  transfers between devices with their start and end apart: 23, of which 14 were waited for; matrix products, arithmetic and copies ran while one was open for 24% of the time, Pallas kernels for 0%

commit v1 on v0

--- a/solution.py
+++ b/solution.py
@@ -1,9 +1,12 @@
+import functools
 from functools import reduce
 import math
 
 import jax
 import jax.numpy as jnp
 from jax import lax
+from jax.experimental import pallas as pl
+from jax.experimental.pallas import tpu as pltpu
 from jax.sharding import PartitionSpec as P
 
 SIMNORM = 8
@@ -12,6 +15,7 @@
 LOG_STD_LO = -2.0
 LOG_STD_HI = 2.0
 HIGHEST = lax.Precision.HIGHEST
+CHUNK_ROWS = 112
 
 
 def product32(left, right):
@@ -59,266 +63,570 @@
     return jnp.sum(jnp.sum((per_row + consistency) * discount, -1) * row_weight)
 
 
-def through_lat(members):
-    (
+MESH_ID = pl.DeviceIdType.MESH
+
+
+def major_minor(size):
+    minor = 1
+    while (minor * 2) * (minor * 2) <= size:
+        minor *= 2
+    return size // minor, minor
+
+
+class Place:
+    def __init__(self, depth, side):
+        self.depth, self.side = depth, side
+        batch, lat = lax.axis_index("batch"), lax.axis_index("lat")
+        self.z, x = batch // side, lax.rem(batch, side)
+        y, self.c = lat // 2, lax.rem(lat, 2)
+        self.i = jnp.where(self.c == 0, y, x)
+        self.j = jnp.where(self.c == 0, x, y)
+
+    def device(self, c=None, i=None, j=None, z=None):
+        c, i = self.c if c is None else c, self.i if i is None else i
+        j, z = self.j if j is None else j, self.z if z is None else z
+        x, y = jnp.where(c == 0, j, i), jnp.where(c == 0, i, j)
+        return (z * self.side + x, y * 2 + c)
+
+    def sibling(self):
+        x, y = jnp.where(self.c == 0, self.j, self.i), jnp.where(self.c == 0, self.i, self.j)
+        return (self.z * self.side + x, y * 2 + 1 - self.c)
+
+    def dims(self):
+        return (
+            ("i", self.i, self.side, lambda p: self.device(i=p)),
+            ("j", self.j, self.side, lambda p: self.device(j=p)),
+            ("z", self.z, self.depth, lambda p: self.device(z=p)),
+        )
+
+    def barrier(self):
+        sem = pltpu.get_barrier_semaphore()
+        pl.semaphore_signal(sem, inc=1, device_id=self.sibling(), device_id_type=MESH_ID)
+        count = 1
+        for _, pos, size, at in self.dims():
+            if size == 2:
+                pl.semaphore_signal(sem, inc=1, device_id=at(1 - pos), device_id_type=MESH_ID)
+                count = count + 1
+            else:
+                for step in (-1, 1):
+
+                    @pl.when((pos + step >= 0) & (pos + step < size))
+                    def _(at=at, pos=pos, step=step):
+                        pl.semaphore_signal(sem, inc=1, device_id=at(pos + step), device_id_type=MESH_ID)
+
+                count = count + jnp.where(pos > 0, 1, 0) + jnp.where(pos < size - 1, 1, 0)
+        pl.semaphore_wait(sem, count)
+
+
+def gather_steps(depth, side):
+    return (
+        [("z", s) for s in range(depth - 1)]
+        + [("j", s) for s in range(side - 1)]
+        + [("i", s) for s in range(side - 1)]
+        + [("c", 0)]
+    )
+
+
+def gather_kernel(depth, side, chunks, chunk_rows, mine_ref, all_ref, own_sem, send_sems, recv_sems):
+    place = Place(depth, side)
+    steps = gather_steps(depth, side)
+    dims = {name: (pos, size, at) for name, pos, size, at in place.dims()}
+    own = pltpu.make_async_copy(mine_ref, all_ref.at[place.c, place.i, place.j, place.z], own_sem)
+    own.start()
+    place.barrier()
+
+    def block(name, owner, rows):
+        if name == "z":
+            return all_ref.at[place.c, place.i, place.j, owner, rows]
+        if name == "j":
+            return all_ref.at[place.c, place.i, owner, :, rows]
+        return all_ref.at[place.c, owner, :, :, rows]
+
+    def copy(which, t, way, source, target, device):
+        return pltpu.make_async_remote_copy(
+            src_ref=source,
+            dst_ref=target,
+            send_sem=send_sems.at[which, way, t],
+            recv_sem=recv_sems.at[which, way, t],
+            device_id=device,
+            device_id_type=MESH_ID,
+        )
+
+    def each(which, t, act, sending):
+        name, s = steps[which]
+        rows = pl.ds(pl.multiple_of(t * chunk_rows, 16), chunk_rows)
+        if name == "c":
+            core = place.c if sending else 1 - place.c
+            ref = all_ref.at[core, :, :, :, rows]
+            act(copy(which, t, 0, ref, ref, place.sibling()))
+            return
+        pos, size, at = dims[name]
+        if size == 2:
+            ref = block(name, pos if sending else 1 - pos, rows)
+            source = mine_ref.at[rows] if sending and name == "z" and s == 0 else ref
+            act(copy(which, t, 0, source, ref, at(1 - pos)))
+            return
+        if sending:
+            ways = (
+                (0, (pos >= s) & (pos + 1 < size), pos - s, pos + 1),
+                (1, (pos + s < size) & (pos >= 1), pos + s, pos - 1),
+            )
+        else:
+            ways = (
+                (0, pos - 1 >= s, pos - 1 - s, pos - 1),
+                (1, pos + 1 + s < size, pos + 1 + s, pos + 1),
+            )
+        for way, valid, owner, target in ways:
+
+            @pl.when(valid)
+            def _(way=way, owner=owner, target=target):
+                ref = block(name, owner, rows)
+                source = mine_ref.at[rows] if sending and name == "z" and s == 0 else ref
+                act(copy(which, t, way, source, ref, at(target)))
+
+    def body(t, carry):
+        for which in range(len(steps) + 1):
+            at = t - which
+
+            @pl.when((at >= 0) & (at < chunks))
+            def _(which=which, at=at):
+                if which > 0:
+                    each(which - 1, at, lambda c: c.wait_recv(), False)
+                if which < len(steps):
+                    if which == depth - 1:
+
+                        @pl.when(at == 0)
+                        def _():
+                            own.wait()
+
+                    each(which, at, lambda c: c.start(), True)
+
+        return carry
+
+    lax.fori_loop(0, chunks + len(steps), body, 0)
+
+    def drain(t, carry):
+        for which in range(len(steps)):
+            each(which, t, lambda c: c.wait_send(), True)
+        return carry
+
+    lax.fori_loop(0, chunks, drain, 0)
+
+
+def gather_all(mine, depth, side, chunks):
+    rows, cols = mine.shape
+    steps = len(gather_steps(depth, side))
+    return pl.pallas_call(
+        functools.partial(gather_kernel, depth, side, chunks, rows // chunks),
+        out_shape=jax.ShapeDtypeStruct((2, side, side, depth, rows, cols), mine.dtype),
+        in_specs=[pl.BlockSpec(memory_space=pl.ANY)],
+        out_specs=pl.BlockSpec(memory_space=pl.ANY),
+        scratch_shapes=[
+            pltpu.SemaphoreType.DMA,
+            pltpu.SemaphoreType.DMA((steps, 2, chunks)),
+            pltpu.SemaphoreType.DMA((steps, 2, chunks)),
+        ],
+        compiler_params=pltpu.CompilerParams(collective_id=1, has_side_effects=True),
+        name="gather_weights",
+    )(mine)
+
+
+def scatter_steps(depth, side):
+    return (
+        [("c", 0)]
+        + [("i", s) for s in range(side - 1)]
+        + [("j", s) for s in range(side - 1)]
+        + [("z", s) for s in range(depth - 1)]
+    )
+
+
+def scatter_kernel(depth, side, chunks, chunk_rows, parts_ref, sum_ref, *scratch):
+    held, own_buf, own_sems, send_sems, recv_sems = scratch[:5]
+    landing = dict(zip(("i", "j", "z"), (scratch[5:7], scratch[7:9], scratch[9:11])))
+    place = Place(depth, side)
+    steps = scatter_steps(depth, side)
+    dims = {name: (pos, size, at) for name, pos, size, at in place.dims()}
+    place.barrier()
+
+    def block(name, owner, rows):
+        if name == "z":
+            return held.at[place.i, place.j, owner, rows]
+        if name == "j":
+            return held.at[place.i, owner, :, rows]
+        return held.at[owner, :, :, rows]
+
+    def land(name, owner, rows):
+        if owner is None:
+            ref = landing[name][1]
+        else:
+            ref = landing[name][0].at[owner]
+        if name == "z":
+            return ref.at[rows]
+        if name == "j":
+            return ref.at[:, rows]
+        return ref.at[:, :, rows]
+
+    def add(into, other):
+        lead = into.shape[:-2]
+        if not lead:
+            into[...] += other[...]
+            return
+
+        def one(n, carry):
+            index = []
+            for extent in reversed(lead):
+                index.insert(0, lax.rem(n, extent))
+                n = n // extent
+            into[tuple(index)] += other[tuple(index)]
+            return carry
+
+        lax.fori_loop(0, math.prod(lead), one, 0)
+
+    def own_copy(t):
+        rows = pl.ds(pl.multiple_of(t * chunk_rows, 16), chunk_rows)
+        slot = lax.rem(t, 2)
+        return pltpu.make_async_copy(
+            parts_ref.at[place.c, :, :, :, rows], own_buf.at[slot], own_sems.at[slot]
+        )
+
+    def copy(which, t, way, source, target, device):
+        return pltpu.make_async_remote_copy(
+            src_ref=source,
+            dst_ref=target,
+            send_sem=send_sems.at[which, way, t],
+            recv_sem=recv_sems.at[which, way, t],
+            device_id=device,
+            device_id_type=MESH_ID,
+        )
+
+    def send(which, t, act):
+        name, s = steps[which]
+        rows = pl.ds(pl.multiple_of(t * chunk_rows, 16), chunk_rows)
+        if name == "c":
+            act(
+                copy(
+                    which, t, 0, parts_ref.at[1 - place.c, :, :, :, rows],
+                    held.at[:, :, :, rows], place.sibling(),
+                )
+            )
+            return
+        pos, size, at = dims[name]
+        if size == 2:
+            act(copy(which, t, 0, block(name, 1 - pos, rows), land(name, None, rows), at(1 - pos)))
+            return
+        back = size - 1 - pos
+        last = s == size - 2
+
+        @pl.when((pos <= s) & (pos < size - 1))
+        def _():
+            owner = size - 1 - (s - pos)
+            act(copy(which, t, 0, block(name, owner, rows), land(name, owner, rows), at(pos + 1)))
+
+        @pl.when((back <= s) & (pos > 0))
+        def _():
+            owner = s - back
+            act(
+                copy(
+                    which, t, 1, block(name, owner, rows),
+                    land(name, None if last else owner, rows), at(pos - 1),
+                )
+            )
+
+    def receive(which, t):
+        name, s = steps[which]
+        rows = pl.ds(pl.multiple_of(t * chunk_rows, 16), chunk_rows)
+        if name == "c":
+            copy(
+                which, t, 0, held.at[:, :, :, rows], held.at[:, :, :, rows], place.sibling()
+            ).wait_recv()
+            own_copy(t).wait()
+            add(held.at[:, :, :, rows], own_buf.at[lax.rem(t, 2)])
+            return
+        pos, size, at = dims[name]
+        if size == 2:
+            ref = land(name, None, rows)
+            copy(which, t, 0, ref, ref, at(1 - pos)).wait_recv()
+            add(block(name, pos, rows), ref)
+            return
+        last = s == size - 2
+
+        @pl.when((pos - 1 <= s) & (pos >= 1))
+        def _():
+            owner = size - 1 - (s - (pos - 1))
+            ref = land(name, owner, rows)
+            copy(which, t, 0, ref, ref, at(pos - 1)).wait_recv()
+            add(block(name, owner, rows), ref)
+
+        @pl.when((size - 2 - pos <= s) & (pos < size - 1))
+        def _():
+            owner = s - (size - 2 - pos)
+            ref = land(name, None if last else owner, rows)
+            copy(which, t, 1, ref, ref, at(pos + 1)).wait_recv()
+            add(block(name, owner, rows), ref)
+
+    def body(t, carry):
+        @pl.when(t < chunks)
+        def _():
+            own_copy(t).start()
+
+        for which in range(len(steps) + 1):
+            at = t - which
+
+            @pl.when((at >= 0) & (at < chunks))
+            def _(which=which, at=at):
+                if which > 0:
+                    receive(which - 1, at)
+                if which < len(steps):
+                    send(which, at, lambda c: c.start())
+                else:
+                    rows = pl.ds(pl.multiple_of(at * chunk_rows, 16), chunk_rows)
+                    sum_ref[rows, :] = held[place.i, place.j, place.z, rows, :].astype(sum_ref.dtype)
+
+        return carry
+
+    lax.fori_loop(0, chunks + len(steps), body, 0)
+
+    def drain(t, carry):
+        for which in range(len(steps)):
+            send(which, t, lambda c: c.wait_send())
+        return carry
+
+    lax.fori_loop(0, chunks, drain, 0)
+
+
+def scatter_sum(parts, depth, side, chunks):
+    rows, cols = parts.shape[-2:]
+    chunk_rows = rows // chunks
+    steps = len(scatter_steps(depth, side))
+    dtype = parts.dtype
+
+    def landing(size, *lead):
+        first = (size,) + lead if size > 2 else (1,)
+        tail = (rows, cols) if size > 2 else (16, 128)
+        return [pltpu.VMEM(first + tail, dtype), pltpu.VMEM(lead + (rows, cols), dtype)]
+
+    return pl.pallas_call(
+        functools.partial(scatter_kernel, depth, side, chunks, chunk_rows),
+        out_shape=jax.ShapeDtypeStruct((rows, cols), jnp.float32),
+        in_specs=[pl.BlockSpec(memory_space=pl.ANY)],
+        out_specs=pl.BlockSpec(memory_space=pltpu.VMEM),
+        scratch_shapes=[
+            pltpu.VMEM((side, side, depth, rows, cols), dtype),
+            pltpu.VMEM((2, side, side, depth, chunk_rows, cols), dtype),
+            pltpu.SemaphoreType.DMA((2,)),
+            pltpu.SemaphoreType.DMA((steps, 2, chunks)),
+            pltpu.SemaphoreType.DMA((steps, 2, chunks)),
+        ]
+        + landing(side, side, depth)
+        + landing(side, depth)
+        + landing(depth),
+        compiler_params=pltpu.CompilerParams(
+            collective_id=2, has_side_effects=True, vmem_limit_bytes=60 * 2**20
+        ),
+        name="scatter_gradients",
+    )(parts)
+
+def round_up(n, to):
+    return -(-n // to) * to
+
+
+class Rows:
+    def __init__(self, shapes, batches, lats):
+        self.batches, self.lats = batches, lats
+        (self.heads, self.latent_rows, self.cols) = shapes["head_latent"]
+        self.middle_rows = shapes["head_middle"][1]
+        self.task_rows = shapes["head_task"][1]
+        self.pieces = self.cols // 128
+        self.share = self.middle_rows // lats
+        self.value_rows = self.share // self.pieces
+        self.latent_cols = shapes["latent_out"][2]
+        self.out_rows = self.middle_rows * self.latent_cols // self.cols
+        self.middle_at = self.latent_rows
+        self.value_at = self.middle_at + self.middle_rows
+        self.task_at = self.value_at + self.value_rows
+        self.table_at = self.task_at + self.task_rows
+        self.head_rows = round_up(self.table_at + 1, 16)
+        self.table_shape = shapes["task_table"]
+        self.small_rows = self.value_rows * batches
+        self.obs = shapes["encoder_in"][0]
+        self.acts = shapes["head_action"][0] * shapes["head_action"][1]
+        self.norms = shapes["norm_gain"][0]
+        self.bias_at = self.obs + self.acts + 2 * self.norms
+        self.wide_at = self.bias_at + 2
+        self.wide_rows = (self.heads - 1) // self.pieces + (1 if (self.heads - 1) % self.pieces else 0)
+        self.total = self.heads * self.head_rows + 2 * self.out_rows
+
+
+def fill(values, shape):
+    return jnp.pad(values, [(0, want - have) for have, want in zip(values.shape, shape)])
+
+
+def narrow(at, values):
+    pieces = [
+        values[..., n * at.value_rows : (n + 1) * at.value_rows, :] for n in range(at.pieces)
+    ]
+    return jnp.concatenate(pieces, -1)
+
+
+def widen(at, values):
+    pieces = [values[..., n * 128 : (n + 1) * 128] for n in range(at.pieces)]
+    return jnp.concatenate(pieces, -2)
+
+
+def pack_small(at, encoder_in, head_action, gain, shift, bias, wide=None):
+    lead = encoder_in.shape[:-2]
+    rows = [
         encoder_in,
-        latent_out,
-        head_latent,
-        head_action,
-        head_task,
-        head_middle,
-        value_out,
-        policy_out,
-        task_table,
-        norm_gain,
-        norm_shift,
-        latent_bias,
-        value_bias,
-        policy_bias,
-    ) = members
-    (
-        encoder_in,
-        latent_out,
-        head_latent,
-        head_action,
-        head_task,
-        head_middle,
-        task_table,
-        norm_gain,
-        norm_shift,
-        latent_bias,
-    ) = (
-        lax.all_gather(encoder_in, "lat", axis=1, tiled=True),
-        lax.all_gather(latent_out, "lat", axis=2, tiled=True),
-        lax.all_gather(head_latent, "lat", axis=2, tiled=True),
-        lax.all_gather(head_action, "lat", axis=2, tiled=True),
-        lax.all_gather(head_task, "lat", axis=2, tiled=True),
-        lax.all_gather(head_middle, "lat", axis=2, tiled=True),
-        lax.all_gather(task_table, "lat", axis=1, tiled=True),
-        lax.all_gather(norm_gain, "lat", axis=1, tiled=True),
-        lax.all_gather(norm_shift, "lat", axis=1, tiled=True),
-        lax.all_gather(latent_bias, "lat", axis=1, tiled=True),
-    )
+        head_action.reshape(lead + (at.acts, at.cols)),
+        gain,
+        shift,
+        fill(bias, lead + (2, at.cols)),
+    ]
+    if wide is not None:
+        rows.append(
+            jnp.broadcast_to(
+                fill(wide, (at.wide_rows * at.pieces, 128)).reshape(at.wide_rows, at.cols),
+                lead + (at.wide_rows, at.cols),
+            )
+        )
+    rows = jnp.concatenate(rows, -2)
+    return fill(rows, lead + (at.small_rows, at.cols))
+
+
+def pack_own(at, members):
+    (encoder_in, latent_out, head_latent, head_action, head_task, head_middle, value_out,
+     policy_out, task_table, norm_gain, norm_shift, latent_bias, value_bias, policy_bias) = members
+    small = pack_small(at, encoder_in, head_action, norm_gain, norm_shift, latent_bias)
+    small = lax.dynamic_slice_in_dim(small, lax.axis_index("batch") * at.value_rows, at.value_rows, 0)
+    lat = lax.axis_index("lat")
+    out = jnp.concatenate(
+        [fill(value_out, value_out.shape[:2] + (128,)), fill(policy_out, (policy_out.shape[0], 128))[None]], 0
+    )
+    out = narrow(at, lax.dynamic_slice_in_dim(out, lat * at.share, at.share, 1))
+    out = jnp.concatenate([small[None], out], 0)
+    table = fill(task_table.reshape(1, 1, -1), (at.heads, at.head_rows - at.table_at, at.cols))
+    heads = jnp.concatenate([head_latent, head_middle, out, head_task, table], 1)
+    tail = latent_out.reshape(2 * at.out_rows, at.cols)
+    return jnp.concatenate([heads.reshape(at.heads * at.head_rows, at.cols), tail], 0)
+
+
+def by_device(at, gathered):
+    first = gathered[0]
+    second = jnp.swapaxes(gathered[1], 0, 1)
+    both = jnp.stack([first, second], 0)
+    return both.transpose(3, 2, 1, 0, 4, 5).reshape((at.batches, at.lats) + gathered.shape[-2:])
+
+
+def from_device(at, values, side):
+    both = values.reshape((at.batches // side, side, side, 2) + values.shape[-2:])
+    both = both.transpose(3, 2, 1, 0, 4, 5)
+    return jnp.stack([both[0], jnp.swapaxes(both[1], 0, 1)], 0)
+
+
+def unpack_all(at, gathered, dims):
+    every = by_device(at, gathered)
+    split = at.heads * at.head_rows
+    heads = every[:, :, :split].reshape(at.batches, at.lats, at.heads, at.head_rows, at.cols)
+
+    def square(first, count):
+        part = heads[:, :, :, first : first + count].transpose(2, 0, 3, 1, 4)
+        return part.reshape(at.heads, at.batches * count, at.lats * at.cols)
+
+    head_latent = square(0, at.latent_rows)
+    head_middle = square(at.middle_at, at.middle_rows)
+    head_task = square(at.task_at, at.task_rows)
+    out = widen(at, heads[:, :, 1:, at.value_at : at.value_at + at.value_rows])
+    out = out.transpose(2, 0, 1, 3, 4).reshape(at.heads - 1, -1, 128)
+    value_out, policy_out = out[:-1, :, : dims["bins"]], out[-1, :, : dims["lin"]]
+    small = heads[:, :, 0, at.value_at : at.value_at + at.value_rows].transpose(1, 0, 2, 3)
+    small = small.reshape(at.lats, at.small_rows, at.cols).transpose(1, 0, 2)
+
+    def wide(first, count):
+        return small[first : first + count].reshape(count, -1)
+
+    encoder_in = wide(0, at.obs)
+    head_action = wide(at.obs, at.acts).reshape(at.heads - 1, -1, at.lats * at.cols)
+    norm_gain = wide(at.obs + at.acts, at.norms)
+    norm_shift = wide(at.obs + at.acts + at.norms, at.norms)
+    latent_bias = small[at.bias_at : at.bias_at + 2, :, : at.latent_cols].reshape(2, -1)
+    tr, tc = at.table_shape
+    table = heads[:, :, 0, at.table_at, : tr * tc].reshape(at.batches, at.lats, tr, tc)
+    task_table = table.transpose(0, 2, 1, 3).reshape(at.batches * tr, at.lats * tc)
+    latent_out = every[:, :, split:].reshape(at.batches, at.lats, 2, at.middle_rows, at.latent_cols)
+    latent_out = latent_out.transpose(2, 0, 3, 1, 4).reshape(2, at.batches * at.middle_rows, -1)
+    return (encoder_in, latent_out, head_latent, head_action, head_task, head_middle, value_out,
+            policy_out, task_table, norm_gain, norm_shift, latent_bias)
+
+
+def pack_grads(at, grads, side):
+    (encoder_in, latent_out, head_latent, head_action, head_task, head_middle, value_out,
+     policy_out, task_table, norm_gain, norm_shift, latent_bias, value_bias, policy_bias) = (
+        g.astype(jnp.bfloat16) for g in grads
+    )
+    nb, nl = at.batches, at.lats
+
+    def square(values, rows, cols):
+        lead = values.shape[0]
+        return values.reshape(lead, nb, rows, nl, cols).transpose(1, 3, 0, 2, 4)
+
+    hidden = nb * at.middle_rows
+    out = jnp.concatenate(
+        [fill(value_out, value_out.shape[:2] + (128,)), fill(policy_out, (hidden, 128))[None]], 0
+    )
+    out = narrow(at, out.reshape(at.heads - 1, nb, nl, at.share, 128).transpose(1, 2, 0, 3, 4))
+
+    def cut(values):
+        return values.reshape(values.shape[0], nl, -1).transpose(1, 0, 2)
+
+    wide = jnp.concatenate([fill(value_bias, (value_bias.shape[0], 128)), fill(policy_bias, (128,))[None]], 0)
+    small = pack_small(
+        at, cut(encoder_in), cut(head_action.reshape(at.acts, -1)), cut(norm_gain), cut(norm_shift),
+        cut(latent_bias), wide,
+    )
+    small = small.reshape(nl, nb, 1, at.value_rows, at.cols).transpose(1, 0, 2, 3, 4)
+    tr, tc = at.table_shape
+    table = task_table.reshape(nb, tr, nl, tc).transpose(0, 2, 1, 3).reshape(nb, nl, 1, 1, tr * tc)
+    table = fill(table, (nb, nl, at.heads, at.head_rows - at.table_at, at.cols))
+    heads = jnp.concatenate(
+        [
+            square(head_latent, at.latent_rows, at.cols),
+            square(head_middle, at.middle_rows, at.cols),
+            jnp.concatenate([small, out], 2),
+            square(head_task, at.task_rows, at.cols),
+            table,
+        ],
+        3,
+    ).reshape(nb, nl, at.heads * at.head_rows, at.cols)
+    tail = square(latent_out, at.middle_rows, at.latent_cols).reshape(nb, nl, 2 * at.out_rows, at.cols)
+    return from_device(at, jnp.concatenate([heads, tail], 2), side)
+
+
+def unpack_own(at, total, dims):
+    split = at.heads * at.head_rows
+    heads = total[:split].reshape(at.heads, at.head_rows, at.cols)
+    part = heads[:, at.value_at : at.value_at + at.value_rows].astype(jnp.bfloat16)
+    small = lax.all_gather(part[0], "batch", axis=0, tiled=True).astype(jnp.float32)
+    out = widen(at, lax.all_gather(part[1:], "lat", axis=0).astype(jnp.float32))
+    out = out.transpose(1, 0, 2, 3).reshape(at.heads - 1, at.middle_rows, 128)
+    tr, tc = at.table_shape
+    wide = small[at.wide_at : at.wide_at + at.wide_rows].reshape(at.wide_rows * at.pieces, 128)
+    norm_at = at.obs + at.acts
     return (
-        encoder_in,
-        latent_out,
-        head_latent,
-        head_action,
-        head_task,
-        head_middle,
-        value_out,
-        policy_out,
-        task_table,
-        norm_gain,
-        norm_shift,
-        latent_bias,
-        value_bias,
-        policy_bias,
-    )
-
-
-def through_batch(members):
-    (
-        encoder_in,
-        latent_out,
-        head_latent,
-        head_action,
-        head_task,
-        head_middle,
-        value_out,
-        policy_out,
-        task_table,
-        norm_gain,
-        norm_shift,
-        latent_bias,
-        value_bias,
-        policy_bias,
-    ) = members
-    latent_out, head_latent, head_task, head_middle, value_out, policy_out, task_table = (
-        lax.all_gather(latent_out, "batch", axis=1, tiled=True),
-        lax.all_gather(head_latent, "batch", axis=1, tiled=True),
-        lax.all_gather(head_task, "batch", axis=1, tiled=True),
-        lax.all_gather(head_middle, "batch", axis=1, tiled=True),
-        lax.all_gather(value_out, "batch", axis=1, tiled=True),
-        lax.all_gather(policy_out, "batch", axis=0, tiled=True),
-        lax.all_gather(task_table, "batch", axis=0, tiled=True),
-    )
-    return (
-        encoder_in,
-        latent_out,
-        head_latent,
-        head_action,
-        head_task,
-        head_middle,
-        value_out,
-        policy_out,
-        task_table,
-        norm_gain,
-        norm_shift,
-        latent_bias,
-        value_bias,
-        policy_bias,
-    )
-
-
-def reduce_batch(grads):
-    (
-        encoder_in,
-        latent_out,
-        head_latent,
-        head_action,
-        head_task,
-        head_middle,
-        value_out,
-        policy_out,
-        task_table,
-        norm_gain,
-        norm_shift,
-        latent_bias,
-        value_bias,
-        policy_bias,
-    ) = grads
-    latent_out, head_latent, head_task, head_middle, value_out, policy_out, task_table = (
-        lax.psum_scatter(
-            latent_out.astype(jnp.bfloat16), "batch", scatter_dimension=1, tiled=True
-        ).astype(jnp.float32),
-        lax.psum_scatter(
-            head_latent.astype(jnp.bfloat16), "batch", scatter_dimension=1, tiled=True
-        ).astype(jnp.float32),
-        lax.psum_scatter(
-            head_task.astype(jnp.bfloat16), "batch", scatter_dimension=1, tiled=True
-        ).astype(jnp.float32),
-        lax.psum_scatter(
-            head_middle.astype(jnp.bfloat16), "batch", scatter_dimension=1, tiled=True
-        ).astype(jnp.float32),
-        lax.psum_scatter(
-            value_out.astype(jnp.bfloat16), "batch", scatter_dimension=1, tiled=True
-        ).astype(jnp.float32),
-        lax.psum_scatter(
-            policy_out.astype(jnp.bfloat16), "batch", scatter_dimension=0, tiled=True
-        ).astype(jnp.float32),
-        lax.psum_scatter(
-            task_table.astype(jnp.bfloat16), "batch", scatter_dimension=0, tiled=True
-        ).astype(jnp.float32),
-    )
-    encoder_in, head_action, norm_gain, norm_shift, latent_bias, value_bias, policy_bias = (
-        lax.psum(encoder_in.astype(jnp.bfloat16), "batch").astype(jnp.float32),
-        lax.psum(head_action.astype(jnp.bfloat16), "batch").astype(jnp.float32),
-        lax.psum(norm_gain.astype(jnp.bfloat16), "batch").astype(jnp.float32),
-        lax.psum(norm_shift.astype(jnp.bfloat16), "batch").astype(jnp.float32),
-        lax.psum(latent_bias.astype(jnp.bfloat16), "batch").astype(jnp.float32),
-        lax.psum(value_bias.astype(jnp.bfloat16), "batch").astype(jnp.float32),
-        lax.psum(policy_bias.astype(jnp.bfloat16), "batch").astype(jnp.float32),
-    )
-    return (
-        encoder_in,
-        latent_out,
-        head_latent,
-        head_action,
-        head_task,
-        head_middle,
-        value_out,
-        policy_out,
-        task_table,
-        norm_gain,
-        norm_shift,
-        latent_bias,
-        value_bias,
-        policy_bias,
-    )
-
-
-def reduce_lat(grads):
-    (
-        encoder_in,
-        latent_out,
-        head_latent,
-        head_action,
-        head_task,
-        head_middle,
-        value_out,
-        policy_out,
-        task_table,
-        norm_gain,
-        norm_shift,
-        latent_bias,
-        value_bias,
-        policy_bias,
-    ) = grads
-    (
-        encoder_in,
-        latent_out,
-        head_latent,
-        head_action,
-        head_task,
-        head_middle,
-        task_table,
-        norm_gain,
-        norm_shift,
-        latent_bias,
-    ) = (
-        lax.psum_scatter(
-            encoder_in.astype(jnp.bfloat16), "lat", scatter_dimension=1, tiled=True
-        ).astype(jnp.float32),
-        lax.psum_scatter(
-            latent_out.astype(jnp.bfloat16), "lat", scatter_dimension=2, tiled=True
-        ).astype(jnp.float32),
-        lax.psum_scatter(
-            head_latent.astype(jnp.bfloat16), "lat", scatter_dimension=2, tiled=True
-        ).astype(jnp.float32),
-        lax.psum_scatter(
-            head_action.astype(jnp.bfloat16), "lat", scatter_dimension=2, tiled=True
-        ).astype(jnp.float32),
-        lax.psum_scatter(
-            head_task.astype(jnp.bfloat16), "lat", scatter_dimension=2, tiled=True
-        ).astype(jnp.float32),
-        lax.psum_scatter(
-            head_middle.astype(jnp.bfloat16), "lat", scatter_dimension=2, tiled=True
-        ).astype(jnp.float32),
-        lax.psum_scatter(
-            task_table.astype(jnp.bfloat16), "lat", scatter_dimension=1, tiled=True
-        ).astype(jnp.float32),
-        lax.psum_scatter(
-            norm_gain.astype(jnp.bfloat16), "lat", scatter_dimension=1, tiled=True
-        ).astype(jnp.float32),
-        lax.psum_scatter(
-            norm_shift.astype(jnp.bfloat16), "lat", scatter_dimension=1, tiled=True
-        ).astype(jnp.float32),
-        lax.psum_scatter(
-            latent_bias.astype(jnp.bfloat16), "lat", scatter_dimension=1, tiled=True
-        ).astype(jnp.float32),
-    )
-    value_out, policy_out, value_bias, policy_bias = (
-        lax.psum(value_out.astype(jnp.bfloat16), "lat").astype(jnp.float32),
-        lax.psum(policy_out.astype(jnp.bfloat16), "lat").astype(jnp.float32),
-        lax.psum(value_bias.astype(jnp.bfloat16), "lat").astype(jnp.float32),
-        lax.psum(policy_bias.astype(jnp.bfloat16), "lat").astype(jnp.float32),
-    )
-    return (
-        encoder_in,
-        latent_out,
-        head_latent,
-        head_action,
-        head_task,
-        head_middle,
-        value_out,
-        policy_out,
-        task_table,
-        norm_gain,
-        norm_shift,
-        latent_bias,
-        value_bias,
-        policy_bias,
-    )
-
-
-def gather_all(members):
-    return through_batch(through_lat(members))
-
-
-def reduce_all(grads):
-    return reduce_lat(reduce_batch(grads))
-
+        small[: at.obs],
+        total[split:].reshape(2, at.middle_rows, at.latent_cols),
+        heads[:, : at.latent_rows],
+        small[at.obs : norm_at].reshape(at.heads - 1, -1, at.cols),
+        heads[:, at.task_at : at.table_at],
+        heads[:, at.middle_at : at.value_at],
+        out[:-1, :, : dims["bins"]],
+        out[-1, :, : dims["lin"]],
+        heads[0, at.table_at, : tr * tc].reshape(tr, tc),
+        small[norm_at : norm_at + at.norms],
+        small[norm_at + at.norms : at.bias_at],
+        small[at.bias_at : at.wide_at, : at.latent_cols],
+        wide[: at.heads - 2, : dims["bins"]],
+        wide[at.heads - 2, : dims["lin"]],
+    )
 
 def local(
     observations,
@@ -342,39 +650,29 @@
     value_bias,
     policy_bias,
 ):
-    (
-        encoder_in,
-        latent_out,
-        head_latent,
-        head_action,
-        head_task,
-        head_middle,
-        value_out,
-        policy_out,
-        task_table,
-        norm_gain,
-        norm_shift,
-        latent_bias,
-        value_bias,
-        policy_bias,
-    ) = gather_all(
-        (
-            encoder_in,
-            latent_out,
-            head_latent,
-            head_action,
-            head_task,
-            head_middle,
-            value_out,
-            policy_out,
-            task_table,
-            norm_gain,
-            norm_shift,
-            latent_bias,
-            value_bias,
-            policy_bias,
-        )
-    )
+    batches, lats = lax.axis_size("batch"), lax.axis_size("lat")
+    depth, side = major_minor(batches)
+    members = (encoder_in, latent_out, head_latent, head_action, head_task, head_middle, value_out,
+               policy_out, task_table, norm_gain, norm_shift, latent_bias, value_bias, policy_bias)
+    at = Rows(
+        {
+            "head_latent": head_latent.shape,
+            "head_middle": head_middle.shape,
+            "head_task": head_task.shape,
+            "latent_out": latent_out.shape,
+            "task_table": task_table.shape,
+            "encoder_in": encoder_in.shape,
+            "head_action": head_action.shape,
+            "norm_gain": norm_gain.shape,
+        },
+        batches,
+        lats,
+    )
+    dims = {"bins": value_out.shape[2], "lin": policy_out.shape[1]}
+    mine = pack_own(at, members)
+    gathered = gather_all(mine, depth, side, at.total // CHUNK_ROWS)
+    (encoder_in, latent_out, head_latent, head_action, head_task, head_middle, value_out,
+     policy_out, task_table, norm_gain, norm_shift, latent_bias) = unpack_all(at, gathered, dims)
     bf16 = jnp.bfloat16
     seq_count = observations.shape[0]
     horizon = actions.shape[1]
@@ -573,8 +871,8 @@
     grad_norm_shift = jnp.concatenate(
         [shift_enc[None], shift_dyn1[None], shift_dyn2[None], head_shifts], 0
     )
-    reduced = reduce_all(
-        (
+    grads = (
+
             grad_encoder_in,
             jnp.stack([grad_latent_enc, grad_latent_dyn], 0),
             jnp.concatenate([grad_latent_in_dyn[None], grad_latent_heads], 0),
@@ -590,7 +888,9 @@
             grad_value_bias,
             grad_policy_bias,
         )
-    )
+    parts = pack_grads(at, grads, side)
+    total = scatter_sum(parts, depth, side, at.total // CHUNK_ROWS)
+    reduced = unpack_own(at, total, dims)
     return (
         grad_observations,
         reduced[0],

time: 2110 us -> 1850 us (0.88)
  waiting for transfers between devices: 1150 us -> 0 us
  local copies, waits for them, and re-layouts: 309 us -> 834 us
  Pallas kernels: 0 us -> 369 us
  blocking collectives: 118 us -> 36.3 us
  other arithmetic: 232 us -> 300 us
  matrix products: 267 us -> 289 us
    reduce_scatter x11 -> x0, waiting for transfers between devices: 628 us -> none  [the longest x1 285 us: reduce_batch(): lax.psum_scatter(head_middle.astype(jnp.bfloat16), 'batch', scatter_dimen...]
    pallas_call x0 -> x2, Pallas kernels: none -> 369 us  [the longest x1 195 us: gather_all(): pl.pallas_call(functools.partial(gather_kernel, depth, side, chunks, rows...]
    all_gather x7 -> x0, waiting for transfers between devices: 296 us -> none  [the longest x1 225 us: through_batch(): lax.all_gather(head_middle, 'batch', axis=1, tiled=True)]
    concatenate x0 -> x14, local copies, waits for them, and re-layouts: none -> 207 us  [the longest x1 146 us: pack_grads(): jnp.concatenate([square(head_latent, at.latent_rows, at.cols), square(hea...]
    slice x2 -> x45, local copies, waits for them, and re-layouts: 3.15 us -> 206 us  [the longest x4 63.1 us: local(): head_latent[1:]]
    unnamed x27 -> x0, waiting for transfers between devices: 156 us -> none
    transpose x0 -> x13, local copies, waits for them, and re-layouts: none -> 75.7 us  [the longest x1 24.7 us: by_device(): both.transpose(3, 2, 1, 0, 4, 5)]
    transpose x0 -> x9, other arithmetic: none -> 75.6 us  [the longest x3 25.7 us: square(): return values.reshape(lead, nb, rows, nl, cols).transpose(1, 3, 0, 2, 4)]
  transfers between devices with their start and end apart: 23 -> 0, of which waited for: 14 -> 0; matrix products, arithmetic and copies ran while one was open for 24% -> 0% of each run, Pallas kernels for 0% -> 0%
where the time goes in v1:
time: 1850 us; the launch traced here: 1830 us
  local copies, waits for them, and re-layouts  834 us (45%)
  Pallas kernels  369 us (20%)
  other arithmetic  300 us (16%)
  matrix products  289 us (16%)
  blocking collectives  36.3 us (2%)
    dot_general x39, matrix products, contract(): return jnp.einsum(form, left, right, preferred_element_type=jnp.float32)  256 us
    pallas_call x1, Pallas kernels, gather_all(): pl.pallas_call(functools.partial(gather_kernel, depth, side, chunks, rows...  195 us
    pallas_call x1, Pallas kernels, scatter_sum(): pl.pallas_call(functools.partial(scatter_kernel, depth, side, chunks, chu...  174 us
    concatenate x1, local copies, waits for them, and re-layouts, pack_grads(): jnp.concatenate([square(head_latent, at.latent_rows, at.cols), square(hea...  146 us
    slice x4, local copies, waits for them, and re-layouts, local(): head_latent[1:]  63.1 us
    div x10, local copies, waits for them, and re-layouts, simnorm(): return jax.nn.softmax(groups, -1).reshape(values.shape)  55.7 us
    another operation x3, local copies, waits for them, and re-layouts, simnorm(): return jax.nn.softmax(groups, -1).reshape(values.shape)  51.7 us
    unnamed x478, local copies, waits for them, and re-layouts  48.7 us

profile of v1, /device:TPU:0, one launch (start us, length us, event | category | flops | bytes accessed | tf_op | source)
XLA Modules:
  0.0 1832.1 jit_solution(1205067836979189933)
XLA Ops:
  24.7 195.1 %gather_weights.1 = bf16[2,2,2,4,2240,256]{5,4,3,2,1,0:T(8,128)(2,1)} custom-call(bf16[2240,256]{1,0:T(8,128)(2,1)} %pad_maximum_fusion.11.mine_ref), custom_call_target="tpu_custom_call" | custom-call | tf_op jit(solution)/shard_map/gather_weights/pallas_call | solution.py:219
  219.8 24.4 %fusion.250 = (bf16[1,2,2,4,2240,256]{5,4,3,2,1,0:T(8,128)(2,1)}, bf16[1,2,2,4,2240,256]{5,4,3,1,2,0:T(8,128)(2,1)}) fusion(bf16[2,2,2,4,2240,256]{5,4,3,2,1,0:T(8,128)(2,1)} %gather_weights.1), kind=kLoop, calls=%fused_computation.521 | loop fusion | bytes 73400320 | tf_op jit(solution)/shard_map/slice | solution.py:514
  244.2 24.7 %maximum_bitcast_fusion = bf16[4,2,2,2,2240,256]{5,4,0,2,1,3:T(8,128)(2,1)} fusion(bf16[1,2,2,4,2240,256]{5,4,3,1,2,0:T(8,128)(2,1)} %get-tuple-element.205, bf16[1,2,2,4,2240,256]{5,4,3,2,1,0:T(8,128)(2,1)} %get-tuple-element.204), kind=kLoop, calls=%fused_computation.6 | loop fusion | flops 73400320 | bytes 73400320 | tf_op jit(solution)/shard_map/transpose | solution.py:517
  268.9 24.7 %copy.426 = bf16[4,2,2,2,2240,256]{5,4,3,2,1,0:T(8,128)(2,1)} copy(bf16[4,2,2,2,2240,256]{5,4,0,2,1,3:T(8,128)(2,1)} %maximum_bitcast_fusion) | data formatting | bytes 73400320 | tf_op jit(solution)/shard_map/transpose | solution.py:517
  295.7 22.9 %slice.416 = bf16[8,4,2048,256]{3,2,1,0:T(8,128)(2,1)} slice(bf16[8,4,2240,256]{3,2,1,0:T(8,128)(2,1)} %bitcast.509), slice={[0:8], [0:4], [0:2048], [0:256]} | slice | bytes 67108864 | tf_op jit(solution)/shard_map/slice | solution.py:529
  419.6 24.9 %copy.427 = bf16[7,8,96,4,256]{4,3,2,1,0:T(4,128)(2,1)} copy(bf16[7,8,96,4,256]{4,2,0,3,1:T(8,128)(2,1)S(1)} %slice.441) | data formatting | bytes 22020096 | tf_op jit(solution)/shard_map/slice | solution.py:730
  460.1 24.1 %slice.365 = bf16[7,1024,1024]{2,1,0:T(8,128)(2,1)} reshape(bf16[7,8,128,4,256]{4,3,2,1,0:T(4,128)(2,1)} %copy.457) | data formatting | bytes 29360128 | tf_op jit(solution)/shard_map/slice | solution.py:732
  488.5 18.6 %reshape.966 = bf16[7,768,1024,1]{2,1,0,3:T(8,128)(2,1)} reshape(bf16[7,8,96,4,256]{4,3,2,1,0:T(4,128)(2,1)} %copy.427) | data formatting | bytes 22020096 | tf_op jit(solution)/shard_map/slice | solution.py:730
  507.1 18.5 %slice.333 = bf16[7,768,1024]{2,1,0:T(8,128)(2,1)} reshape(bf16[7,8,96,4,256]{4,3,2,1,0:T(4,128)(2,1)} %copy.427) | data formatting | bytes 22020096 | tf_op jit(solution)/shard_map/slice | solution.py:730
  557.6 26.8 %sub.253 = f32[192,4,768]{2,1,0:T(4,128)} reshape(f32[768,96,8]{2,1,0:T(8,128)} %sub.252.clone) | data formatting | bytes 4718592 | tf_op jit(solution)/shard_map/jvp()/sub | solution.py:41
  597.1 27.2 %div.316 = f32[192,4,768]{2,1,0:T(4,128)} reshape(f32[768,96,8]{2,1,0:T(8,128)} %div.315.clone) | data formatting | bytes 4718592 | tf_op jit(solution)/shard_map/jvp()/div | solution.py:41
  669.0 30.1 %fusion.265 = (f32[7,576]{1,0:T(8,128)S(1)}, f32[7,576,1024]{2,1,0:T(8,128)}) fusion(f32[7,576,1024]{2,0,1:T(8,128)} %bitcast.527, f32[6,576,1024]{2,1,0:T(8,128)} %convolution_bitcast_fusion, bf16[576,768,1]{1,0,2:T(8,128)(2,1)S(1)} %reshape.964, bf16[7,768,1024]{2,1,0:T(8,128)(2,1)} %slice.333), kind=kOutput, calls=%fused_computation.536 | convolution fusion | flops 6354169856 | bytes 59096832 | tf_op jit(solution)/shard_map/rl,klf->krf/dot_general | solution.py:26
  746.6 24.0 %fusion.266 = (f32[7,576]{1,0:T(8,128)S(1)}, f32[7,576,1024]{2,1,0:T(8,128)}) fusion(bf16[7,1024,1024]{2,1,0:T(8,128)(2,1)} %slice.365, f32[7,576,1024]{2,1,0:T(8,128)S(1)} %bitcast.507, f32[7,1024]{1,0:T(8,128)S(1)} %copy-done.147, f32[7,1024]{1,0:T(8,128)S(1)} %copy-done.116, f32[7,576]{1,0:T(8,128)S(1)} %fusion.177, ...), kind=kOutput, calls=%fused_computation.537 | convolution fusion | flops 8509386752 | bytes 47815936 | tf_op jit(solution)/shard_map/krf,kfg->krg/dot_general | solution.py:26
  778.2 37.3 %fusion.10 = bf16[7,576,1024]{2,1,0:T(8,128)(2,1)S(1)} fusion(f32[7,576,1024]{2,1,0:T(8,128)} %get-tuple-element.260, f32[7,1024]{1,0:T(8,128)S(1)} %copy-done.115, f32[7,1024]{1,0:T(8,128)S(1)} %copy-done.108, f32[7,576]{1,0:T(8,128)S(1)} %fusion.178, f32[7,576]{1,0:T(8,128)S(1)} %broadcast_multiply_fusion.1), kind=kLoop, calls=%fused_computation.38 | loop fusion | flops 49545216 | bytes 24862208 | tf_op jit(solution)/shard_map/convert_element_type | solution.py:733
  844.4 30.4 %multiply_reduce_fusion = (bf16[7,1024]{1,0:T(8,128)(2,1)S(1)}, f32[7,576]{1,0:T(8,128)S(1)}, bf16[7,1024]{1,0:T(8,128)(2,1)S(1)}, f32[7,576,1024]{2,1,0:T(8,128)S(1)}) fusion(f32[7,576,1024]{2,1,0:T(8,128)} %get-tuple-element.260, f32[7,576]{1,0:T(8,128)S(1)} %fusion.178, f32[7,576]{1,0:T(8,128)S(1)} %broadcast_multiply_fusion.1, ...), kind=kLoop, calls=%fused_computation.27 | loop fusion | flops 123844672 | bytes 49679616 | tf_op jit(solution)/shard_map/transpose(jvp())/reduce_sum | solution.py:36
  883.4 39.0 %fusion.232 = (bf16[7,1024]{1,0:T(8,128)(2,1)S(1)}, f32[7,576]{1,0:T(8,128)S(1)}, f32[7,576,1024]{2,1,0:T(8,128)}) fusion(f32[7,1024]{1,0:T(8,128)S(1)} %copy-done.116, f32[7,576,1024]{2,1,0:T(8,128)} %get-tuple-element.258, f32[7,576]{1,0:T(8,128)S(1)} %broadcast_multiply_fusion.2, f32[7,1024]{1,0:T(8,128)S(1)} %copy-done.147, f32[7,576]{1,0:T(8,128)S(1)} %fusion.177, ...), kind=kOutput, calls=%fused_computation.508 | convolution fusion | flops 8575439872 | bytes 64361472 | tf_op jit(solution)/shard_map/krg,kfg->krf/dot_general | solution.py:26
  922.4 30.9 %convolution_convert_fusion = bf16[7,1024,1024]{2,1,0:T(8,128)(2,1)} fusion(f32[7,576,1024]{2,1,0:T(8,128)} %get-tuple-element.190, f32[7,576]{1,0:T(8,128)S(1)} %negate_multiply_fusion.1, f32[7,576,1024]{2,1,0:T(8,128)} %get-tuple-element.258, f32[7,1024]{1,0:T(8,128)S(1)} %copy-done.147, f32[7,1024]{1,0:T(8,128)S(1)} %copy-done.116, ...), kind=kOutput, calls=%fused_computation.48 | convolution fusion | flops 8520859648 | bytes 47815936 | tf_op jit(solution)/shard_map/krf,krg->kfg/dot_general | solution.py:26
  953.3 24.6 %concatenate.125 = bf16[7,8,128,4,256]{4,3,2,1,0:T(4,128)(2,1)} reshape(bf16[7,1024,1024]{2,1,0:T(8,128)(2,1)} %convolution_convert_fusion) | data formatting | bytes 29360128 | tf_op jit(solution)/shard_map/concatenate | solution.py:881
  977.9 14.4 copy.484
  1036.8 33.0 %fusion.62 = f32[192,3,768]{2,0,1:T(8,128)S(1)} fusion(bf16[7,768,1024,1]{2,1,0,3:T(8,128)(2,1)} %reshape.966, bf16[192,3,1024,7]{2,3,1,0:T(8,128)(2,1)} %bitcast.535), kind=kOutput, calls=%fused_computation.155 | convolution fusion | flops 6341787648 | bytes 21037056 | tf_op jit(solution)/shard_map/krf,klf->rl/dot_general | solution.py:26
  1153.5 14.0 maximum_bitcast_fusion.1
  1179.4 14.7 copy.482
  1194.1 18.9 %concatenate.122 = bf16[7,8,96,4,256]{4,3,2,1,0:T(4,128)(2,1)} reshape(bf16[7,768,1024]{2,1,0:T(8,128)(2,1)} %copy.482) | data formatting | bytes 22020096 | tf_op jit(solution)/shard_map/concatenate | solution.py:878
  1229.3 14.7 copy.490
  1278.1 23.2 %reshape_reshape.8 = f32[768,96,8]{2,1,0:T(8,128)} reshape(f32[192,4,768]{2,1,0:T(4,128)S(1)} %copy.475) | data formatting | bytes 4718592 | tf_op jit(solution)/shard_map/transpose(jvp())/reshape;reshape | solution.py:41
  1301.4 26.6 %copy.478 = f32[768,96,8]{0,2,1:T(8,128)} copy(f32[768,96,8]{2,1,0:T(8,128)} %reshape_reshape.8) | data formatting | bytes 4718592 | tf_op jit(solution)/shard_map/transpose(jvp())/reshape;reshape | solution.py:41
  1375.2 145.5 %concatenate.142 = bf16[8,4,8,256,256]{4,3,2,1,0:T(8,128)(2,1)} concatenate(bf16[8,4,8,96,256]{4,3,2,1,0:T(8,128)(2,1)} %copy.495, bf16[8,4,8,128,256]{4,3,2,1,0:T(8,128)(2,1)} %maximum_bitcast_fusion.1, bf16[8,4,8,16,256]{4,3,2,1,0:T(8,128)(2,1)} %copy.496, bf16[8,4,8,12,256]{4,3,2,1,0:T(8,128)(2,1)} %bitcast.536, bf16[8,4,8,4,256]{4,3,2,1,0:T(4,128)(2,1)} %pad.89.clone), dimensions={3} | concatenate | bytes 67108864 | tf_op jit(solution)/shard_map/concatenate | solution.py:590
  1533.1 24.7 %copy_bitcast_fusion = bf16[2,2,2,4,2240,256]{5,4,3,1,2,0:T(8,128)(2,1)} fusion(bf16[4,2,2,2,192,256]{5,4,3,2,1,0:T(8,128)(2,1)S(1)} %concatenate.144, bf16[4,2,2,2,2048,256]{5,4,3,2,1,0:T(8,128)(2,1)} %bitcast.519), kind=kLoop, calls=%fused_computation.9 | loop fusion | flops 73400320 | bytes 73400320 | tf_op jit(solution)/shard_map/transpose | solution.py:522
  1557.8 24.4 %fusion.249 = (bf16[1,2,2,4,2240,256]{5,4,3,1,2,0:T(8,128)(2,1)}, bf16[1,2,2,4,2240,256]{5,4,3,2,1,0:T(8,128)(2,1)}) fusion(bf16[2,2,2,4,2240,256]{5,4,3,1,2,0:T(8,128)(2,1)} %copy_bitcast_fusion), kind=kLoop, calls=%fused_computation.520 | loop fusion | bytes 73400320 | tf_op jit(solution)/shard_map/slice | solution.py:523
  1582.2 24.7 %pad_maximum_fusion.1.parts_ref = bf16[2,2,2,4,2240,256]{5,4,3,2,1,0:T(8,128)(2,1)} fusion(bf16[1,2,2,4,2240,256]{5,4,3,2,1,0:T(8,128)(2,1)} %get-tuple-element.203, bf16[1,2,2,4,2240,256]{5,4,3,1,2,0:T(8,128)(2,1)} %get-tuple-element.202), kind=kLoop, calls=%fused_computation.8 | loop fusion | flops 73400320 | bytes 73400320 | tf_op jit(solution)/shard_map/stack | solution.py:523
  1606.9 174.1 %scatter_gradients.1 = f32[2240,256]{1,0:T(8,128)} custom-call(bf16[2,2,2,4,2240,256]{5,4,3,2,1,0:T(8,128)(2,1)} %pad_maximum_fusion.1.parts_ref), custom_call_target="tpu_custom_call" | custom-call | tf_op jit(solution)/shard_map/scatter_gradients/pallas_call | solution.py:408
  1787.0 30.6 %all-gather = bf16[1,128,256]{2,1,0:T(8,128)(2,1)S(1)} all-gather(bf16[1,16,256]{2,1,0:T(8,128)(2,1)S(1)} %slice.463), channel_id=2, replica_groups=mesh['batch'=8,'lat'=4] {'batch'}, dimensions={1}, use_global_device_ids=true | all-gather | bytes 73728 | tf_op jit(solution)/shard_map/all_gather | solution.py:608
  (835 shorter events, 596.0 us)
Async XLA Ops:
  0.6 19.3 %copy-start.128 = (bf16[192,3,6]{0,2,1:T(8,128)(2,1)S(1)}, bf16[192,3,6]{0,2,1:T(8,128)(2,1)}, u32[]{:S(2)}) copy-start(bf16[192,3,6]{0,2,1:T(8,128)(2,1)} %param.23) | copy-start | bytes 20740
  0.7 21.5 %copy-start.109 = (bf16[8,128,256]{2,1,0:T(8,128)(2,1)S(1)}, bf16[8,128,256]{2,1,0:T(8,128)(2,1)}, u32[]{:S(2)}) copy-start(bf16[8,128,256]{2,1,0:T(8,128)(2,1)} %param.33) | copy-start | bytes 1572868
  0.7 21.5 %copy-start.113 = (bf16[8,96,256]{2,1,0:T(8,128)(2,1)S(1)}, bf16[8,96,256]{2,1,0:T(8,128)(2,1)}, u32[]{:S(2)}) copy-start(bf16[8,96,256]{2,1,0:T(8,128)(2,1)} %param.30) | copy-start | bytes 1179652
  15.4 352.4 %copy-start.82 = (bf16[192,4,39]{2,1,0:T(4,128)(2,1)}, bf16[192,4,39]{2,1,0:T(4,128)(2,1)S(1)}, u32[]{:S(2)}) copy-start(bf16[192,4,39]{2,1,0:T(4,128)(2,1)S(1)} %copy.430) | copy-start | bytes 179716
  320.8 67.4 %copy-start.110 = (bf16[192,96,1]{1,0,2:T(8,128)(2,1)}, bf16[192,96,1]{1,0,2:T(8,128)(2,1)S(1)}, u32[]{:S(2)}) copy-start(bf16[192,96,1]{1,0,2:T(8,128)(2,1)S(1)} %fusion.91) | copy-start | bytes 110596
  328.8 40.1 %copy-start.139 = (f32[1,4,256]{2,0,1:T(1,128)}, f32[1,4,256]{2,0,1:T(1,128)S(1)}, u32[]{:S(2)}) copy-start(f32[1,4,256]{2,0,1:T(1,128)S(1)} %get-tuple-element.228) | copy-start | bytes 12292
  328.8 40.1 %copy-start.158 = (f32[1,4,256]{2,0,1:T(1,128)}, f32[1,4,256]{2,0,1:T(1,128)S(1)}, u32[]{:S(2)}) copy-start(f32[1,4,256]{2,0,1:T(1,128)S(1)} %get-tuple-element.269) | copy-start | bytes 12292
  419.5 24.9 %slice-start.12 = ((bf16[8,8,96,4,256]{4,2,0,3,1:T(8,128)(2,1)}), bf16[1,8,96,4,256]{4,2,0,3,1:T(8,128)(2,1)S(1)}, s32[]{:S(2)}) async-start(bf16[8,8,96,4,256]{4,2,0,3,1:T(8,128)(2,1)} %copy-done.4), calls=%async_computation.12 | async-start | bytes 3145728 | tf_op jit(solution)/shard_map/slice | solution.py:706
  446.1 219.0 %copy-start.2 = (bf16[96,8,4,256]{3,1,2,0:T(8,128)(2,1)}, bf16[96,8,4,256]{3,1,2,0:T(8,128)(2,1)S(1)}, u32[]{:S(2)}) copy-start(bf16[96,8,4,256]{3,1,2,0:T(8,128)(2,1)S(1)} %copy.525) | copy-start | bytes 4718596
  667.0 39.6 %copy-start.29 = (f32[192,1024]{1,0:T(8,128)}, f32[192,1024]{1,0:T(8,128)S(1)}, u32[]{:S(2)}) copy-start(f32[192,1024]{1,0:T(8,128)S(1)} %get-tuple-element.252) | copy-start | bytes 2359300
  667.4 66.9 %copy-start.178 = (f32[192]{0:T(256)}, f32[192]{0:T(256)S(1)}, u32[]{:S(2)}) copy-start(f32[192]{0:T(256)S(1)} %fusion.202) | copy-start | bytes 2308
  668.9 30.1 %copy-start.69 = (bf16[576,768,1]{1,0,2:T(8,128)(2,1)}, bf16[576,768,1]{1,0,2:T(8,128)(2,1)S(1)}, u32[]{:S(2)}) copy-start(bf16[576,768,1]{1,0,2:T(8,128)(2,1)S(1)} %reshape.964) | copy-start | bytes 2654212
  731.8 14.8 slice-start.6
  732.1 14.4 slice-start.7
  778.2 37.3 %copy-start.13 = (bf16[7,8,4,32,128]{4,3,2,1,0:T(8,128)(2,1)S(1)}, bf16[7,8,4,32,128]{4,3,2,1,0:T(8,128)(2,1)}, u32[]{:S(2)}) copy-start(bf16[7,8,4,32,128]{4,3,2,1,0:T(8,128)(2,1)} %copy.458) | copy-start | bytes 5505028
  778.2 37.3 %copy-start.210 = (f32[12]{0:T(128)S(1)}, f32[12]{0:T(128)}, u32[]{:S(2)}) copy-start(f32[12]{0:T(128)} %convert_element_type.283) | copy-start | bytes 148
  778.2 37.8 %copy-start.138 = (bf16[576,6]{0,1:T(8,128)(2,1)S(1)}, bf16[576,6]{0,1:T(8,128)(2,1)}, u32[]{:S(2)}) copy-start(bf16[576,6]{0,1:T(8,128)(2,1)} %reshape.925) | copy-start | bytes 20740
  778.2 37.8 %copy-start.146 = (f32[576]{0:T(1024)S(1)}, f32[576]{0:T(1024)}, u32[]{:S(2)}) copy-start(f32[576]{0:T(1024)} %copy-done.145) | copy-start | bytes 6916
  837.2 37.6 %slice-start.2 = ((s8[16515072]{0:T(1024)(128)(4,1)}), s8[3932160]{0:T(1024)(128)(4,1)S(1)}, s32[]{:S(2)}) async-start(s8[16515072]{0:T(1024)(128)(4,1)} %bitcast.504), calls=%async_computation.2 | async-start | bytes 7864320
  844.4 30.5 %slice-start.3 = ((s8[16515072]{0:T(1024)(128)(4,1)}), s8[4194304]{0:T(1024)(128)(4,1)S(1)}, s32[]{:S(2)}) async-start(s8[16515072]{0:T(1024)(128)(4,1)} %bitcast.504), calls=%async_computation.3 | async-start | bytes 8388608
  844.4 30.5 %slice-start.4 = ((s8[16515072]{0:T(1024)(128)(4,1)}), s8[4194304]{0:T(1024)(128)(4,1)S(1)}, s32[]{:S(2)}) async-start(s8[16515072]{0:T(1024)(128)(4,1)} %bitcast.504), calls=%async_computation.4 | async-start | bytes 8388608
  844.4 30.5 %slice-start.5 = ((s8[16515072]{0:T(1024)(128)(4,1)}), s8[4194304]{0:T(1024)(128)(4,1)S(1)}, s32[]{:S(2)}) async-start(s8[16515072]{0:T(1024)(128)(4,1)} %bitcast.504), calls=%async_computation.5 | async-start | bytes 8388608
  977.9 14.5 copy-start.123
  1007.6 15.5 copy-start.130
  1036.8 34.3 %copy-start.3 = (bf16[96,8,4,256]{3,1,2,0:T(8,128)(2,1)S(1)}, bf16[96,8,4,256]{3,1,2,0:T(8,128)(2,1)}, u32[]{:S(2)}) copy-start(bf16[96,8,4,256]{3,1,2,0:T(8,128)(2,1)} %copy-done.2) | copy-start | bytes 4718596
  1036.8 34.3 %copy-start.52 = (bf16[192,1024]{1,0:T(8,128)(2,1)S(1)}, bf16[192,1024]{1,0:T(8,128)(2,1)}, u32[]{:S(2)}) copy-start(bf16[192,1024]{1,0:T(8,128)(2,1)} %copy-done.51) | copy-start | bytes 1179652
  1151.3 16.2 slice-start.10
  1301.4 26.6 %copy-start.8 = (f32[768,768]{0,1:T(8,128)S(1)}, f32[768,768]{0,1:T(8,128)}, u32[]{:S(2)}) copy-start(f32[768,768]{0,1:T(8,128)} %copy-done.7) | copy-start | bytes 7077892
  1301.4 26.6 %copy-start.66 = (f32[768,96]{0,1:T(8,128)S(1)}, f32[768,96]{0,1:T(8,128)}, u32[]{:S(2)}) copy-start(f32[768,96]{0,1:T(8,128)} %copy-done.65) | copy-start | bytes 884740
  1301.4 26.6 %copy-start.96 = (f32[768,96]{0,1:T(8,128)S(1)}, f32[768,96]{0,1:T(8,128)}, u32[]{:S(2)}) copy-start(f32[768,96]{0,1:T(8,128)} %multiply_divide_fusion) | copy-start | bytes 884740
  1375.2 145.5 %copy-start.18 = (bf16[8,4,2,128,192]{3,0,4,1,2:T(8,128)(2,1)S(1)}, bf16[8,4,2,128,192]{3,0,4,1,2:T(8,128)(2,1)}, u32[]{:S(2)}) copy-start(bf16[8,4,2,128,192]{3,0,4,1,2:T(8,128)(2,1)} %maximum_bitcast_fusion.3) | copy-start | bytes 9437188
  1787.0 42.8 %copy-start.37 = (f32[2048,256]{1,0:T(8,128)S(1)}, f32[2048,256]{1,0:T(8,128)}, u32[]{:S(2)}) copy-start(f32[2048,256]{1,0:T(8,128)} %copy-done.36) | copy-start | bytes 6291460
  (192 other events, 782.2 us)

commit v2 on v1

v2 whole, which is shorter than its diff:
```python
import functools
import math

import jax
import jax.numpy as jnp
from jax import lax
from jax.experimental import pallas as pl
from jax.experimental.pallas import tpu as pltpu
from jax.sharding import PartitionSpec as P

SIMNORM = 8
HIGHEST = lax.Precision.HIGHEST
CHUNK_ROWS = 112
NORM_ROWS = 32
SOFT_ROWS = 64
LOSS_ROWS = 64
GAIN_AT = 40
SHIFT_AT = 64
BIAS_AT = 88
TABLE_AT = 96
WIDE_AT = 112
WEIGHT_AT = 12
REWARD_AT = 13
VALUE_AT = 14
ID_AT = 15


MESH_ID = pl.DeviceIdType.MESH


def major_minor(size):
    minor = 1
    while (minor * 2) * (minor * 2) <= size:
        minor *= 2
    return size // minor, minor


class Place:
    def __init__(self, depth, side):
        self.depth, self.side = depth, side
        batch, lat = lax.axis_index("batch"), lax.axis_index("lat")
        self.z, x = batch // side, lax.rem(batch, side)
        y, self.c = lat // 2, lax.rem(lat, 2)
        self.i = jnp.where(self.c == 0, y, x)
        self.j = jnp.where(self.c == 0, x, y)

    def device(self, c=None, i=None, j=None, z=None):
        c, i = self.c if c is None else c, self.i if i is None else i
        j, z = self.j if j is None else j, self.z if z is None else z
        x, y = jnp.where(c == 0, j, i), jnp.where(c == 0, i, j)
        return (z * self.side + x, y * 2 + c)

    def sibling(self):
        x, y = jnp.where(self.c == 0, self.j, self.i), jnp.where(self.c == 0, self.i, self.j)
        return (self.z * self.side + x, y * 2 + 1 - self.c)

    def dims(self):
        return (
            ("i", self.i, self.side, lambda p: self.device(i=p)),
            ("j", self.j, self.side, lambda p: self.device(j=p)),
            ("z", self.z, self.depth, lambda p: self.device(z=p)),
        )

    def barrier(self):
        sem = pltpu.get_barrier_semaphore()
        pl.semaphore_signal(sem, inc=1, device_id=self.sibling(), device_id_type=MESH_ID)
        count = 1
        for _, pos, size, at in self.dims():
            if size == 2:
                pl.semaphore_signal(sem, inc=1, device_id=at(1 - pos), device_id_type=MESH_ID)
                count = count + 1
            else:
                for step in (-1, 1):

                    @pl.when((pos + step >= 0) & (pos + step < size))
                    def _(at=at, pos=pos, step=step):
                        pl.semaphore_signal(sem, inc=1, device_id=at(pos + step), device_id_type=MESH_ID)

                count = count + jnp.where(pos > 0, 1, 0) + jnp.where(pos < size - 1, 1, 0)
        pl.semaphore_wait(sem, count)


def gather_steps(depth, side):
    return (
        [("z", s) for s in range(depth - 1)]
        + [("j", s) for s in range(side - 1)]
        + [("i", s) for s in range(side - 1)]
        + [("c", 0)]
    )


def gather_kernel(depth, side, chunks, chunk_rows, mine_ref, all_ref, own_sem, send_sems, recv_sems):
    place = Place(depth, side)
    steps = gather_steps(depth, side)
    dims = {name: (pos, size, at) for name, pos, size, at in place.dims()}
    own = pltpu.make_async_copy(mine_ref, all_ref.at[place.c, place.i, place.j, place.z], own_sem)
    own.start()
    place.barrier()

    def block(name, owner, rows):
        if name == "z":
            return all_ref.at[place.c, place.i, place.j, owner, rows]
        if name == "j":
            return all_ref.at[place.c, place.i, owner, :, rows]
        return all_ref.at[place.c, owner, :, :, rows]

    def copy(which, t, way, source, target, device):
        return pltpu.make_async_remote_copy(
            src_ref=source,
            dst_ref=target,
            send_sem=send_sems.at[which, way, t],
            recv_sem=recv_sems.at[which, way, t],
            device_id=device,
            device_id_type=MESH_ID,
        )

    def each(which, t, act, sending):
        name, s = steps[which]
        rows = pl.ds(pl.multiple_of(t * chunk_rows, 16), chunk_rows)
        if name == "c":
            core = place.c if sending else 1 - place.c
            ref = all_ref.at[core, :, :, :, rows]
            act(copy(which, t, 0, ref, ref, place.sibling()))
            return
        pos, size, at = dims[name]
        if size == 2:
            ref = block(name, pos if sending else 1 - pos, rows)
            source = mine_ref.at[rows] if sending and name == "z" and s == 0 else ref
            act(copy(which, t, 0, source, ref, at(1 - pos)))
            return
        if sending:
            ways = (
                (0, (pos >= s) & (pos + 1 < size), pos - s, pos + 1),
                (1, (pos + s < size) & (pos >= 1), pos + s, pos - 1),
            )
        else:
            ways = (
                (0, pos - 1 >= s, pos - 1 - s, pos - 1),
                (1, pos + 1 + s < size, pos + 1 + s, pos + 1),
            )
        for way, valid, owner, target in ways:

            @pl.when(valid)
            def _(way=way, owner=owner, target=target):
                ref = block(name, owner, rows)
                source = mine_ref.at[rows] if sending and name == "z" and s == 0 else ref
                act(copy(which, t, way, source, ref, at(target)))

    def body(t, carry):
        for which in range(len(steps) + 1):
            at = t - which

            @pl.when((at >= 0) & (at < chunks))
            def _(which=which, at=at):
                if which > 0:
                    each(which - 1, at, lambda c: c.wait_recv(), False)
                if which < len(steps):
                    if which == depth - 1:

                        @pl.when(at == 0)
                        def _():
                            own.wait()

                    each(which, at, lambda c: c.start(), True)

        return carry

    lax.fori_loop(0, chunks + len(steps), body, 0)

    def drain(t, carry):
        for which in range(len(steps)):
            each(which, t, lambda c: c.wait_send(), True)
        return carry

    lax.fori_loop(0, chunks, drain, 0)


def gather_all(mine, depth, side, chunks):
    rows, cols = mine.shape
    steps = len(gather_steps(depth, side))
    return pl.pallas_call(
        functools.partial(gather_kernel, depth, side, chunks, rows // chunks),
        out_shape=jax.ShapeDtypeStruct((2, side, side, depth, rows, cols), mine.dtype),
        in_specs=[pl.BlockSpec(memory_space=pl.ANY)],
        out_specs=pl.BlockSpec(memory_space=pl.ANY),
        scratch_shapes=[
            pltpu.SemaphoreType.DMA,
            pltpu.SemaphoreType.DMA((steps, 2, chunks)),
            pltpu.SemaphoreType.DMA((steps, 2, chunks)),
        ],
        compiler_params=pltpu.CompilerParams(collective_id=1, has_side_effects=True),
        name="gather_weights",
    )(mine)


def scatter_steps(depth, side):
    return (
        [("c", 0)]
        + [("i", s) for s in range(side - 1)]
        + [("j", s) for s in range(side - 1)]
        + [("z", s) for s in range(depth - 1)]
    )


def scatter_kernel(depth, side, chunks, chunk_rows, parts_ref, sum_ref, *scratch):
    held, own_buf, own_sems, send_sems, recv_sems = scratch[:5]
    landing = dict(zip(("i", "j", "z"), (scratch[5:7], scratch[7:9], scratch[9:11])))
    place = Place(depth, side)
    steps = scatter_steps(depth, side)
    dims = {name: (pos, size, at) for name, pos, size, at in place.dims()}
    place.barrier()

    def block(name, owner, rows):
        if name == "z":
            return held.at[place.i, place.j, owner, rows]
        if name == "j":
            return held.at[place.i, owner, :, rows]
        return held.at[owner, :, :, rows]

    def land(name, owner, rows):
        if owner is None:
            ref = landing[name][1]
        else:
            ref = landing[name][0].at[owner]
        if name == "z":
            return ref.at[rows]
        if name == "j":
            return ref.at[:, rows]
        return ref.at[:, :, rows]

    def add(into, other):
        lead = into.shape[:-2]
        if not lead:
            into[...] += other[...]
            return

        def one(n, carry):
            index = []
            for extent in reversed(lead):
                index.insert(0, lax.rem(n, extent))
                n = n // extent
            into[tuple(index)] += other[tuple(index)]
            return carry

        lax.fori_loop(0, math.prod(lead), one, 0)

    def own_copy(t):
        rows = pl.ds(pl.multiple_of(t * chunk_rows, 16), chunk_rows)
        slot = lax.rem(t, 2)
        return pltpu.make_async_copy(
            parts_ref.at[place.c, :, :, :, rows], own_buf.at[slot], own_sems.at[slot]
        )

    def copy(which, t, way, source, target, device):
        return pltpu.make_async_remote_copy(
            src_ref=source,
            dst_ref=target,
            send_sem=send_sems.at[which, way, t],
            recv_sem=recv_sems.at[which, way, t],
            device_id=device,
            device_id_type=MESH_ID,
        )

    def send(which, t, act):
        name, s = steps[which]
        rows = pl.ds(pl.multiple_of(t * chunk_rows, 16), chunk_rows)
        if name == "c":
            act(
                copy(
                    which, t, 0, parts_ref.at[1 - place.c, :, :, :, rows],
                    held.at[:, :, :, rows], place.sibling(),
                )
            )
            return
        pos, size, at = dims[name]
        if size == 2:
            act(copy(which, t, 0, block(name, 1 - pos, rows), land(name, None, rows), at(1 - pos)))
            return
        back = size - 1 - pos
        last = s == size - 2

        @pl.when((pos <= s) & (pos < size - 1))
        def _():
            owner = size - 1 - (s - pos)
            act(copy(which, t, 0, block(name, owner, rows), land(name, owner, rows), at(pos + 1)))

        @pl.when((back <= s) & (pos > 0))
        def _():
            owner = s - back
            act(
                copy(
                    which, t, 1, block(name, owner, rows),
                    land(name, None if last else owner, rows), at(pos - 1),
                )
            )

    def receive(which, t):
        name, s = steps[which]
        rows = pl.ds(pl.multiple_of(t * chunk_rows, 16), chunk_rows)
        if name == "c":
            copy(
                which, t, 0, held.at[:, :, :, rows], held.at[:, :, :, rows], place.sibling()
            ).wait_recv()
            own_copy(t).wait()
            add(held.at[:, :, :, rows], own_buf.at[lax.rem(t, 2)])
            return
        pos, size, at = dims[name]
        if size == 2:
            ref = land(name, None, rows)
            copy(which, t, 0, ref, ref, at(1 - pos)).wait_recv()
            add(block(name, pos, rows), ref)
            return
        last = s == size - 2

        @pl.when((pos - 1 <= s) & (pos >= 1))
        def _():
            owner = size - 1 - (s - (pos - 1))
            ref = land(name, owner, rows)
            copy(which, t, 0, ref, ref, at(pos - 1)).wait_recv()
            add(block(name, owner, rows), ref)

        @pl.when((size - 2 - pos <= s) & (pos < size - 1))
        def _():
            owner = s - (size - 2 - pos)
            ref = land(name, None if last else owner, rows)
            copy(which, t, 1, ref, ref, at(pos + 1)).wait_recv()
            add(block(name, owner, rows), ref)

    def body(t, carry):
        @pl.when(t < chunks)
        def _():
            own_copy(t).start()

        for which in range(len(steps) + 1):
            at = t - which

            @pl.when((at >= 0) & (at < chunks))
            def _(which=which, at=at):
                if which > 0:
                    receive(which - 1, at)
                if which < len(steps):
                    send(which, at, lambda c: c.start())
                else:
                    rows = pl.ds(pl.multiple_of(at * chunk_rows, 16), chunk_rows)
                    sum_ref[rows, :] = held[place.i, place.j, place.z, rows, :].astype(sum_ref.dtype)

        return carry

    lax.fori_loop(0, chunks + len(steps), body, 0)

    def drain(t, carry):
        for which in range(len(steps)):
            send(which, t, lambda c: c.wait_send())
        return carry

    lax.fori_loop(0, chunks, drain, 0)


def scatter_sum(parts, depth, side, chunks):
    rows, cols = parts.shape[-2:]
    chunk_rows = rows // chunks
    steps = len(scatter_steps(depth, side))
    dtype = parts.dtype

    def landing(size, *lead):
        first = (size,) + lead if size > 2 else (1,)
        tail = (rows, cols) if size > 2 else (16, 128)
        return [pltpu.VMEM(first + tail, dtype), pltpu.VMEM(lead + (rows, cols), dtype)]

    return pl.pallas_call(
        functools.partial(scatter_kernel, depth, side, chunks, chunk_rows),
        out_shape=jax.ShapeDtypeStruct((rows, cols), jnp.float32),
        in_specs=[pl.BlockSpec(memory_space=pl.ANY)],
        out_specs=pl.BlockSpec(memory_space=pltpu.VMEM),
        scratch_shapes=[
            pltpu.VMEM((side, side, depth, rows, cols), dtype),
            pltpu.VMEM((2, side, side, depth, chunk_rows, cols), dtype),
            pltpu.SemaphoreType.DMA((2,)),
            pltpu.SemaphoreType.DMA((steps, 2, chunks)),
            pltpu.SemaphoreType.DMA((steps, 2, chunks)),
        ]
        + landing(side, side, depth)
        + landing(side, depth)
        + landing(depth),
        compiler_params=pltpu.CompilerParams(
            collective_id=2, has_side_effects=True, vmem_limit_bytes=60 * 2**20
        ),
        name="scatter_gradients",
    )(parts)


def dot(a, b):
    return jnp.dot(a, b, preferred_element_type=jnp.float32)


def dot_t(a, b):
    return lax.dot_general(a, b, (((1,), (1,)), ((), ())), preferred_element_type=jnp.float32)


def t_dot(a, b):
    return lax.dot_general(a, b, (((0,), (0,)), ((), ())), preferred_element_type=jnp.float32)


def group_all(values, op):
    lanes = values.shape[-1]
    lane = lax.broadcasted_iota(jnp.int32, values.shape, 1)
    step = 1
    while step < SIMNORM:
        up = pltpu.roll(values, lanes - step, 1)
        down = pltpu.roll(values, step, 1)
        values = op(values, jnp.where((lane & step) == 0, up, down))
        step *= 2
    return values


def loop(count, body):
    def one(n, carry):
        body(n)
        return carry

    lax.fori_loop(0, count, one, 0)


def rows_of(n, size, base=0):
    return pl.ds(pl.multiple_of(base + n * size, 16 if size % 16 == 0 else 8), size)


def norm_forward(pre, rows, base, gain, shift, hat, slope, hidden, inv):
    width = pre.shape[-1]

    def body(n):
        values = pre[rows_of(n, NORM_ROWS), :]
        at = rows_of(n, NORM_ROWS, base)
        mean = jnp.sum(values, -1, keepdims=True) * (1.0 / width)
        centered = values - mean
        variance = jnp.sum(centered * centered, -1, keepdims=True) * (1.0 / width)
        scale = lax.rsqrt(variance + 1e-05)
        normal = centered * scale
        act = normal * gain + shift
        grown = jnp.exp(jnp.minimum(act, 20.0))
        top = grown * (grown + 2.0)
        under = pl.reciprocal(top + 2.0, approx=True)
        part = top * under
        hidden[at, :] = (act * part).astype(hidden.dtype)
        slope[at, :] = (part + 4.0 * act * (grown * (grown + 1.0)) * (under * under)).astype(slope.dtype)
        hat[at, :] = normal.astype(hat.dtype)
        inv[at, :] = jnp.broadcast_to(scale, (NORM_ROWS, inv.shape[-1]))

    loop(rows // NORM_ROWS, body)


def norm_backward(grad, rows, base, gain, hat, slope, inv, low, sums):
    width = grad.shape[-1]

    def body(n):
        at = rows_of(n, NORM_ROWS, base)
        d_act = grad[rows_of(n, NORM_ROWS), :] * slope[at, :].astype(jnp.float32)
        normal = hat[at, :].astype(jnp.float32)
        by_gain = d_act * normal
        sums[0] += jnp.sum(by_gain.reshape(NORM_ROWS // 8, 8, width), 0)
        sums[1] += jnp.sum(d_act.reshape(NORM_ROWS // 8, 8, width), 0)
        d_normal = d_act * gain
        first = jnp.sum(d_normal, -1, keepdims=True) * (1.0 / width)
        second = jnp.sum(by_gain * gain, -1, keepdims=True) * (1.0 / width)
        low[at, :] = ((d_normal - first - normal * second) * inv[at, :1]).astype(low.dtype)

    loop(rows // NORM_ROWS, body)


def train_kernel(
    at, depth, side, horizon, bins, lin, obs_ref, extra_ref, info_ref, table_ref, bias_ref, all_ref,
    parts_ref, d_obs_ref, *scratch,
):
    (small, small32, lat_bias, xa, xat, w1d, w2d, lo, stage, enc_hat, enc_slope, enc_hid, enc_inv,
     d1_hat, d1_slope, d1_hid, d1_inv, d2_hat, d2_slope, d2_hid, d2_inv, encoded, predicted,
     w1, w2, vo, hat1, slope1, hid1, inv1, hat2, slope2, hid2, inv2, d_logits, pre,
     dx, g1, g2, gv, d_lin, sums, d_small, d_small_low, d_bias, load_sems, store_sems, first_sems, last_sems) = scratch
    f32, bf16 = jnp.float32, jnp.bfloat16
    rows = xa.shape[0]
    seqs = rows // horizon
    latent = encoded.shape[1]
    hidden = pre.shape[1]
    all_rows = seqs * (horizon + 1)
    unit = at.cols // 4
    head_rows = at.head_rows

    def for_blocks(body):
        def one(b, carry):
            z, x = lax.div(b, side), lax.rem(b, side)
            for l in range(at.lats):
                y, c = divmod(l, 2)
                body(b, l, (c,) + ((y, x) if c == 0 else (x, y)) + (z,))
            return carry

        lax.fori_loop(0, at.batches, one, 0)

    def move_head(k, first, second, third, sems, load):
        base = k * head_rows

        def body(b, l, where):
            cols = pl.ds(l * at.cols, at.cols)

            def one(which, start, count, here, *lanes):
                there = (all_ref if load else parts_ref).at[(*where, rows_of(0, count, base + start), *lanes)]
                pair = (there, here) if load else (here, there)
                pltpu.make_async_copy(*pair, sems.at[which]).start()

            one(0, 0, at.latent_rows, first.at[rows_of(b, at.latent_rows), cols])
            one(0, at.task_at, at.tail_rows, first.at[rows_of(b, at.tail_rows, latent), cols])
            one(1, at.middle_at, at.middle_rows, second.at[rows_of(b, at.middle_rows), cols])
            if third is not None:
                for n in range(at.pieces):
                    here = third.at[value_rows(b, l, n)]
                    one(2, at.value_at, at.value_rows, here, pl.ds(n * 128, 128))

        for_blocks(body)

    def value_rows(b, l, n):
        start = b * at.middle_rows + (l * at.share + n * at.value_rows)
        return pl.ds(pl.multiple_of(start, 16 if at.value_rows % 16 == 0 else 8), at.value_rows)

    def wait_head(first, second, third, sems):
        for which, ref in enumerate((first, second, third)):
            if ref is not None:
                pltpu.make_async_copy(ref, ref, sems.at[which]).wait()

    def move_small(ref, sem, load):
        def body(b, l, where):
            here = ref.at[rows_of(b, at.value_rows), pl.ds(l * at.cols, at.cols)]
            there = (all_ref if load else parts_ref).at[(*where, pl.ds(at.value_at, at.value_rows))]
            pltpu.make_async_copy(*((there, here) if load else (here, there)), sem).start()

        for_blocks(body)

    def move_out(n, sem, load):
        def body(b, l, where):
            here = stage.at[b * at.lats + l]
            there = (all_ref if load else parts_ref).at[
                (*where, pl.ds(at.heads * head_rows + n * at.out_rows, at.out_rows))
            ]
            pltpu.make_async_copy(*((there, here) if load else (here, there)), sem).start()

        for_blocks(body)

    def stage_to_out(n):
        def body(b):
            block_rows = rows_of(b, at.middle_rows)
            for l in range(at.lats):
                values = stage[b * at.lats + l].astype(f32)
                half, quarter = at.middle_rows // 2, at.middle_rows // 4
                left = jnp.concatenate([values[:half, : 2 * unit], values[:half, 2 * unit :]], 0)
                right = jnp.concatenate(
                    [values[half : half + quarter, m * unit : (m + 1) * unit] for m in range(4)], 0
                )
                both = jnp.concatenate([left, right], 1)
                pre[: at.middle_rows, l * 3 * unit : (l + 1) * 3 * unit] = both
            lo[n, block_rows, :] = pre[: at.middle_rows, :latent].astype(bf16)

        loop(at.batches, body)

    def out_to_stage(hid, total):
        many = max(1, 128 // at.middle_rows)

        def body(n):
            cols = pl.ds(pl.multiple_of(n * many * at.middle_rows, 128), many * at.middle_rows)
            grads = t_dot(hid[:total, cols], d_lin[:total, :])
            half, quarter = at.middle_rows // 2, at.middle_rows // 4
            for p in range(many):
                grad = grads[p * at.middle_rows : (p + 1) * at.middle_rows]
                for l in range(at.lats):
                    values = grad[:, l * 3 * unit : (l + 1) * 3 * unit]
                    left = jnp.concatenate([values[:half, : 2 * unit], values[half:, : 2 * unit]], 1)
                    right = jnp.concatenate(
                        [values[m * quarter : (m + 1) * quarter, 2 * unit :] for m in range(4)], 1
                    )
                    stage[(n * many + p) * at.lats + l] = jnp.concatenate([left, right], 0).astype(bf16)

        loop(at.batches // many, body)

    def gain_row(n):
        return small32[pl.ds(GAIN_AT + n, 1), :], small32[pl.ds(SHIFT_AT + n, 1), :]

    def keep_sums(n, which=0):
        d_small[pl.ds(GAIN_AT + n, 1), :] = jnp.sum(sums[which, 0], 0, keepdims=True)
        d_small[pl.ds(SHIFT_AT + n, 1), :] = jnp.sum(sums[which, 1], 0, keepdims=True)

    def clear_sums():
        sums[...] = jnp.zeros_like(sums)

    def simnorm_forward(count, base, out):
        def body(n):
            for m in range(latent // 128):
                values = pre[rows_of(n, SOFT_ROWS), m * 128 : (m + 1) * 128]
                grown = jnp.exp(values - group_all(values, jnp.maximum))
                out[rows_of(n, SOFT_ROWS, base), m * 128 : (m + 1) * 128] = grown / group_all(grown, jnp.add)

        loop(count // SOFT_ROWS, body)

    def simnorm_backward(count, base, out, grad_of, low_base):
        def body(n):
            for m in range(latent // 128):
                cols = slice(m * 128, (m + 1) * 128)
                values = out[rows_of(n, SOFT_ROWS, base), cols]
                grad = grad_of(n, cols)
                grad = values * (grad - group_all(grad * values, jnp.add))
                low = grad.astype(bf16)
                d_lin[rows_of(n, SOFT_ROWS, low_base), cols] = low
                sums[0, 0, :, cols] += jnp.sum(low.astype(f32).reshape(SOFT_ROWS // 8, 8, 128), 0)

        loop(count // SOFT_ROWS, body)

    def big_dot(out, count, a, b, how=dot):
        total = b.shape[-1] if how is dot else b.shape[0]
        tile = 256 if total % 256 == 0 else 128
        for n in range(total // tile):
            cols = slice(n * tile, (n + 1) * tile)
            part = b[:, cols] if how is dot else b[cols, :]
            out[:count, cols] = how(a, part)

    move_small(small, first_sems.at[0], True)
    move_out(0, first_sems.at[1], True)
    move_head(0, w1d, w2d, None, first_sems.at[pl.ds(2, 3)], True)
    move_head(1, w1.at[0], w2.at[0], vo.at[0], load_sems.at[0], True)
    d_small[...] = jnp.zeros_like(d_small)
    dx[...] = jnp.zeros_like(dx)
    ids = info_ref[:seqs, ID_AT : ID_AT + 1]
    lanes = lax.broadcasted_iota(jnp.int32, (seqs, 128), 1).astype(f32)
    task_hot = (lanes == ids).astype(f32)
    embedded = dot(task_hot.astype(bf16), table_ref[...])
    for t in range(horizon):
        part = slice(t * seqs, (t + 1) * seqs)
        xa[part, latent:] = (embedded + extra_ref[part, :].astype(f32)).astype(bf16)
    pltpu.make_async_copy(small, small, first_sems.at[0]).wait()
    small32[...] = small[...].astype(f32)
    for l in range(at.lats):
        lat_bias[0:2, l * 3 * unit : (l + 1) * 3 * unit] = small32[
            BIAS_AT : BIAS_AT + 2, l * at.cols : l * at.cols + 3 * unit
        ]
    pltpu.make_async_copy(stage, stage, first_sems.at[1]).wait()
    stage_to_out(0)
    move_out(1, first_sems.at[1], True)

    big_dot(pre, all_rows, obs_ref[...], small)
    gain, shift = gain_row(0)
    norm_forward(pre, all_rows, 0, gain, shift, enc_hat, enc_slope, enc_hid, enc_inv)
    big_dot(pre, all_rows, enc_hid[...], lo.at[0])
    pre[:all_rows, :latent] += lat_bias[0:1, :]
    simnorm_forward(all_rows, 0, encoded)
    xa[:seqs, :latent] = encoded[:seqs, :].astype(bf16)
    pltpu.make_async_copy(stage, stage, first_sems.at[1]).wait()
    stage_to_out(1)
    wait_head(w1d, w2d, None, first_sems.at[pl.ds(2, 3)])

    gain1, shift1 = gain_row(1)
    gain2, shift2 = gain_row(2)
    for t in range(horizon):
        part = slice(t * seqs, (t + 1) * seqs)
        big_dot(pre, seqs, xa[part, :], w1d)
        norm_forward(pre, seqs, t * seqs, gain1, shift1, d1_hat, d1_slope, d1_hid, d1_inv)
        big_dot(pre, seqs, d1_hid[part, :], w2d)
        norm_forward(pre, seqs, t * seqs, gain2, shift2, d2_hat, d2_slope, d2_hid, d2_inv)
        big_dot(pre, seqs, d2_hid[part, :], lo.at[1])
        pre[:seqs, :latent] += lat_bias[1:2, :]
        simnorm_forward(seqs, t * seqs, predicted)
        if t + 1 < horizon:
            xa[(t + 1) * seqs : (t + 2) * seqs, :latent] = predicted[part, :].astype(bf16)
    for n in range(xa.shape[1] // 128):
        xat[n * 128 : (n + 1) * 128, :] = xa[:, n * 128 : (n + 1) * 128].T

    heads = at.heads
    lane = lax.broadcasted_iota(jnp.int32, (LOSS_ROWS, 128), 1)
    acts = lin // 2

    def head(k):
        slot = lax.rem(k - 1, 2)
        wait_head(w1.at[slot], w2.at[slot], vo.at[slot], load_sems.at[slot])

        @pl.when(k + 1 < heads)
        def _():
            move_head(k + 1, w1.at[1 - slot], w2.at[1 - slot], vo.at[1 - slot], load_sems.at[1 - slot], True)

        gain1, shift1 = gain_row(2 * k + 1)
        gain2, shift2 = gain_row(2 * k + 2)
        big_dot(pre, rows, xa[...], w1.at[slot])
        norm_forward(pre, rows, 0, gain1, shift1, hat1, slope1, hid1, inv1)
        big_dot(pre, rows, hid1[...], w2.at[slot])
        norm_forward(pre, rows, 0, gain2, shift2, hat2, slope2, hid2, inv2)
        pre[:rows, :128] = dot(hid2[...], vo[slot]) + bias_ref[pl.ds(k, 1), :]
        clear_sums()

        def loss(n):
            part = rows_of(n, LOSS_ROWS)
            logits = pre[part, :128]
            weight = info_ref[part, WEIGHT_AT : WEIGHT_AT + 1] * 0.1

            @pl.when(k < heads - 1)
            def _():
                chosen = jnp.where(
                    k == 1, info_ref[part, REWARD_AT : REWARD_AT + 1], info_ref[part, VALUE_AT : VALUE_AT + 1]
                )
                share = weight * jnp.where(k == 1, 1.0, 1.0 / (heads - 3))
                kept = jnp.where(lane < bins, logits, -1e30)
                grown = jnp.exp(kept - jnp.max(kept, -1, keepdims=True))
                soft = grown / jnp.sum(grown, -1, keepdims=True)
                hot = (lane.astype(f32) == chosen).astype(f32)
                d_logits[part, :] = (share * (soft - hot)).astype(bf16)

            @pl.when(k == heads - 1)
            def _():
                bent = jnp.tanh(logits)
                first = lane < acts
                mean = jnp.where(first, bent, pltpu.roll(bent, acts, 1))
                wide = jnp.where(first, pltpu.roll(bent, 128 - acts, 1), bent)
                off = info_ref[part, :] - mean
                narrow_by = jnp.exp(-2.0 * wide)
                scaled = off * narrow_by
                d_mean = -scaled * narrow_by * (1.0 - mean * mean)
                d_wide = (1.0 - scaled * scaled) * 2.0 * (1.0 - wide * wide)
                grad = weight * jnp.where(first, d_mean, d_wide)
                d_logits[part, :] = jnp.where(lane < lin, grad, 0.0).astype(bf16)

            sums[0, 0, :, :128] += jnp.sum(
                d_logits[part, :].astype(f32).reshape(LOSS_ROWS // 8, 8, 128), 0
            )

        loop(rows // LOSS_ROWS, loss)
        d_bias[pl.ds(k - 1, 1), :] = jnp.sum(sums[0, 0, :, :128], 0, keepdims=True)
        big_dot(pre, rows, d_logits[...], vo.at[slot], dot_t)
        clear_sums()
        norm_backward(pre, rows, 0, gain2, hat2, slope2, inv2, hat2, sums.at[0])
        keep_sums(2 * k + 2)
        big_dot(pre, rows, hat2[...], w2.at[slot], dot_t)
        clear_sums()
        norm_backward(pre, rows, 0, gain1, hat1, slope1, inv1, hat1, sums.at[0])
        keep_sums(2 * k + 1)
        for n in range(dx.shape[1] // 128):
            dx[:, n * 128 : (n + 1) * 128] += dot_t(hat1[...], w1[slot, n * 128 : (n + 1) * 128, :])

        @pl.when(k > 1)
        def _():
            wait_head(g1, g2, gv, store_sems)

        gv[...] = t_dot(hid2[...], d_logits[...]).astype(bf16)
        weight_grads(hid1, hat2, hat1)
        move_head(k, g1, g2, gv, store_sems, False)

    def weight_grads(hid_first, low_second, low_first):
        for n in range(hidden // 256):
            part = slice(n * 256, (n + 1) * 256)
            for m in range(hidden // 256):
                cols = slice(m * 256, (m + 1) * 256)
                g2[part, cols] = t_dot(hid_first[:, part], low_second[:, cols]).astype(bf16)
        for n in range(xat.shape[0] // 128):
            part = slice(n * 128, (n + 1) * 128)
            for m in range(hidden // 256):
                cols = slice(m * 256, (m + 1) * 256)
                g1[part, cols] = dot(xat[part, :], low_first[:, cols]).astype(bf16)

    def heads_body(k, carry):
        head(k)
        return carry

    lax.fori_loop(1, heads, heads_body, 0)

    scale = 2.0 * 20.0 / latent

    def pull(t, n, cols):
        weight = info_ref[rows_of(n, SOFT_ROWS, t * seqs), WEIGHT_AT : WEIGHT_AT + 1] * scale
        gap = predicted[rows_of(n, SOFT_ROWS, t * seqs), cols] - encoded[rows_of(n, SOFT_ROWS, (t + 1) * seqs), cols]
        return weight * gap

    def keep_bias(n):
        total = jnp.sum(sums[0, 0], 0, keepdims=True)
        for l in range(at.lats):
            d_small[BIAS_AT + n : BIAS_AT + n + 1, l * at.cols : l * at.cols + 3 * unit] = total[
                :, l * 3 * unit : (l + 1) * 3 * unit
            ]

    clear_sums()
    for t in reversed(range(horizon)):
        part = slice(t * seqs, (t + 1) * seqs)

        def grad_of(n, cols, t=t):
            grad = pull(t, n, cols)
            if t + 1 < horizon:
                grad = grad + dx[rows_of(n, SOFT_ROWS, (t + 1) * seqs), cols]
            return grad

        simnorm_backward(seqs, t * seqs, predicted, grad_of, t * seqs)
        big_dot(pre, seqs, d_lin[part, :], lo.at[1], dot_t)
        norm_backward(pre, seqs, t * seqs, gain2, d2_hat, d2_slope, d2_inv, d2_hat, sums.at[2])
        big_dot(pre, seqs, d2_hat[part, :], w2d, dot_t)
        norm_backward(pre, seqs, t * seqs, gain1, d1_hat, d1_slope, d1_inv, d1_hat, sums.at[1])
        for n in range(dx.shape[1] // 128):
            cols = slice(n * 128, (n + 1) * 128)
            dx[part, cols] += dot_t(d1_hat[part, :], w1d[cols, :])
    keep_bias(1)
    keep_sums(1, 1)
    keep_sums(2, 2)
    out_to_stage(d2_hid, rows)
    move_out(1, last_sems.at[0], False)
    wait_head(g1, g2, gv, store_sems)
    weight_grads(d1_hid, d2_hat, d1_hat)
    move_head(0, g1, g2, None, store_sems, False)

    clear_sums()
    simnorm_backward(seqs, 0, encoded, lambda n, cols: dx[rows_of(n, SOFT_ROWS), cols], 0)
    for t in range(horizon):
        simnorm_backward(
            seqs, (t + 1) * seqs, encoded, lambda n, cols, t=t: -pull(t, n, cols), (t + 1) * seqs
        )
    keep_bias(0)
    clear_sums()
    big_dot(pre, all_rows, d_lin[...], lo.at[0], dot_t)
    norm_backward(pre, all_rows, 0, gain_row(0)[0], enc_hat, enc_slope, enc_inv, enc_hat, sums.at[0])
    keep_sums(0)
    d_obs_ref[...] = dot_t(enc_hat[...], small[...])
    for n in range(hidden // 256):
        cols = slice(n * 256, (n + 1) * 256)
        d_small[:GAIN_AT, cols] = t_dot(obs_ref[...], enc_hat[:, cols])[:GAIN_AT]
    d_embedded = dx[:seqs, latent:]
    for t in range(1, horizon):
        d_embedded = d_embedded + dx[t * seqs : (t + 1) * seqs, latent:]
    d_table = lax.dot_general(
        d_embedded, task_hot, (((0,), (0,)), ((), ())), precision=HIGHEST, preferred_element_type=f32
    )
    for l in range(at.lats):
        for n in range(at.pieces):
            cols = slice(l * at.cols + n * 128, l * at.cols + (n + 1) * 128)
            first = (l * at.pieces + n) * 16
            d_small[TABLE_AT : TABLE_AT + 16, cols] = d_table[first : first + 16, :]
            d_small[WIDE_AT : WIDE_AT + at.wide_rows, cols] = d_bias[
                n * at.wide_rows : (n + 1) * at.wide_rows, :
            ]
    d_small_low[...] = d_small[...].astype(bf16)
    move_small(d_small_low, last_sems.at[1], False)
    pltpu.make_async_copy(stage, stage, last_sems.at[0]).wait()
    out_to_stage(enc_hid, all_rows)
    move_out(0, last_sems.at[0], False)
    wait_head(g1, g2, None, store_sems)
    pltpu.make_async_copy(d_small_low, d_small_low, last_sems.at[1]).wait()
    pltpu.make_async_copy(stage, stage, last_sems.at[0]).wait()


def train(at, depth, side, dims, obs, extra, info, table, bias, gathered):
    rows, all_rows = extra.shape[0], obs.shape[0]
    latent = at.latent_rows * at.batches
    hidden = at.middle_rows * at.batches
    wide = latent + at.tail_rows * at.batches
    f32, bf16 = jnp.float32, jnp.bfloat16

    def saved(count):
        return [
            pltpu.VMEM((count, hidden), bf16),
            pltpu.VMEM((count, hidden), bf16),
            pltpu.VMEM((count, hidden), bf16),
            pltpu.VMEM((count, 128), f32),
        ]

    vmem = pl.BlockSpec(memory_space=pltpu.VMEM)
    hbm = pl.BlockSpec(memory_space=pl.ANY)
    return pl.pallas_call(
        functools.partial(train_kernel, at, depth, side, dims["horizon"], dims["bins"], dims["lin"]),
        out_shape=[
            jax.ShapeDtypeStruct(gathered.shape, bf16),
            jax.ShapeDtypeStruct((all_rows, 128), f32),
        ],
        in_specs=[vmem, vmem, vmem, vmem, vmem, hbm],
        out_specs=[hbm, vmem],
        scratch_shapes=[
            pltpu.VMEM((128, hidden), bf16),
            pltpu.VMEM((128, hidden), f32),
            pltpu.VMEM((8, latent), f32),
            pltpu.VMEM((rows, wide), bf16),
            pltpu.VMEM((wide, rows), bf16),
            pltpu.VMEM((wide, hidden), bf16),
            pltpu.VMEM((hidden, hidden), bf16),
            pltpu.VMEM((2, hidden, latent), bf16),
            pltpu.VMEM((at.batches * at.lats, at.out_rows, at.cols), bf16),
        ]
        + saved(all_rows)
        + saved(rows)
        + saved(rows)
        + [
            pltpu.VMEM((all_rows, latent), f32),
            pltpu.VMEM((rows, latent), f32),
            pltpu.VMEM((2, wide, hidden), bf16),
            pltpu.VMEM((2, hidden, hidden), bf16),
            pltpu.VMEM((2, hidden, 128), bf16),
        ]
        + saved(rows)
        + saved(rows)
        + [
            pltpu.VMEM((rows, 128), bf16),
            pltpu.VMEM((all_rows, hidden), f32),
            pltpu.VMEM((rows, wide), f32),
            pltpu.VMEM((wide, hidden), bf16),
            pltpu.VMEM((hidden, hidden), bf16),
            pltpu.VMEM((hidden, 128), bf16),
            pltpu.VMEM((all_rows, latent), bf16),
            pltpu.VMEM((3, 2, 8, hidden), f32),
            pltpu.VMEM((128, hidden), f32),
            pltpu.VMEM((128, hidden), bf16),
            pltpu.VMEM((8, 128), f32),
            pltpu.SemaphoreType.DMA((2, 3)),
            pltpu.SemaphoreType.DMA((3,)),
            pltpu.SemaphoreType.DMA((5,)),
            pltpu.SemaphoreType.DMA((2,)),
        ],
        compiler_params=pltpu.CompilerParams(vmem_limit_bytes=62 * 2**20),
        name="train",
    )(obs, extra, info, table, bias, gathered)


def round_up(n, to):
    return -(-n // to) * to


class Rows:
    def __init__(self, members, batches, lats):
        (encoder_in, latent_out, head_latent, head_action, head_task, head_middle, value_out,
         policy_out, task_table, norm_gain, norm_shift, latent_bias, value_bias, policy_bias) = members
        self.batches, self.lats = batches, lats
        (self.heads, self.latent_rows, self.cols) = head_latent.shape
        self.middle_rows = head_middle.shape[1]
        self.task_rows = head_task.shape[1]
        self.pieces = self.cols // 128
        self.share = self.middle_rows // lats
        self.value_rows = self.share // self.pieces
        self.out_rows = self.middle_rows * latent_out.shape[2] // self.cols
        self.middle_at = self.latent_rows
        self.value_at = self.middle_at + self.middle_rows
        self.task_at = self.value_at + self.value_rows
        self.tail_rows = round_up(self.task_rows + 2, 4)
        self.head_rows = self.task_at + self.tail_rows
        self.table_shape = task_table.shape
        self.obs = encoder_in.shape[0]
        self.norms = norm_gain.shape[0]
        self.acts = head_action.shape[1]
        self.latent_cols = latent_out.shape[2]
        self.wide_rows = 8 // self.pieces
        self.total = self.heads * self.head_rows + 2 * self.out_rows


def fill(values, shape, before=None):
    before = before or (0,) * len(shape)
    return jnp.pad(
        values, [(skip, want - have - skip) for skip, have, want in zip(before, values.shape, shape)]
    )


def narrow(at, values):
    pieces = [
        values[..., n * at.value_rows : (n + 1) * at.value_rows, :] for n in range(at.pieces)
    ]
    return jnp.concatenate(pieces, -1)


def widen(at, values):
    pieces = [values[..., n * 128 : (n + 1) * 128] for n in range(at.pieces)]
    return jnp.concatenate(pieces, -2)


def out_pack(at, values):
    half, quarter, unit = at.middle_rows // 2, at.middle_rows // 4, at.cols // 4
    left = [values[..., n * half : (n + 1) * half, : 2 * unit] for n in range(2)]
    right = [values[..., n * quarter : (n + 1) * quarter, 2 * unit :] for n in range(4)]
    return jnp.concatenate([jnp.concatenate(left, -1), jnp.concatenate(right, -1)], -2)


def out_unpack(at, values):
    half, unit = at.middle_rows // 2, at.cols // 4
    left = [values[..., :half, n * 2 * unit : (n + 1) * 2 * unit] for n in range(2)]
    right = [values[..., half:, n * unit : (n + 1) * unit] for n in range(4)]
    return jnp.concatenate([jnp.concatenate(left, -2), jnp.concatenate(right, -2)], -1)


def pack_own(at, members):
    (encoder_in, latent_out, head_latent, head_action, head_task, head_middle, value_out,
     policy_out, task_table, norm_gain, norm_shift, latent_bias, value_bias, policy_bias) = members
    batch, lat = lax.axis_index("batch"), lax.axis_index("lat")
    small = jnp.concatenate(
        [
            fill(encoder_in, (GAIN_AT, at.cols)),
            fill(norm_gain, (SHIFT_AT - GAIN_AT, at.cols)),
            fill(norm_shift, (BIAS_AT - SHIFT_AT, at.cols)),
            fill(latent_bias, (128 - BIAS_AT, at.cols)),
        ],
        0,
    )
    small = lax.dynamic_slice_in_dim(small, batch * at.value_rows, at.value_rows, 0)
    out = jnp.concatenate(
        [fill(value_out, value_out.shape[:2] + (128,)), fill(policy_out, (policy_out.shape[0], 128))[None]], 0
    )
    out = narrow(at, lax.dynamic_slice_in_dim(out, lat * at.share, at.share, 1))
    out = jnp.concatenate([small[None], out], 0)
    action = fill(head_action, (at.heads, at.batches, at.cols))
    action = lax.dynamic_slice_in_dim(action, batch, 1, 1)
    table = fill(task_table.reshape(1, 1, -1), (at.heads, at.tail_rows - at.task_rows - 1, at.cols))
    heads = jnp.concatenate([head_latent, head_middle, out, head_task, action, table], 1)
    tail = out_pack(at, latent_out).reshape(2 * at.out_rows, at.cols)
    return jnp.concatenate([heads.reshape(at.heads * at.head_rows, at.cols), tail], 0)


def by_device(at, gathered):
    both = jnp.stack([gathered[0], jnp.swapaxes(gathered[1], 0, 1)], 0)
    return both.transpose(3, 2, 1, 0, 4, 5).reshape((at.batches, at.lats) + gathered.shape[-2:])


def whole_table(at, gathered):
    tr, tc = at.table_shape
    row = at.task_at + at.task_rows + 1
    table = by_device(at, gathered[:, :, :, :, row : row + 1, : tr * tc])
    table = table.reshape(at.batches, at.lats, tr, tc).transpose(0, 2, 1, 3)
    table = table.reshape(at.batches * tr, at.batches, at.task_rows)
    table = fill(table, (128, at.batches, at.tail_rows))
    return table.reshape(128, at.batches * at.tail_rows)


def unpack_own(at, total, dims):
    split = at.heads * at.head_rows
    heads = total[:split].reshape(at.heads, at.head_rows, at.cols)
    part = heads[:, at.value_at : at.value_at + at.value_rows].astype(jnp.bfloat16)
    action = heads[:, at.task_at + at.task_rows].astype(jnp.bfloat16)
    split_over_lat = lax.all_gather(jnp.concatenate([part[0], action], 0), "batch", axis=0)
    split_over_lat = split_over_lat.astype(jnp.float32)
    small = split_over_lat[:, : at.value_rows].reshape(-1, at.cols)
    action = split_over_lat[: at.acts, at.value_rows :].transpose(1, 0, 2)[: at.heads - 1]
    out = widen(at, lax.all_gather(part[1:], "lat", axis=0).astype(jnp.float32))
    out = out.transpose(1, 0, 2, 3).reshape(at.heads - 1, at.middle_rows, 128)
    tr, tc = at.table_shape
    table = small[TABLE_AT : TABLE_AT + 16].reshape(16, at.pieces, 128).transpose(1, 0, 2)
    table = table.reshape(tc // at.task_rows, at.tail_rows, 128)[:, : at.task_rows].reshape(tc, 128)
    table = lax.dynamic_slice_in_dim(table, lax.axis_index("batch") * tr, tr, 1).T
    wide = small[WIDE_AT : WIDE_AT + at.wide_rows].reshape(at.wide_rows, at.pieces, 128)
    wide = wide.transpose(1, 0, 2).reshape(8, 128)
    return (
        small[: at.obs],
        out_unpack(at, total[split:].reshape(2, at.out_rows, at.cols)),
        heads[:, : at.latent_rows],
        action,
        heads[:, at.task_at : at.task_at + at.task_rows],
        heads[:, at.middle_at : at.value_at],
        out[:-1, :, : dims["bins"]],
        out[-1, :, : dims["lin"]],
        table,
        small[GAIN_AT : GAIN_AT + at.norms],
        small[SHIFT_AT : SHIFT_AT + at.norms],
        small[BIAS_AT : BIAS_AT + 2, : at.latent_cols],
        wide[: at.heads - 2, : dims["bins"]],
        wide[at.heads - 2, : dims["lin"]],
    )


def local(
    observations, actions, task_ids, counts, reward_bins, value_bins, encoder_in, latent_out,
    head_latent, head_action, head_task, head_middle, value_out, policy_out, task_table, norm_gain,
    norm_shift, latent_bias, value_bias, policy_bias,
):
    f32, bf16 = jnp.float32, jnp.bfloat16
    batches, lats = lax.axis_size("batch"), lax.axis_size("lat")
    depth, side = major_minor(batches)
    members = (encoder_in, latent_out, head_latent, head_action, head_task, head_middle, value_out,
               policy_out, task_table, norm_gain, norm_shift, latent_bias, value_bias, policy_bias)
    at = Rows(members, batches, lats)
    seqs, horizon, acts = actions.shape
    obs_dim = observations.shape[2]
    tasks = counts.shape[0]
    dims = {"bins": value_out.shape[2], "lin": policy_out.shape[1], "horizon": horizon}
    mine = pack_own(at, members)
    gathered = gather_all(mine, depth, side, at.total // CHUNK_ROWS)

    rows = seqs * horizon
    obs = fill(observations.transpose(1, 0, 2), (horizon + 1, seqs, 128)).reshape(-1, 128)
    by_time = actions.transpose(1, 0, 2).reshape(rows, acts)
    extra = fill(by_time[:, :, None], (rows, at.batches, at.tail_rows), (0, 0, at.task_rows))
    extra = extra.reshape(rows, at.batches * at.tail_rows)
    task_hot = (task_ids[:, None] == jnp.arange(tasks)[None, :]).astype(f32)
    task_counts = jnp.sum(task_hot * counts.astype(f32)[None, :], 1)
    row_weight = 64.0 * lax.rsqrt(task_counts) * (1.0 / math.sqrt(seqs * batches * lats))
    discount = jnp.power(0.5, jnp.arange(horizon).astype(f32))
    columns = [
        by_time.astype(f32),
        by_time.astype(f32),
        (discount[:, None] * row_weight[None, :]).reshape(rows, 1),
        reward_bins.T.reshape(rows, 1).astype(f32),
        value_bins.T.reshape(rows, 1).astype(f32),
        jnp.broadcast_to(task_ids[None].astype(f32), (horizon, seqs)).reshape(rows, 1),
    ]
    info = fill(jnp.concatenate(columns, 1), (rows, 128))
    bias = jnp.concatenate(
        [
            fill(value_bias.astype(f32), (at.heads - 1, 128), (1, 0)),
            fill(policy_bias.astype(f32)[None], (1, 128)),
        ],
        0,
    )
    table = whole_table(at, gathered)
    parts, d_obs = train(at, depth, side, dims, obs, extra, info, table, bias, gathered)
    total = scatter_sum(parts, depth, side, at.total // CHUNK_ROWS)
    grad_observations = d_obs[:, :obs_dim].reshape(horizon + 1, seqs, obs_dim).transpose(1, 0, 2)
    return (grad_observations,) + unpack_own(at, total, dims)


def solution(mesh):
    placed = (
        P(("batch", "lat"), None, None),
        P(("batch", "lat"), None, None),
        P(("batch", "lat")),
        P(),
        P(("batch", "lat"), None),
        P(("batch", "lat"), None),
        P(None, "lat"),
        P(None, "batch", "lat"),
        P(None, "batch", "lat"),
        P(None, None, "lat"),
        P(None, "batch", "lat"),
        P(None, "batch", "lat"),
        P(None, "batch", None),
        P("batch", None),
        P("batch", "lat"),
        P(None, "lat"),
        P(None, "lat"),
        P(None, "lat"),
        P(),
        P(),
    )
    return jax.shard_map(
        local,
        mesh=mesh,
        in_specs=placed,
        out_specs=(
            P(("batch", "lat"), None, None),
            P(None, "lat"),
            P(None, "batch", "lat"),
            P(None, "batch", "lat"),
            P(None, None, "lat"),
            P(None, "batch", "lat"),
            P(None, "batch", "lat"),
            P(None, "batch", None),
            P("batch", None),
            P("batch", "lat"),
            P(None, "lat"),
            P(None, "lat"),
            P(None, "lat"),
            P(),
            P(),
        ),
        check_vma=False,
    )
```

time: 1850 us -> 766 us (0.41)
  local copies, waits for them, and re-layouts: 834 us -> 26 us
  Pallas kernels: 369 us -> 683 us
  other arithmetic: 300 us -> 8.83 us
  matrix products: 289 us -> 0 us
    pallas_call x0 -> x1, Pallas kernels: none -> 314 us  [train(): pl.pallas_call(functools.partial(train_kernel, at, depth, side, dims['hor...]
    dot_general x58 -> x0, matrix products: 289 us -> none  [the longest x39 256 us: contract(): return jnp.einsum(form, left, right, preferred_element_type=jnp.float32)]
    concatenate x17 -> x5, local copies, waits for them, and re-layouts: 231 us -> 0.83 us  [the longest x1 0.33 us: pack_own(): jnp.concatenate([head_latent, head_middle, out, head_task, action, table]...]
    slice x45 -> x13, local copies, waits for them, and re-layouts: 215 us -> 5.21 us  [the longest x1 1.02 us: out_pack(): values[..., n * quarter:(n + 1) * quarter, 2 * unit:]]
    reduce_sum x33 -> x1, other arithmetic: 111 us -> 0.77 us  [local(): task_counts = jnp.sum(task_hot * counts.astype(f32)[None, :], 1)]
    another operation x12 -> x3, local copies, waits for them, and re-layouts: 58.5 us -> 0.26 us  [the longest x1 0.15 us: whole_table(): table = table.reshape(at.batches, at.lats, tr, tc).transpose(0, 2, 1, 3)]
    div x11 -> x0, local copies, waits for them, and re-layouts: 55.9 us -> none  [the longest x10 55.7 us: simnorm(): return jax.nn.softmax(groups, -1).reshape(values.shape)]
    convert_element_type x13 -> x6, other arithmetic: 57.4 us -> 3.51 us  [the longest x1 0.72 us: local(): task_counts = jnp.sum(task_hot * counts.astype(f32)[None, :], 1)]
where the time goes in v2:
time: 766 us; the launch traced here: 755 us
  Pallas kernels  683 us (89%)
  blocking collectives  36.2 us (5%)
  local copies, waits for them, and re-layouts  26 us (3%)
  other arithmetic  8.83 us (1%)
    pallas_call x1, Pallas kernels, train(): pl.pallas_call(functools.partial(train_kernel, at, depth, side, dims['hor...  314 us
    pallas_call x1, Pallas kernels, gather_all(): pl.pallas_call(functools.partial(gather_kernel, depth, side, chunks, rows...  195 us
    pallas_call x1, Pallas kernels, scatter_sum(): pl.pallas_call(functools.partial(scatter_kernel, depth, side, chunks, chu...  174 us
    all_gather x1, blocking collectives, unpack_own(): lax.all_gather(jnp.concatenate([part[0], action], 0), 'batch', axis=0)  30.5 us

profile of v2, /device:TPU:0, one launch (start us, length us, event | category | flops | bytes accessed | tf_op | source)
XLA Modules:
  0.0 755.5 jit_solution(1319153151393951699)
XLA Ops:
  0.7 0.7 convert_element_type.99
  1.4 0.8 select_reduce_fusion
  2.2 0.8 reshape.154
  3.9 0.7 convert_bitcast_fusion.1
  5.4 1.3 fusion.21.bias_ref
  6.7 0.7 fusion.17
  7.5 0.7 copy.157
  8.3 0.7 bitcast_convert_fusion
  9.2 0.7 copy.163
  10.0 0.8 copy.162
  10.9 0.8 copy.164
  11.7 1.0 fusion.28
  13.3 1.0 fusion.27
  14.6 0.8 copy.175.extra_ref
  15.6 0.7 pad.57.clone
  16.7 0.7 pad.59.info_ref
  17.8 1.1 pad_maximum_fusion.mine_ref
  19.0 195.1 %gather_weights.1.all_ref = bf16[2,2,2,4,2240,256]{5,4,3,2,1,0:T(8,128)(2,1)} custom-call(bf16[2240,256]{1,0:T(8,128)(2,1)} %pad_maximum_fusion.mine_ref), custom_call_target="tpu_custom_call" | custom-call | tf_op jit(solution)/shard_map/gather_weights/pallas_call | solution.py:181
  214.1 0.9 fusion.22
  215.7 0.7 copy.176.table_ref
  216.5 314.0 %train.1 = (bf16[2,2,2,4,2240,256]{5,4,3,2,1,0:T(8,128)(2,1)}, f32[768,128]{1,0:T(8,128)}) custom-call(bf16[768,128]{1,0:T(8,128)(2,1)} %bitcast.87, bf16[576,128]{1,0:T(8,128)(2,1)} %copy.175.extra_ref, f32[576,128]{1,0:T(8,128)} %pad.59.info_ref, bf16[128,128]{1,0:T(8,128)(2,1)} %copy.176.table_ref, f32[8,128]{1,0:T(8,128)} %fusion.21.bias_ref, ...), custom_call_target="tpu_custom_call" | custom-call | tf_op jit(solution)/shard_map/train/pallas_call | solution.py:862
  530.4 1.9 copy.177
  532.3 174.1 %scatter_gradients.1 = f32[2240,256]{1,0:T(8,128)} custom-call(bf16[2,2,2,4,2240,256]{5,4,3,2,1,0:T(8,128)(2,1)} %get-tuple-element.18.parts_ref), custom_call_target="tpu_custom_call" | custom-call | tf_op jit(solution)/shard_map/scatter_gradients/pallas_call | solution.py:370
  706.4 0.9 slice.149
  707.3 1.7 slice.144
  709.1 0.7 copy.187
  710.4 0.8 maximum_maximum_fusion
  711.3 1.0 slice.186
  712.3 1.1 slice.190
  713.5 30.5 %all-gather = bf16[192,256]{1,0:T(8,128)(2,1)S(1)} all-gather(bf16[24,256]{1,0:T(8,128)(2,1)S(1)} %pad_maximum_fusion.3), channel_id=2, replica_groups=mesh['batch'=8,'lat'=4] {'batch'}, dimensions={0}, use_global_device_ids=true | all-gather | bytes 110592 | tf_op jit(solution)/shard_map/all_gather | solution.py:1025
  747.8 5.7 all-gather.1
  753.7 0.9 copy.188
  (86 shorter events, 10.0 us)
Async XLA Ops:
  0.6 15.7 %copy-start.2 = (bf16[6,128,101]{1,2,0:T(8,128)(2,1)S(1)}, bf16[6,128,101]{1,2,0:T(8,128)(2,1)}, u32[]{:S(2)}) copy-start(bf16[6,128,101]{1,2,0:T(8,128)(2,1)} %param.32) | copy-start | bytes 465412
  0.7 14.7 %copy-start.3 = (bf16[192,4,39]{0,1,2:T(4,128)(2,1)S(1)}, bf16[192,4,39]{0,1,2:T(4,128)(2,1)}, u32[]{:S(2)}) copy-start(bf16[192,4,39]{0,1,2:T(4,128)(2,1)} %param.20) | copy-start | bytes 179716
  11.7 5.8 copy-start
  11.7 5.8 copy-start.1
  745.4 9.2 %copy-start.4 = (f32[4,256]{1,0:T(4,128)}, f32[4,256]{1,0:T(4,128)S(1)}, u32[]{:S(2)}) copy-start(f32[4,256]{1,0:T(4,128)S(1)} %slice.201) | copy-start | bytes 12292

commit v3 on v2

--- a/solution.py
+++ b/solution.py
@@ -10,7 +10,6 @@
 
 SIMNORM = 8
 HIGHEST = lax.Precision.HIGHEST
-CHUNK_ROWS = 112
 NORM_ROWS = 32
 SOFT_ROWS = 64
 LOSS_ROWS = 64
@@ -23,6 +22,10 @@
 REWARD_AT = 13
 VALUE_AT = 14
 ID_AT = 15
+HIGH_AT = 16
+LOW_AT = 17
+ENTRY_TICKS = 10
+HEAD_TICKS = 6
 
 
 MESH_ID = pl.DeviceIdType.MESH
@@ -89,44 +92,48 @@
     )
 
 
-def gather_kernel(depth, side, chunks, chunk_rows, mine_ref, all_ref, own_sem, send_sems, recv_sems):
-    place = Place(depth, side)
-    steps = gather_steps(depth, side)
-    dims = {name: (pos, size, at) for name, pos, size, at in place.dims()}
-    own = pltpu.make_async_copy(mine_ref, all_ref.at[place.c, place.i, place.j, place.z], own_sem)
-    own.start()
-    place.barrier()
-
-    def block(name, owner, rows):
+class Gather:
+    def __init__(self, place, chunks, chunk_rows, mine_ref, all_ref, own_sem, send_sems, recv_sems):
+        self.place, self.chunks, self.chunk_rows = place, chunks, chunk_rows
+        self.mine_ref, self.all_ref = mine_ref, all_ref
+        self.send_sems, self.recv_sems = send_sems, recv_sems
+        self.steps = gather_steps(place.depth, place.side)
+        self.ticks = chunks + len(self.steps)
+        self.dims = {name: (pos, size, at) for name, pos, size, at in place.dims()}
+        self.own = pltpu.make_async_copy(mine_ref, all_ref.at[place.c, place.i, place.j, place.z], own_sem)
+
+    def block(self, name, owner, rows):
+        place = self.place
         if name == "z":
-            return all_ref.at[place.c, place.i, place.j, owner, rows]
+            return self.all_ref.at[place.c, place.i, place.j, owner, rows]
         if name == "j":
-            return all_ref.at[place.c, place.i, owner, :, rows]
-        return all_ref.at[place.c, owner, :, :, rows]
-
-    def copy(which, t, way, source, target, device):
+            return self.all_ref.at[place.c, place.i, owner, :, rows]
+        return self.all_ref.at[place.c, owner, :, :, rows]
+
+    def copy(self, which, t, way, source, target, device):
         return pltpu.make_async_remote_copy(
             src_ref=source,
             dst_ref=target,
-            send_sem=send_sems.at[which, way, t],
-            recv_sem=recv_sems.at[which, way, t],
+            send_sem=self.send_sems.at[which, way, t],
+            recv_sem=self.recv_sems.at[which, way, t],
             device_id=device,
             device_id_type=MESH_ID,
         )
 
-    def each(which, t, act, sending):
-        name, s = steps[which]
-        rows = pl.ds(pl.multiple_of(t * chunk_rows, 16), chunk_rows)
+    def each(self, which, t, act, sending):
+        name, s = self.steps[which]
+        place = self.place
+        rows = pl.ds(pl.multiple_of(t * self.chunk_rows, 16), self.chunk_rows)
         if name == "c":
             core = place.c if sending else 1 - place.c
-            ref = all_ref.at[core, :, :, :, rows]
-            act(copy(which, t, 0, ref, ref, place.sibling()))
+            ref = self.all_ref.at[core, :, :, :, rows]
+            act(self.copy(which, t, 0, ref, ref, place.sibling()))
             return
-        pos, size, at = dims[name]
+        pos, size, at = self.dims[name]
         if size == 2:
-            ref = block(name, pos if sending else 1 - pos, rows)
-            source = mine_ref.at[rows] if sending and name == "z" and s == 0 else ref
-            act(copy(which, t, 0, source, ref, at(1 - pos)))
+            ref = self.block(name, pos if sending else 1 - pos, rows)
+            source = self.mine_ref.at[rows] if sending and name == "z" and s == 0 else ref
+            act(self.copy(which, t, 0, source, ref, at(1 - pos)))
             return
         if sending:
             ways = (
@@ -142,55 +149,35 @@
 
             @pl.when(valid)
             def _(way=way, owner=owner, target=target):
-                ref = block(name, owner, rows)
-                source = mine_ref.at[rows] if sending and name == "z" and s == 0 else ref
-                act(copy(which, t, way, source, ref, at(target)))
-
-    def body(t, carry):
-        for which in range(len(steps) + 1):
-            at = t - which
-
-            @pl.when((at >= 0) & (at < chunks))
-            def _(which=which, at=at):
-                if which > 0:
-                    each(which - 1, at, lambda c: c.wait_recv(), False)
-                if which < len(steps):
-                    if which == depth - 1:
-
-                        @pl.when(at == 0)
-                        def _():
-                            own.wait()
-
-                    each(which, at, lambda c: c.start(), True)
-
-        return carry
-
-    lax.fori_loop(0, chunks + len(steps), body, 0)
-
-    def drain(t, carry):
-        for which in range(len(steps)):
-            each(which, t, lambda c: c.wait_send(), True)
-        return carry
-
-    lax.fori_loop(0, chunks, drain, 0)
-
-
-def gather_all(mine, depth, side, chunks):
-    rows, cols = mine.shape
-    steps = len(gather_steps(depth, side))
-    return pl.pallas_call(
-        functools.partial(gather_kernel, depth, side, chunks, rows // chunks),
-        out_shape=jax.ShapeDtypeStruct((2, side, side, depth, rows, cols), mine.dtype),
-        in_specs=[pl.BlockSpec(memory_space=pl.ANY)],
-        out_specs=pl.BlockSpec(memory_space=pl.ANY),
-        scratch_shapes=[
-            pltpu.SemaphoreType.DMA,
-            pltpu.SemaphoreType.DMA((steps, 2, chunks)),
-            pltpu.SemaphoreType.DMA((steps, 2, chunks)),
-        ],
-        compiler_params=pltpu.CompilerParams(collective_id=1, has_side_effects=True),
-        name="gather_weights",
-    )(mine)
+                ref = self.block(name, owner, rows)
+                source = self.mine_ref.at[rows] if sending and name == "z" and s == 0 else ref
+                act(self.copy(which, t, way, source, ref, at(target)))
+
+    def tick(self, t):
+        for which in range(len(self.steps) + 1):
+            self.one(t - which, which)
+
+    def one(self, at, which):
+        @pl.when((at >= 0) & (at < self.chunks))
+        def _():
+            if which > 0:
+                self.each(which - 1, at, lambda c: c.wait_recv(), False)
+            if which < len(self.steps):
+                if which == self.place.depth - 1:
+
+                    @pl.when(at == 0)
+                    def _():
+                        self.own.wait()
+
+                self.each(which, at, lambda c: c.start(), True)
+
+    def drain(self):
+        def one(t, carry):
+            for which in range(len(self.steps)):
+                self.each(which, t, lambda c: c.wait_send(), True)
+            return carry
+
+        lax.fori_loop(0, self.chunks, one, 0)
 
 
 def scatter_steps(depth, side):
@@ -468,13 +455,14 @@
 
 
 def train_kernel(
-    at, depth, side, horizon, bins, lin, obs_ref, extra_ref, info_ref, table_ref, bias_ref, all_ref,
-    parts_ref, d_obs_ref, *scratch,
+    at, depth, side, horizon, bins, lin, obs_ref, extra_ref, info_ref, bias_ref, mine_ref,
+    all_ref, parts_ref, d_obs_ref, *scratch,
 ):
     (small, small32, lat_bias, xa, xat, w1d, w2d, lo, stage, enc_hat, enc_slope, enc_hid, enc_inv,
      d1_hat, d1_slope, d1_hid, d1_inv, d2_hat, d2_slope, d2_hid, d2_inv, encoded, predicted,
      w1, w2, vo, hat1, slope1, hid1, inv1, hat2, slope2, hid2, inv2, d_logits, pre,
-     dx, g1, g2, gv, d_lin, sums, d_small, d_small_low, d_bias, load_sems, store_sems, first_sems, last_sems) = scratch
+     dx, g1, g2, gv, d_lin, sums, d_small, d_small_low, d_bias, load_sems, store_sems, first_sems, last_sems,
+     own_sem, gather_send_sems, gather_recv_sems) = scratch
     f32, bf16 = jnp.float32, jnp.bfloat16
     rows = xa.shape[0]
     seqs = rows // horizon
@@ -495,7 +483,7 @@
         lax.fori_loop(0, at.batches, one, 0)
 
     def move_head(k, first, second, third, sems, load):
-        base = k * head_rows
+        base = at.head_at(k)
 
         def body(b, l, where):
             cols = pl.ds(l * at.cols, at.cols)
@@ -527,7 +515,7 @@
     def move_small(ref, sem, load):
         def body(b, l, where):
             here = ref.at[rows_of(b, at.value_rows), pl.ds(l * at.cols, at.cols)]
-            there = (all_ref if load else parts_ref).at[(*where, pl.ds(at.value_at, at.value_rows))]
+            there = (all_ref if load else parts_ref).at[(*where, pl.ds(at.head_at(0) + at.value_at, at.value_rows))]
             pltpu.make_async_copy(*((there, here) if load else (here, there)), sem).start()
 
         for_blocks(body)
@@ -536,7 +524,7 @@
         def body(b, l, where):
             here = stage.at[b * at.lats + l]
             there = (all_ref if load else parts_ref).at[
-                (*where, pl.ds(at.heads * head_rows + n * at.out_rows, at.out_rows))
+                (*where, pl.ds(at.out_at(n), at.out_rows))
             ]
             pltpu.make_async_copy(*((there, here) if load else (here, there)), sem).start()
 
@@ -577,6 +565,26 @@
 
         loop(at.batches // many, body)
 
+    def task_rows(info, first):
+        tail = at.tail_rows * at.batches
+        lanes_of = tail // at.lats
+        per_row = at.cols // lanes_of
+        high = info[:seqs, HIGH_AT : HIGH_AT + 1]
+        low = info[:seqs, LOW_AT : LOW_AT + 1]
+        lane = lax.broadcasted_iota(jnp.int32, (seqs, tail), 1).astype(f32)
+        column = lax.broadcasted_iota(jnp.int32, (1, hidden), 1)
+        piece = (lax.rem(column, at.cols) // lanes_of).astype(f32)
+        down = lax.broadcasted_iota(jnp.int32, (hidden, tail), 0)
+        across = lax.broadcasted_iota(jnp.int32, (hidden, tail), 1)
+        fold = (down // at.cols * lanes_of + lax.rem(down, lanes_of) == across).astype(f32).astype(bf16)
+        total = jnp.zeros((seqs, tail), f32)
+        for n in range(-(-at.table_shape[0] // per_row)):
+            pick = (lane == high * at.tail_rows + (at.task_rows + 1 + n)).astype(f32).astype(bf16)
+            wide = dot(pick, first[latent:, :])
+            wide = jnp.where(piece + n * per_row == low, wide, 0.0).astype(bf16)
+            total = total + dot(wide, fold)
+        return total
+
     def gain_row(n):
         return small32[pl.ds(GAIN_AT + n, 1), :], small32[pl.ds(SHIFT_AT + n, 1), :]
 
@@ -617,16 +625,35 @@
             part = b[:, cols] if how is dot else b[cols, :]
             out[:count, cols] = how(a, part)
 
+    place = Place(depth, side)
+    chunk_rows = at.chunk_rows
+    gather = Gather(
+        place, at.total // chunk_rows, chunk_rows, mine_ref, all_ref, own_sem, gather_send_sems, gather_recv_sems
+    )
+    gather.own.start()
+    place.barrier()
+    entry = at.head_at(1) // chunk_rows + len(gather.steps)
+    ticks = iter(range(entry, entry + ENTRY_TICKS))
+
+    def tick_body(t, carry):
+        gather.tick(t)
+        return carry
+
+    lax.fori_loop(0, entry, tick_body, 0)
+
+    def tick():
+        gather.tick(next(ticks))
+
     move_small(small, first_sems.at[0], True)
     move_out(0, first_sems.at[1], True)
     move_head(0, w1d, w2d, None, first_sems.at[pl.ds(2, 3)], True)
-    move_head(1, w1.at[0], w2.at[0], vo.at[0], load_sems.at[0], True)
     d_small[...] = jnp.zeros_like(d_small)
     dx[...] = jnp.zeros_like(dx)
     ids = info_ref[:seqs, ID_AT : ID_AT + 1]
     lanes = lax.broadcasted_iota(jnp.int32, (seqs, 128), 1).astype(f32)
     task_hot = (lanes == ids).astype(f32)
-    embedded = dot(task_hot.astype(bf16), table_ref[...])
+    wait_head(w1d, w2d, None, first_sems.at[pl.ds(2, 3)])
+    embedded = task_rows(info_ref, w1d)
     for t in range(horizon):
         part = slice(t * seqs, (t + 1) * seqs)
         xa[part, latent:] = (embedded + extra_ref[part, :].astype(f32)).astype(bf16)
@@ -641,15 +668,18 @@
     move_out(1, first_sems.at[1], True)
 
     big_dot(pre, all_rows, obs_ref[...], small)
+    tick()
     gain, shift = gain_row(0)
     norm_forward(pre, all_rows, 0, gain, shift, enc_hat, enc_slope, enc_hid, enc_inv)
+    tick()
     big_dot(pre, all_rows, enc_hid[...], lo.at[0])
+    tick()
     pre[:all_rows, :latent] += lat_bias[0:1, :]
     simnorm_forward(all_rows, 0, encoded)
+    tick()
     xa[:seqs, :latent] = encoded[:seqs, :].astype(bf16)
     pltpu.make_async_copy(stage, stage, first_sems.at[1]).wait()
     stage_to_out(1)
-    wait_head(w1d, w2d, None, first_sems.at[pl.ds(2, 3)])
 
     gain1, shift1 = gain_row(1)
     gain2, shift2 = gain_row(2)
@@ -657,13 +687,16 @@
         part = slice(t * seqs, (t + 1) * seqs)
         big_dot(pre, seqs, xa[part, :], w1d)
         norm_forward(pre, seqs, t * seqs, gain1, shift1, d1_hat, d1_slope, d1_hid, d1_inv)
+        tick()
         big_dot(pre, seqs, d1_hid[part, :], w2d)
         norm_forward(pre, seqs, t * seqs, gain2, shift2, d2_hat, d2_slope, d2_hid, d2_inv)
+        tick()
         big_dot(pre, seqs, d2_hid[part, :], lo.at[1])
         pre[:seqs, :latent] += lat_bias[1:2, :]
         simnorm_forward(seqs, t * seqs, predicted)
         if t + 1 < horizon:
             xa[(t + 1) * seqs : (t + 2) * seqs, :latent] = predicted[part, :].astype(bf16)
+    move_head(1, w1.at[0], w2.at[0], vo.at[0], load_sems.at[0], True)
     for n in range(xa.shape[1] // 128):
         xat[n * 128 : (n + 1) * 128, :] = xa[:, n * 128 : (n + 1) * 128].T
 
@@ -674,17 +707,28 @@
     def head(k):
         slot = lax.rem(k - 1, 2)
         wait_head(w1.at[slot], w2.at[slot], vo.at[slot], load_sems.at[slot])
+        first_tick = entry + ENTRY_TICKS + (k - 1) * HEAD_TICKS
+
+        def tick(n):
+            @pl.when(first_tick + n < gather.ticks)
+            def _():
+                gather.tick(first_tick + n)
+
+        gain1, shift1 = gain_row(2 * k + 1)
+        gain2, shift2 = gain_row(2 * k + 2)
+        big_dot(pre, rows, xa[...], w1.at[slot])
+        tick(0)
+        norm_forward(pre, rows, 0, gain1, shift1, hat1, slope1, hid1, inv1)
+        tick(1)
+        big_dot(pre, rows, hid1[...], w2.at[slot])
+        tick(2)
+        norm_forward(pre, rows, 0, gain2, shift2, hat2, slope2, hid2, inv2)
+        tick(3)
 
         @pl.when(k + 1 < heads)
         def _():
             move_head(k + 1, w1.at[1 - slot], w2.at[1 - slot], vo.at[1 - slot], load_sems.at[1 - slot], True)
 
-        gain1, shift1 = gain_row(2 * k + 1)
-        gain2, shift2 = gain_row(2 * k + 2)
-        big_dot(pre, rows, xa[...], w1.at[slot])
-        norm_forward(pre, rows, 0, gain1, shift1, hat1, slope1, hid1, inv1)
-        big_dot(pre, rows, hid1[...], w2.at[slot])
-        norm_forward(pre, rows, 0, gain2, shift2, hat2, slope2, hid2, inv2)
         pre[:rows, :128] = dot(hid2[...], vo[slot]) + bias_ref[pl.ds(k, 1), :]
         clear_sums()
 
@@ -728,10 +772,12 @@
         big_dot(pre, rows, d_logits[...], vo.at[slot], dot_t)
         clear_sums()
         norm_backward(pre, rows, 0, gain2, hat2, slope2, inv2, hat2, sums.at[0])
+        tick(4)
         keep_sums(2 * k + 2)
         big_dot(pre, rows, hat2[...], w2.at[slot], dot_t)
         clear_sums()
         norm_backward(pre, rows, 0, gain1, hat1, slope1, inv1, hat1, sums.at[0])
+        tick(5)
         keep_sums(2 * k + 1)
         for n in range(dx.shape[1] // 128):
             dx[:, n * 128 : (n + 1) * 128] += dot_t(hat1[...], w1[slot, n * 128 : (n + 1) * 128, :])
@@ -761,6 +807,9 @@
         return carry
 
     lax.fori_loop(1, heads, heads_body, 0)
+
+    assert next(ticks, None) is None
+    gather.drain()
 
     scale = 2.0 * 20.0 / latent
 
@@ -842,12 +891,13 @@
     pltpu.make_async_copy(stage, stage, last_sems.at[0]).wait()
 
 
-def train(at, depth, side, dims, obs, extra, info, table, bias, gathered):
+def train(at, depth, side, dims, obs, extra, info, bias, mine):
     rows, all_rows = extra.shape[0], obs.shape[0]
     latent = at.latent_rows * at.batches
     hidden = at.middle_rows * at.batches
     wide = latent + at.tail_rows * at.batches
     f32, bf16 = jnp.float32, jnp.bfloat16
+    gather_count = len(gather_steps(depth, side))
 
     def saved(count):
         return [
@@ -862,11 +912,12 @@
     return pl.pallas_call(
         functools.partial(train_kernel, at, depth, side, dims["horizon"], dims["bins"], dims["lin"]),
         out_shape=[
-            jax.ShapeDtypeStruct(gathered.shape, bf16),
+            jax.ShapeDtypeStruct((2, side, side, depth, *mine.shape), bf16),
+            jax.ShapeDtypeStruct((2, side, side, depth, *mine.shape), bf16),
             jax.ShapeDtypeStruct((all_rows, 128), f32),
         ],
-        in_specs=[vmem, vmem, vmem, vmem, vmem, hbm],
-        out_specs=[hbm, vmem],
+        in_specs=[vmem, vmem, vmem, vmem, hbm],
+        out_specs=[hbm, hbm, vmem],
         scratch_shapes=[
             pltpu.VMEM((128, hidden), bf16),
             pltpu.VMEM((128, hidden), f32),
@@ -906,10 +957,15 @@
             pltpu.SemaphoreType.DMA((3,)),
             pltpu.SemaphoreType.DMA((5,)),
             pltpu.SemaphoreType.DMA((2,)),
+            pltpu.SemaphoreType.DMA,
+            pltpu.SemaphoreType.DMA((gather_count, 2, at.total // at.chunk_rows)),
+            pltpu.SemaphoreType.DMA((gather_count, 2, at.total // at.chunk_rows)),
         ],
-        compiler_params=pltpu.CompilerParams(vmem_limit_bytes=62 * 2**20),
+        compiler_params=pltpu.CompilerParams(
+            collective_id=1, has_side_effects=True, vmem_limit_bytes=62 * 2**20
+        ),
         name="train",
-    )(obs, extra, info, table, bias, gathered)
+    )(obs, extra, info, bias, mine)[1:]
 
 
 def round_up(n, to):
@@ -940,6 +996,15 @@
         self.latent_cols = latent_out.shape[2]
         self.wide_rows = 8 // self.pieces
         self.total = self.heads * self.head_rows + 2 * self.out_rows
+        self.chunk_rows = self.head_rows // 4
+
+    def head_at(self, k):
+        if isinstance(k, int):
+            return k * self.head_rows + (2 * self.out_rows if k else 0)
+        return k * self.head_rows + jnp.where(k > 0, 2 * self.out_rows, 0)
+
+    def out_at(self, n):
+        return self.head_rows + (1 - n) * self.out_rows
 
 
 def fill(values, shape, before=None):
@@ -996,30 +1061,21 @@
     out = jnp.concatenate([small[None], out], 0)
     action = fill(head_action, (at.heads, at.batches, at.cols))
     action = lax.dynamic_slice_in_dim(action, batch, 1, 1)
-    table = fill(task_table.reshape(1, 1, -1), (at.heads, at.tail_rows - at.task_rows - 1, at.cols))
+    tr, tc = at.table_shape
+    per_row = at.cols // (at.batches * at.tail_rows // at.lats)
+    table = fill(task_table.reshape(tr, -1, at.task_rows), (round_up(tr, per_row), tc // at.task_rows, at.tail_rows))
+    table = table.reshape(1, -1, at.cols)
+    table = fill(table, (at.heads, at.tail_rows - at.task_rows - 1, at.cols))
     heads = jnp.concatenate([head_latent, head_middle, out, head_task, action, table], 1)
-    tail = out_pack(at, latent_out).reshape(2 * at.out_rows, at.cols)
-    return jnp.concatenate([heads.reshape(at.heads * at.head_rows, at.cols), tail], 0)
-
-
-def by_device(at, gathered):
-    both = jnp.stack([gathered[0], jnp.swapaxes(gathered[1], 0, 1)], 0)
-    return both.transpose(3, 2, 1, 0, 4, 5).reshape((at.batches, at.lats) + gathered.shape[-2:])
-
-
-def whole_table(at, gathered):
-    tr, tc = at.table_shape
-    row = at.task_at + at.task_rows + 1
-    table = by_device(at, gathered[:, :, :, :, row : row + 1, : tr * tc])
-    table = table.reshape(at.batches, at.lats, tr, tc).transpose(0, 2, 1, 3)
-    table = table.reshape(at.batches * tr, at.batches, at.task_rows)
-    table = fill(table, (128, at.batches, at.tail_rows))
-    return table.reshape(128, at.batches * at.tail_rows)
+    tail = out_pack(at, latent_out)
+    return jnp.concatenate([heads[0], tail[1], tail[0], heads[1:].reshape(-1, at.cols)], 0)
 
 
 def unpack_own(at, total, dims):
-    split = at.heads * at.head_rows
-    heads = total[:split].reshape(at.heads, at.head_rows, at.cols)
+    split = at.head_at(1)
+    heads = jnp.concatenate([total[: at.head_rows], total[split:]], 0)
+    heads = heads.reshape(at.heads, at.head_rows, at.cols)
+    outs = total[at.head_rows : split].reshape(2, at.out_rows, at.cols)[::-1]
     part = heads[:, at.value_at : at.value_at + at.value_rows].astype(jnp.bfloat16)
     action = heads[:, at.task_at + at.task_rows].astype(jnp.bfloat16)
     split_over_lat = lax.all_gather(jnp.concatenate([part[0], action], 0), "batch", axis=0)
@@ -1036,7 +1092,7 @@
     wide = wide.transpose(1, 0, 2).reshape(8, 128)
     return (
         small[: at.obs],
-        out_unpack(at, total[split:].reshape(2, at.out_rows, at.cols)),
+        out_unpack(at, outs),
         heads[:, : at.latent_rows],
         action,
         heads[:, at.task_at : at.task_at + at.task_rows],
@@ -1068,8 +1124,6 @@
     tasks = counts.shape[0]
     dims = {"bins": value_out.shape[2], "lin": policy_out.shape[1], "horizon": horizon}
     mine = pack_own(at, members)
-    gathered = gather_all(mine, depth, side, at.total // CHUNK_ROWS)
-
     rows = seqs * horizon
     obs = fill(observations.transpose(1, 0, 2), (horizon + 1, seqs, 128)).reshape(-1, 128)
     by_time = actions.transpose(1, 0, 2).reshape(rows, acts)
@@ -1079,13 +1133,19 @@
     task_counts = jnp.sum(task_hot * counts.astype(f32)[None, :], 1)
     row_weight = 64.0 * lax.rsqrt(task_counts) * (1.0 / math.sqrt(seqs * batches * lats))
     discount = jnp.power(0.5, jnp.arange(horizon).astype(f32))
+
+    def each_time(values):
+        return jnp.broadcast_to(values[None].astype(f32), (horizon, seqs)).reshape(rows, 1)
+
     columns = [
         by_time.astype(f32),
         by_time.astype(f32),
         (discount[:, None] * row_weight[None, :]).reshape(rows, 1),
         reward_bins.T.reshape(rows, 1).astype(f32),
         value_bins.T.reshape(rows, 1).astype(f32),
-        jnp.broadcast_to(task_ids[None].astype(f32), (horizon, seqs)).reshape(rows, 1),
+        each_time(task_ids),
+        each_time(lax.div(task_ids, at.table_shape[0])),
+        each_time(lax.rem(task_ids, at.table_shape[0])),
     ]
     info = fill(jnp.concatenate(columns, 1), (rows, 128))
     bias = jnp.concatenate(
@@ -1095,9 +1155,8 @@
         ],
         0,
     )
-    table = whole_table(at, gathered)
-    parts, d_obs = train(at, depth, side, dims, obs, extra, info, table, bias, gathered)
-    total = scatter_sum(parts, depth, side, at.total // CHUNK_ROWS)
+    parts, d_obs = train(at, depth, side, dims, obs, extra, info, bias, mine)
+    total = scatter_sum(parts, depth, side, at.total // at.chunk_rows)
     grad_observations = d_obs[:, :obs_dim].reshape(horizon + 1, seqs, obs_dim).transpose(1, 0, 2)
     return (grad_observations,) + unpack_own(at, total, dims)
 

time: 766 us -> 702 us (0.916)
  Pallas kernels: 683 us -> 621 us
    pallas_call x1 -> x0, Pallas kernels: 195 us -> none  [gather_all(): pl.pallas_call(functools.partial(gather_kernel, depth, side, chunks, rows...]
    pallas_call x1, Pallas kernels: 314 us -> 447 us  [train(): pl.pallas_call(functools.partial(train_kernel, at, depth, side, dims['hor...]
where the time goes in v3:
time: 702 us; the launch traced here: 692 us
  Pallas kernels  621 us (88%)
  blocking collectives  36.2 us (5%)
  local copies, waits for them, and re-layouts  23.9 us (3%)
  other arithmetic  8.82 us (1%)
    pallas_call x1, Pallas kernels, train(): pl.pallas_call(functools.partial(train_kernel, at, depth, side, dims['hor...  447 us
    pallas_call x1, Pallas kernels, scatter_sum(): pl.pallas_call(functools.partial(scatter_kernel, depth, side, chunks, chu...  174 us
    all_gather x1, blocking collectives, unpack_own(): lax.all_gather(jnp.concatenate([part[0], action], 0), 'batch', axis=0)  30.5 us

profile of v3, /device:TPU:0, one launch (start us, length us, event | category | flops | bytes accessed | tf_op | source)
XLA Modules:
  0.0 691.5 jit_solution(8418137316733602878)
XLA Ops:
  0.7 0.7 convert_element_type.107
  1.4 0.8 select_reduce_fusion
  2.3 0.8 remainder_convert_fusion
  3.4 0.7 convert_bitcast_fusion.1
  4.2 0.7 convert_bitcast_fusion
  4.9 1.3 fusion.21.bias_ref
  6.2 0.8 reshape.160
  7.1 0.7 fusion.17
  7.8 0.7 copy.162
  8.7 0.7 bitcast_convert_fusion
  9.6 0.7 copy.168
  10.4 0.8 copy.167
  11.2 0.8 copy.169
  12.0 1.0 fusion.27
  13.5 1.0 fusion.26
  14.9 0.8 copy.176.extra_ref
  15.9 0.7 pad.57.clone
  17.0 0.7 pad.59.info_ref
  18.2 1.1 pad_maximum_fusion.1.mine_ref
  19.3 446.9 %train.1 = (bf16[2,2,2,4,2240,256]{5,4,3,2,1,0:T(8,128)(2,1)}, bf16[2,2,2,4,2240,256]{5,4,3,2,1,0:T(8,128)(2,1)}, f32[768,128]{1,0:T(8,128)}) custom-call(bf16[768,128]{1,0:T(8,128)(2,1)} %bitcast.75, bf16[576,128]{1,0:T(8,128)(2,1)} %copy.176.extra_ref, f32[576,128]{1,0:T(8,128)} %pad.59.info_ref, f32[8,128]{1,0:T(8,128)} %fusion.21.bias_ref, ...), custom_call_target="tpu_custom_call" | custom-call | tf_op jit(solution)/shard_map/train/pallas_call | solution.py:912
  466.2 1.9 copy.177
  468.1 174.3 %scatter_gradients.1 = f32[2240,256]{1,0:T(8,128)} custom-call(bf16[2,2,2,4,2240,256]{5,4,3,2,1,0:T(8,128)(2,1)} %get-tuple-element.18.parts_ref), custom_call_target="tpu_custom_call" | custom-call | tf_op jit(solution)/shard_map/scatter_gradients/pallas_call | solution.py:357
  642.4 0.9 slice.176
  644.0 0.8 maximum_maximum_fusion
  644.9 0.9 slice-done
  646.6 0.7 copy.187
  647.3 0.9 slice.223
  648.4 1.0 slice.227
  649.5 30.5 %all-gather = bf16[192,256]{1,0:T(8,128)(2,1)S(1)} all-gather(bf16[24,256]{1,0:T(8,128)(2,1)S(1)} %pad_maximum_fusion.2), channel_id=2, replica_groups=mesh['batch'=8,'lat'=4] {'batch'}, dimensions={0}, use_global_device_ids=true | all-gather | bytes 110592 | tf_op jit(solution)/shard_map/all_gather | solution.py:1081
  680.1 0.7 copy.190
  683.8 5.7 all-gather.1
  689.7 0.9 copy.188
  (93 shorter events, 8.3 us)
Async XLA Ops:
  0.6 15.9 %copy-start.2 = (bf16[6,128,101]{1,2,0:T(8,128)(2,1)S(1)}, bf16[6,128,101]{1,2,0:T(8,128)(2,1)}, u32[]{:S(2)}) copy-start(bf16[6,128,101]{1,2,0:T(8,128)(2,1)} %param.32) | copy-start | bytes 465412
  0.7 15.0 %copy-start.3 = (bf16[192,4,39]{0,1,2:T(4,128)(2,1)S(1)}, bf16[192,4,39]{0,1,2:T(4,128)(2,1)}, u32[]{:S(2)}) copy-start(bf16[192,4,39]{0,1,2:T(4,128)(2,1)} %param.20) | copy-start | bytes 179716
  13.1 4.7 copy-start
  13.1 4.7 copy-start.1
  644.9 0.9 slice-start
  644.9 1.6 slice-start.1
  681.4 8.3 %copy-start.4 = (f32[4,256]{1,0:T(4,128)}, f32[4,256]{1,0:T(4,128)S(1)}, u32[]{:S(2)}) copy-start(f32[4,256]{1,0:T(4,128)S(1)} %slice.238) | copy-start | bytes 12292

commit v4 on v3

--- a/solution.py
+++ b/solution.py
@@ -10,9 +10,9 @@
 
 SIMNORM = 8
 HIGHEST = lax.Precision.HIGHEST
-NORM_ROWS = 32
-SOFT_ROWS = 64
-LOSS_ROWS = 64
+NORM_ROWS = 192
+SOFT_ROWS = 192
+LOSS_ROWS = 192
 GAIN_AT = 40
 SHIFT_AT = 64
 BIAS_AT = 88
@@ -26,6 +26,9 @@
 LOW_AT = 17
 ENTRY_TICKS = 10
 HEAD_TICKS = 6
+LAG = 2
+SCATTER_LAG = 2
+VMEM_LIMIT = 62 * 2**20
 
 
 MESH_ID = pl.DeviceIdType.MESH
@@ -98,7 +101,7 @@
         self.mine_ref, self.all_ref = mine_ref, all_ref
         self.send_sems, self.recv_sems = send_sems, recv_sems
         self.steps = gather_steps(place.depth, place.side)
-        self.ticks = chunks + len(self.steps)
+        self.ticks = chunks + LAG * len(self.steps)
         self.dims = {name: (pos, size, at) for name, pos, size, at in place.dims()}
         self.own = pltpu.make_async_copy(mine_ref, all_ref.at[place.c, place.i, place.j, place.z], own_sem)
 
@@ -153,12 +156,12 @@
                 source = self.mine_ref.at[rows] if sending and name == "z" and s == 0 else ref
                 act(self.copy(which, t, way, source, ref, at(target)))
 
-    def tick(self, t):
+    def tick(self, t, first, last, lag):
         for which in range(len(self.steps) + 1):
-            self.one(t - which, which)
-
-    def one(self, at, which):
-        @pl.when((at >= 0) & (at < self.chunks))
+            self.one(t - lag * which, which, first, last)
+
+    def one(self, at, which, first, last):
+        @pl.when((at >= first) & (at < last))
         def _():
             if which > 0:
                 self.each(which - 1, at, lambda c: c.wait_recv(), False)
@@ -189,191 +192,310 @@
     )
 
 
-def scatter_kernel(depth, side, chunks, chunk_rows, parts_ref, sum_ref, *scratch):
-    held, own_buf, own_sems, send_sems, recv_sems = scratch[:5]
-    landing = dict(zip(("i", "j", "z"), (scratch[5:7], scratch[7:9], scratch[9:11])))
-    place = Place(depth, side)
-    steps = scatter_steps(depth, side)
-    dims = {name: (pos, size, at) for name, pos, size, at in place.dims()}
-    place.barrier()
-
-    def block(name, owner, rows):
+class Scatter:
+    def __init__(self, place, chunks, chunk_rows, row_of, parts_ref, sum_ref, scratch):
+        self.place, self.chunks, self.chunk_rows, self.row_of = place, chunks, chunk_rows, row_of
+        self.parts_ref, self.sum_ref = parts_ref, sum_ref
+        self.held, self.own_buf, self.own_sems, self.send_sems, self.recv_sems, self.free_sems = scratch[:6]
+        self.landing = dict(zip(("i", "j", "z"), (scratch[6:8], scratch[8:10], scratch[10:12])))
+        self.steps = scatter_steps(place.depth, place.side)
+        self.lag = scatter_lag(place.side)
+        self.ticks = chunks + self.lag * len(self.steps)
+        self.rings = scatter_rings(place.depth, place.side)
+        self.dims = {name: (pos, size, at) for name, pos, size, at in place.dims()}
+
+    def rows(self, n):
+        return pl.ds(pl.multiple_of(self.row_of(n), 16), self.chunk_rows)
+
+    def block(self, name, owner, n):
         if name == "z":
-            return held.at[place.i, place.j, owner, rows]
+            return self.result("j", n).at[owner]
         if name == "j":
-            return held.at[place.i, owner, :, rows]
-        return held.at[owner, :, :, rows]
-
-    def land(name, owner, rows):
+            return self.result("i", n).at[owner]
+        return self.result("c", n).at[owner]
+
+    def result(self, name, n):
+        slot = lax.rem(n, self.rings[name])
+        return self.held.at[slot] if name == "c" else self.landing[name][1].at[slot]
+
+    def land(self, name, owner, n):
+        slot = lax.rem(n, self.rings[name])
         if owner is None:
-            ref = landing[name][1]
-        else:
-            ref = landing[name][0].at[owner]
-        if name == "z":
-            return ref.at[rows]
-        if name == "j":
-            return ref.at[:, rows]
-        return ref.at[:, :, rows]
-
-    def add(into, other):
+            return self.landing[name][1].at[slot]
+        return self.landing[name][0].at[slot, owner]
+
+    def add(self, into, other):
         lead = into.shape[:-2]
         if not lead:
             into[...] += other[...]
             return
 
-        def one(n, carry):
+        def one(m, carry):
             index = []
             for extent in reversed(lead):
-                index.insert(0, lax.rem(n, extent))
-                n = n // extent
+                index.insert(0, lax.rem(m, extent))
+                m = lax.div(m, extent)
             into[tuple(index)] += other[tuple(index)]
             return carry
 
         lax.fori_loop(0, math.prod(lead), one, 0)
 
-    def own_copy(t):
-        rows = pl.ds(pl.multiple_of(t * chunk_rows, 16), chunk_rows)
-        slot = lax.rem(t, 2)
+    def own_copy(self, n):
+        slot = lax.rem(n, self.lag + 1)
         return pltpu.make_async_copy(
-            parts_ref.at[place.c, :, :, :, rows], own_buf.at[slot], own_sems.at[slot]
+            self.parts_ref.at[self.place.c, :, :, :, self.rows(n)], self.own_buf.at[slot], self.own_sems.at[slot]
         )
 
-    def copy(which, t, way, source, target, device):
+    def copy(self, which, n, way, source, target, device):
         return pltpu.make_async_remote_copy(
             src_ref=source,
             dst_ref=target,
-            send_sem=send_sems.at[which, way, t],
-            recv_sem=recv_sems.at[which, way, t],
+            send_sem=self.send_sems.at[which, way, n],
+            recv_sem=self.recv_sems.at[which, way, n],
             device_id=device,
             device_id_type=MESH_ID,
         )
 
-    def send(which, t, act):
-        name, s = steps[which]
-        rows = pl.ds(pl.multiple_of(t * chunk_rows, 16), chunk_rows)
+    def free(self, name, way=0):
+        return self.free_sems.at[0 if name == "c" else 1 + 2 * "ijz".index(name) + way]
+
+    def await_free(self, name, n, way=0):
+        @pl.when(n >= self.rings[name])
+        def _():
+            pl.semaphore_wait(self.free(name, way), 1)
+
+    def send(self, which, n, starting):
+        name, s = self.steps[which]
+        place = self.place
+
+        def act(copy):
+            if starting:
+                copy.start()
+            else:
+                copy.wait_send()
+
         if name == "c":
-            act(
-                copy(
-                    which, t, 0, parts_ref.at[1 - place.c, :, :, :, rows],
-                    held.at[:, :, :, rows], place.sibling(),
-                )
-            )
+            if starting:
+                self.await_free(name, n)
+            source = self.parts_ref.at[1 - place.c, :, :, :, self.rows(n)]
+            act(self.copy(which, n, 0, source, self.result("c", n), place.sibling()))
             return
-        pos, size, at = dims[name]
+        pos, size, at = self.dims[name]
         if size == 2:
-            act(copy(which, t, 0, block(name, 1 - pos, rows), land(name, None, rows), at(1 - pos)))
+            if starting:
+                self.await_free(name, n)
+            act(self.copy(which, n, 0, self.block(name, 1 - pos, n), self.land(name, None, n), at(1 - pos)))
             return
         back = size - 1 - pos
         last = s == size - 2
 
         @pl.when((pos <= s) & (pos < size - 1))
         def _():
+            if starting:
+
+                @pl.when(pos == s)
+                def _():
+                    self.await_free(name, n, 0)
+
             owner = size - 1 - (s - pos)
-            act(copy(which, t, 0, block(name, owner, rows), land(name, owner, rows), at(pos + 1)))
+            act(self.copy(which, n, 0, self.block(name, owner, n), self.land(name, owner, n), at(pos + 1)))
 
         @pl.when((back <= s) & (pos > 0))
         def _():
+            if starting:
+
+                @pl.when(back == s)
+                def _():
+                    self.await_free(name, n, 1)
+
             owner = s - back
-            act(
-                copy(
-                    which, t, 1, block(name, owner, rows),
-                    land(name, None if last else owner, rows), at(pos - 1),
-                )
-            )
-
-    def receive(which, t):
-        name, s = steps[which]
-        rows = pl.ds(pl.multiple_of(t * chunk_rows, 16), chunk_rows)
+            target = self.land(name, None if last else owner, n)
+            act(self.copy(which, n, 1, self.block(name, owner, n), target, at(pos - 1)))
+
+    def receive(self, which, n):
+        name, s = self.steps[which]
         if name == "c":
-            copy(
-                which, t, 0, held.at[:, :, :, rows], held.at[:, :, :, rows], place.sibling()
-            ).wait_recv()
-            own_copy(t).wait()
-            add(held.at[:, :, :, rows], own_buf.at[lax.rem(t, 2)])
+            ref = self.result("c", n)
+            self.copy(which, n, 0, ref, ref, self.place.sibling()).wait_recv()
+            self.own_copy(n).wait()
+            self.add(ref, self.own_buf.at[lax.rem(n, self.lag + 1)])
             return
-        pos, size, at = dims[name]
+        pos, size, at = self.dims[name]
         if size == 2:
-            ref = land(name, None, rows)
-            copy(which, t, 0, ref, ref, at(1 - pos)).wait_recv()
-            add(block(name, pos, rows), ref)
+            ref = self.land(name, None, n)
+            self.copy(which, n, 0, ref, ref, at(1 - pos)).wait_recv()
+            self.add(ref, self.block(name, pos, n))
             return
         last = s == size - 2
 
         @pl.when((pos - 1 <= s) & (pos >= 1))
         def _():
             owner = size - 1 - (s - (pos - 1))
-            ref = land(name, owner, rows)
-            copy(which, t, 0, ref, ref, at(pos - 1)).wait_recv()
-            add(block(name, owner, rows), ref)
+            ref = self.land(name, owner, n)
+            self.copy(which, n, 0, ref, ref, at(pos - 1)).wait_recv()
+            self.add(self.block(name, owner, n), ref)
 
         @pl.when((size - 2 - pos <= s) & (pos < size - 1))
         def _():
             owner = s - (size - 2 - pos)
-            ref = land(name, None if last else owner, rows)
-            copy(which, t, 1, ref, ref, at(pos + 1)).wait_recv()
-            add(block(name, owner, rows), ref)
-
-    def body(t, carry):
-        @pl.when(t < chunks)
+            ref = self.land(name, None if last else owner, n)
+            self.copy(which, n, 1, ref, ref, at(pos + 1)).wait_recv()
+            if last:
+                self.add(ref, self.block(name, owner, n))
+            else:
+                self.add(self.block(name, owner, n), ref)
+
+        if last:
+
+            @pl.when(pos == size - 1)
+            def _():
+                self.result(name, n)[...] = self.block(name, pos, n)[...]
+
+    def over(self, which, n):
+        name, s = self.steps[which]
+        if name == "c" or s != self.dims[name][1] - 2:
+            return
+        for other, (its, _) in enumerate(self.steps):
+            if its == name or (its == "c" and name == "i"):
+                self.send(other, n, False)
+        fed_by = {"i": "c", "j": "i", "z": "j"}[name]
+        self.release(fed_by, n)
+        if name == "z":
+            self.sum_ref[self.rows(n), :] = self.result("z", n)[...]
+            self.release("z", n)
+
+    def release(self, name, n):
+        place = self.place
+
+        @pl.when(n + self.rings[name] < self.chunks)
         def _():
-            own_copy(t).start()
-
-        for which in range(len(steps) + 1):
-            at = t - which
-
-            @pl.when((at >= 0) & (at < chunks))
-            def _(which=which, at=at):
-                if which > 0:
-                    receive(which - 1, at)
-                if which < len(steps):
-                    send(which, at, lambda c: c.start())
-                else:
-                    rows = pl.ds(pl.multiple_of(at * chunk_rows, 16), chunk_rows)
-                    sum_ref[rows, :] = held[place.i, place.j, place.z, rows, :].astype(sum_ref.dtype)
-
-        return carry
-
-    lax.fori_loop(0, chunks + len(steps), body, 0)
-
-    def drain(t, carry):
-        for which in range(len(steps)):
-            send(which, t, lambda c: c.wait_send())
-        return carry
-
-    lax.fori_loop(0, chunks, drain, 0)
-
-
-def scatter_sum(parts, depth, side, chunks):
-    rows, cols = parts.shape[-2:]
-    chunk_rows = rows // chunks
+            def signal(sem, device):
+                pl.semaphore_signal(sem, inc=1, device_id=device, device_id_type=MESH_ID)
+
+            if name == "c":
+                signal(self.free("c"), place.sibling())
+                return
+            pos, size, at = self.dims[name]
+            if size == 2:
+                signal(self.free(name), at(1 - pos))
+                return
+            for way, valid, target in ((0, pos > 0, pos - 1), (1, pos < size - 1, pos + 1)):
+
+                @pl.when(valid)
+                def _(way=way, target=target):
+                    signal(self.free(name, way), at(target))
+
+    def tick(self, t):
+        @pl.when(t < self.chunks)
+        def _():
+            self.own_copy(t).start()
+
+        for which in range(len(self.steps) + 1):
+            self.one(t - self.lag * which, which)
+
+    def one(self, n, which):
+        @pl.when((n >= 0) & (n < self.chunks))
+        def _():
+            if which > 0:
+                self.receive(which - 1, n)
+                self.over(which - 1, n)
+            if which < len(self.steps):
+                self.send(which, n, True)
+
+
+def scatter_lag(side):
+    return SCATTER_LAG if side == 2 else 1
+
+
+def scatter_rings(depth, side):
+    lag = scatter_lag(side)
+    return {"c": side * lag + 2, "i": side * lag + 2, "j": depth * lag + 1, "z": (depth - 1) * lag + 2}
+
+
+def scatter_scratch(depth, side, chunks, chunk_rows, cols, dtype):
     steps = len(scatter_steps(depth, side))
-    dtype = parts.dtype
-
-    def landing(size, *lead):
-        first = (size,) + lead if size > 2 else (1,)
-        tail = (rows, cols) if size > 2 else (16, 128)
-        return [pltpu.VMEM(first + tail, dtype), pltpu.VMEM(lead + (rows, cols), dtype)]
-
-    return pl.pallas_call(
-        functools.partial(scatter_kernel, depth, side, chunks, chunk_rows),
-        out_shape=jax.ShapeDtypeStruct((rows, cols), jnp.float32),
-        in_specs=[pl.BlockSpec(memory_space=pl.ANY)],
-        out_specs=pl.BlockSpec(memory_space=pltpu.VMEM),
-        scratch_shapes=[
-            pltpu.VMEM((side, side, depth, rows, cols), dtype),
-            pltpu.VMEM((2, side, side, depth, chunk_rows, cols), dtype),
-            pltpu.SemaphoreType.DMA((2,)),
+
+    rings = scatter_rings(depth, side)
+
+    def landing(name, size, *lead):
+        tail = (chunk_rows, cols)
+        first = (rings[name], size) + lead + tail if size > 2 else (1, 1, 16, 128)
+        return [pltpu.VMEM(first, dtype), pltpu.VMEM((rings[name],) + lead + tail, dtype)]
+
+    return (
+        [
+            pltpu.VMEM((rings["c"], side, side, depth, chunk_rows, cols), dtype),
+            pltpu.VMEM((scatter_lag(side) + 1, side, side, depth, chunk_rows, cols), dtype),
+            pltpu.SemaphoreType.DMA((scatter_lag(side) + 1,)),
             pltpu.SemaphoreType.DMA((steps, 2, chunks)),
             pltpu.SemaphoreType.DMA((steps, 2, chunks)),
+            pltpu.SemaphoreType.REGULAR((7,)),
         ]
-        + landing(side, side, depth)
-        + landing(side, depth)
-        + landing(depth),
-        compiler_params=pltpu.CompilerParams(
-            collective_id=2, has_side_effects=True, vmem_limit_bytes=60 * 2**20
-        ),
-        name="scatter_gradients",
-    )(parts)
+        + landing("i", side, side, depth)
+        + landing("j", side, depth)
+        + landing("z", depth)
+    )
+
+
+def share_steps(depth, side):
+    over_batch = [("x", s) for s in range(side - 1)] + [("z", s) for s in range(depth - 1)]
+    over_lat = [("c", 0)] + [("y", s) for s in range(side - 1)]
+    return over_batch, over_lat
+
+
+def share(place, batch_ref, lat_ref, send_sems, recv_sems):
+    z, side, c = place.z, place.side, place.c
+    x, y = jnp.where(c == 0, place.j, place.i), jnp.where(c == 0, place.i, place.j)
+    lines = {
+        "x": (x, side, lambda o: batch_ref.at[z * side + o], lambda p: (z * side + p, y * 2 + c)),
+        "z": (z, place.depth, lambda o: batch_ref.at[pl.ds(o * side, side)], lambda p: (p * side + x, y * 2 + c)),
+        "y": (y, side, lambda o: lat_ref.at[pl.ds(o * 2, 2)], lambda p: (z * side + x, p * 2 + c)),
+        "c": (c, 2, lambda o: lat_ref.at[y * 2 + o], lambda p: (z * side + x, y * 2 + p)),
+    }
+
+    def each(kind, turn, step, act, sending):
+        name, s = step
+        pos, size, block, device = lines[name]
+
+        def copy(way, owner, target):
+            return pltpu.make_async_remote_copy(
+                src_ref=block(owner),
+                dst_ref=block(owner),
+                send_sem=send_sems.at[kind, turn, way],
+                recv_sem=recv_sems.at[kind, turn, way],
+                device_id=device(target),
+                device_id_type=MESH_ID,
+            )
+
+        if size == 2:
+            act(copy(0, pos if sending else 1 - pos, 1 - pos))
+            return
+        if sending:
+            ways = (
+                (0, (pos >= s) & (pos + 1 < size), pos - s, pos + 1),
+                (1, (pos + s < size) & (pos >= 1), pos + s, pos - 1),
+            )
+        else:
+            ways = (
+                (0, pos - 1 >= s, pos - 1 - s, pos - 1),
+                (1, pos + 1 + s < size, pos + 1 + s, pos + 1),
+            )
+        for way, valid, owner, target in ways:
+
+            @pl.when(valid)
+            def _(way=way, owner=owner, target=target):
+                act(copy(way, owner, target))
+
+    both = share_steps(place.depth, side)
+    for turn in range(max(len(steps) for steps in both)):
+        for act, sending in (
+            (lambda copy: copy.start(), True),
+            (lambda copy: copy.wait_send(), True),
+            (lambda copy: copy.wait_recv(), False),
+        ):
+            for kind, steps in enumerate(both):
+                if turn < len(steps):
+                    each(kind, turn, steps[turn], act, sending)
 
 
 def dot(a, b):
@@ -456,13 +578,13 @@
 
 def train_kernel(
     at, depth, side, horizon, bins, lin, obs_ref, extra_ref, info_ref, bias_ref, mine_ref,
-    all_ref, parts_ref, d_obs_ref, *scratch,
+    all_ref, parts_ref, d_obs_ref, sum_ref, batch_ref, lat_ref, *scratch,
 ):
-    (small, small32, lat_bias, xa, xat, w1d, w2d, lo, stage, enc_hat, enc_slope, enc_hid, enc_inv,
+    (small, small32, lat_bias, xa, xat, lo, enc_hat, enc_slope, enc_hid, enc_inv,
      d1_hat, d1_slope, d1_hid, d1_inv, d2_hat, d2_slope, d2_hid, d2_inv, encoded, predicted,
      w1, w2, vo, hat1, slope1, hid1, inv1, hat2, slope2, hid2, inv2, d_logits, pre,
      dx, g1, g2, gv, d_lin, sums, d_small, d_small_low, d_bias, load_sems, store_sems, first_sems, last_sems,
-     own_sem, gather_send_sems, gather_recv_sems) = scratch
+     own_sem, gather_send_sems, gather_recv_sems, share_send_sems, share_recv_sems) = scratch[:-12]
     f32, bf16 = jnp.float32, jnp.bfloat16
     rows = xa.shape[0]
     seqs = rows // horizon
@@ -482,13 +604,15 @@
 
         lax.fori_loop(0, at.batches, one, 0)
 
-    def move_head(k, first, second, third, sems, load):
+    def move_head(k, first, second, third, sems, load, only=None):
         base = at.head_at(k)
 
         def body(b, l, where):
             cols = pl.ds(l * at.cols, at.cols)
 
             def one(which, start, count, here, *lanes):
+                if only is not None and which != only:
+                    return
                 there = (all_ref if load else parts_ref).at[(*where, rows_of(0, count, base + start), *lanes)]
                 pair = (there, here) if load else (here, there)
                 pltpu.make_async_copy(*pair, sems.at[which]).start()
@@ -520,9 +644,12 @@
 
         for_blocks(body)
 
-    def move_out(n, sem, load):
+    def stage_place(b, l):
+        return rows_of(b, at.out_rows), slice(l * at.cols, (l + 1) * at.cols)
+
+    def move_out(n, stage, sem, load):
         def body(b, l, where):
-            here = stage.at[b * at.lats + l]
+            here = stage.at[stage_place(b, l)]
             there = (all_ref if load else parts_ref).at[
                 (*where, pl.ds(at.out_at(n), at.out_rows))
             ]
@@ -530,11 +657,15 @@
 
         for_blocks(body)
 
-    def stage_to_out(n):
+    def wait_out(stage, sem):
+        ref = stage.at[: at.batches * at.out_rows]
+        pltpu.make_async_copy(ref, ref, sem).wait()
+
+    def stage_to_out(n, stage):
         def body(b):
             block_rows = rows_of(b, at.middle_rows)
             for l in range(at.lats):
-                values = stage[b * at.lats + l].astype(f32)
+                values = stage[stage_place(b, l)].astype(f32)
                 half, quarter = at.middle_rows // 2, at.middle_rows // 4
                 left = jnp.concatenate([values[:half, : 2 * unit], values[:half, 2 * unit :]], 0)
                 right = jnp.concatenate(
@@ -546,7 +677,7 @@
 
         loop(at.batches, body)
 
-    def out_to_stage(hid, total):
+    def out_to_stage(hid, total, stage):
         many = max(1, 128 // at.middle_rows)
 
         def body(n):
@@ -561,7 +692,7 @@
                     right = jnp.concatenate(
                         [values[m * quarter : (m + 1) * quarter, 2 * unit :] for m in range(4)], 1
                     )
-                    stage[(n * many + p) * at.lats + l] = jnp.concatenate([left, right], 0).astype(bf16)
+                    stage[stage_place(n * many + p, l)] = jnp.concatenate([left, right], 0).astype(bf16)
 
         loop(at.batches // many, body)
 
@@ -632,28 +763,49 @@
     )
     gather.own.start()
     place.barrier()
-    entry = at.head_at(1) // chunk_rows + len(gather.steps)
+    before = at.head_at(1) // chunk_rows
+    entry = before + len(gather.steps)
     ticks = iter(range(entry, entry + ENTRY_TICKS))
 
     def tick_body(t, carry):
-        gather.tick(t)
+        gather.tick(t, 0, before, 1)
+        gather.tick(t, before, gather.chunks, LAG)
         return carry
 
     lax.fori_loop(0, entry, tick_body, 0)
 
     def tick():
-        gather.tick(next(ticks))
+        gather.tick(next(ticks), before, gather.chunks, LAG)
+
+    chunks = at.total // chunk_rows
+    head_chunks = head_rows // chunk_rows
+    in_heads = chunks - before
+
+    def row_of(n):
+        m = n - in_heads
+        m = jnp.where(m == head_chunks - 1, head_chunks, jnp.where(m == head_chunks, head_chunks - 1, m))
+        return jnp.where(n < in_heads, n + before, m) * chunk_rows
+
+    scatter = Scatter(place, chunks, chunk_rows, row_of, parts_ref, sum_ref, scratch[-12:])
+
+    def scatter_ticks(first, last):
+        def one(n, carry):
+            scatter.tick(n)
+            return carry
+
+        lax.fori_loop(first, last, one, 0)
 
     move_small(small, first_sems.at[0], True)
-    move_out(0, first_sems.at[1], True)
-    move_head(0, w1d, w2d, None, first_sems.at[pl.ds(2, 3)], True)
+    move_out(0, g2, first_sems.at[1], True)
+    move_out(1, g1, first_sems.at[2], True)
+    move_head(0, w1, w2, vo, load_sems, True)
     d_small[...] = jnp.zeros_like(d_small)
     dx[...] = jnp.zeros_like(dx)
     ids = info_ref[:seqs, ID_AT : ID_AT + 1]
     lanes = lax.broadcasted_iota(jnp.int32, (seqs, 128), 1).astype(f32)
     task_hot = (lanes == ids).astype(f32)
-    wait_head(w1d, w2d, None, first_sems.at[pl.ds(2, 3)])
-    embedded = task_rows(info_ref, w1d)
+    wait_head(w1, w2, vo, load_sems)
+    embedded = task_rows(info_ref, w1)
     for t in range(horizon):
         part = slice(t * seqs, (t + 1) * seqs)
         xa[part, latent:] = (embedded + extra_ref[part, :].astype(f32)).astype(bf16)
@@ -663,9 +815,8 @@
         lat_bias[0:2, l * 3 * unit : (l + 1) * 3 * unit] = small32[
             BIAS_AT : BIAS_AT + 2, l * at.cols : l * at.cols + 3 * unit
         ]
-    pltpu.make_async_copy(stage, stage, first_sems.at[1]).wait()
-    stage_to_out(0)
-    move_out(1, first_sems.at[1], True)
+    wait_out(g2, first_sems.at[1])
+    stage_to_out(0, g2)
 
     big_dot(pre, all_rows, obs_ref[...], small)
     tick()
@@ -678,17 +829,17 @@
     simnorm_forward(all_rows, 0, encoded)
     tick()
     xa[:seqs, :latent] = encoded[:seqs, :].astype(bf16)
-    pltpu.make_async_copy(stage, stage, first_sems.at[1]).wait()
-    stage_to_out(1)
+    wait_out(g1, first_sems.at[2])
+    stage_to_out(1, g1)
 
     gain1, shift1 = gain_row(1)
     gain2, shift2 = gain_row(2)
     for t in range(horizon):
         part = slice(t * seqs, (t + 1) * seqs)
-        big_dot(pre, seqs, xa[part, :], w1d)
+        big_dot(pre, seqs, xa[part, :], w1)
         norm_forward(pre, seqs, t * seqs, gain1, shift1, d1_hat, d1_slope, d1_hid, d1_inv)
         tick()
-        big_dot(pre, seqs, d1_hid[part, :], w2d)
+        big_dot(pre, seqs, d1_hid[part, :], w2)
         norm_forward(pre, seqs, t * seqs, gain2, shift2, d2_hat, d2_slope, d2_hid, d2_inv)
         tick()
         big_dot(pre, seqs, d2_hid[part, :], lo.at[1])
@@ -696,7 +847,8 @@
         simnorm_forward(seqs, t * seqs, predicted)
         if t + 1 < horizon:
             xa[(t + 1) * seqs : (t + 2) * seqs, :latent] = predicted[part, :].astype(bf16)
-    move_head(1, w1.at[0], w2.at[0], vo.at[0], load_sems.at[0], True)
+    for which in range(3):
+        move_head(1, w1, w2, vo, load_sems, True, which)
     for n in range(xa.shape[1] // 128):
         xat[n * 128 : (n + 1) * 128, :] = xa[:, n * 128 : (n + 1) * 128].T
 
@@ -705,31 +857,38 @@
     acts = lin // 2
 
     def head(k):
-        slot = lax.rem(k - 1, 2)
-        wait_head(w1.at[slot], w2.at[slot], vo.at[slot], load_sems.at[slot])
+        wait_head(w1, w2, vo, load_sems)
+        following = lax.rem(k + 1, heads)
         first_tick = entry + ENTRY_TICKS + (k - 1) * HEAD_TICKS
 
         def tick(n):
             @pl.when(first_tick + n < gather.ticks)
             def _():
-                gather.tick(first_tick + n)
+                gather.tick(first_tick + n, before, gather.chunks, LAG)
+
+            if n > 1:
+
+                @pl.when(k > 1)
+                def _():
+                    scatter.tick((k - 2) * head_chunks + (n - 2))
 
         gain1, shift1 = gain_row(2 * k + 1)
         gain2, shift2 = gain_row(2 * k + 2)
-        big_dot(pre, rows, xa[...], w1.at[slot])
+        big_dot(pre, rows, xa[...], w1)
         tick(0)
+
+        @pl.when(k > 1)
+        def _():
+            wait_head(g1, g2, gv, store_sems)
+
         norm_forward(pre, rows, 0, gain1, shift1, hat1, slope1, hid1, inv1)
         tick(1)
-        big_dot(pre, rows, hid1[...], w2.at[slot])
+        big_dot(pre, rows, hid1[...], w2)
         tick(2)
         norm_forward(pre, rows, 0, gain2, shift2, hat2, slope2, hid2, inv2)
         tick(3)
 
-        @pl.when(k + 1 < heads)
-        def _():
-            move_head(k + 1, w1.at[1 - slot], w2.at[1 - slot], vo.at[1 - slot], load_sems.at[1 - slot], True)
-
-        pre[:rows, :128] = dot(hid2[...], vo[slot]) + bias_ref[pl.ds(k, 1), :]
+        pre[:rows, :128] = dot(hid2[...], vo[...]) + bias_ref[pl.ds(k, 1), :]
         clear_sums()
 
         def loss(n):
@@ -769,23 +928,21 @@
 
         loop(rows // LOSS_ROWS, loss)
         d_bias[pl.ds(k - 1, 1), :] = jnp.sum(sums[0, 0, :, :128], 0, keepdims=True)
-        big_dot(pre, rows, d_logits[...], vo.at[slot], dot_t)
+        big_dot(pre, rows, d_logits[...], vo, dot_t)
+        move_head(following, w1, w2, vo, load_sems, True, 2)
         clear_sums()
         norm_backward(pre, rows, 0, gain2, hat2, slope2, inv2, hat2, sums.at[0])
         tick(4)
         keep_sums(2 * k + 2)
-        big_dot(pre, rows, hat2[...], w2.at[slot], dot_t)
+        big_dot(pre, rows, hat2[...], w2, dot_t)
+        move_head(following, w1, w2, vo, load_sems, True, 1)
         clear_sums()
         norm_backward(pre, rows, 0, gain1, hat1, slope1, inv1, hat1, sums.at[0])
         tick(5)
         keep_sums(2 * k + 1)
         for n in range(dx.shape[1] // 128):
-            dx[:, n * 128 : (n + 1) * 128] += dot_t(hat1[...], w1[slot, n * 128 : (n + 1) * 128, :])
-
-        @pl.when(k > 1)
-        def _():
-            wait_head(g1, g2, gv, store_sems)
-
+            dx[:, n * 128 : (n + 1) * 128] += dot_t(hat1[...], w1[n * 128 : (n + 1) * 128, :])
+        move_head(following, w1, w2, vo, load_sems, True, 0)
         gv[...] = t_dot(hid2[...], d_logits[...]).astype(bf16)
         weight_grads(hid1, hat2, hat1)
         move_head(k, g1, g2, gv, store_sems, False)
@@ -810,6 +967,9 @@
 
     assert next(ticks, None) is None
     gather.drain()
+    wait_head(g1, g2, gv, store_sems)
+    wait_head(w1, w2, vo, load_sems)
+    done = in_heads - head_chunks
 
     scale = 2.0 * 20.0 / latent
 
@@ -836,19 +996,24 @@
             return grad
 
         simnorm_backward(seqs, t * seqs, predicted, grad_of, t * seqs)
+        if t > 0:
+            scatter_ticks(done, done + 1)
+            done += 1
         big_dot(pre, seqs, d_lin[part, :], lo.at[1], dot_t)
         norm_backward(pre, seqs, t * seqs, gain2, d2_hat, d2_slope, d2_inv, d2_hat, sums.at[2])
-        big_dot(pre, seqs, d2_hat[part, :], w2d, dot_t)
+        if done < in_heads:
+            scatter_ticks(done, done + 1)
+            done += 1
+        big_dot(pre, seqs, d2_hat[part, :], w2, dot_t)
         norm_backward(pre, seqs, t * seqs, gain1, d1_hat, d1_slope, d1_inv, d1_hat, sums.at[1])
         for n in range(dx.shape[1] // 128):
             cols = slice(n * 128, (n + 1) * 128)
-            dx[part, cols] += dot_t(d1_hat[part, :], w1d[cols, :])
+            dx[part, cols] += dot_t(d1_hat[part, :], w1[cols, :])
     keep_bias(1)
     keep_sums(1, 1)
     keep_sums(2, 2)
-    out_to_stage(d2_hid, rows)
-    move_out(1, last_sems.at[0], False)
-    wait_head(g1, g2, gv, store_sems)
+    out_to_stage(d2_hid, rows, w2)
+    move_out(1, w2, last_sems.at[0], False)
     weight_grads(d1_hid, d2_hat, d1_hat)
     move_head(0, g1, g2, None, store_sems, False)
 
@@ -858,10 +1023,15 @@
         simnorm_backward(
             seqs, (t + 1) * seqs, encoded, lambda n, cols, t=t: -pull(t, n, cols), (t + 1) * seqs
         )
+    wait_head(g1, g2, None, store_sems)
+    wait_out(w2, last_sems.at[0])
+    scatter_ticks(done, done + 1)
     keep_bias(0)
     clear_sums()
     big_dot(pre, all_rows, d_lin[...], lo.at[0], dot_t)
+    scatter_ticks(done + 1, done + 2)
     norm_backward(pre, all_rows, 0, gain_row(0)[0], enc_hat, enc_slope, enc_inv, enc_hat, sums.at[0])
+    scatter_ticks(done + 2, done + 3)
     keep_sums(0)
     d_obs_ref[...] = dot_t(enc_hat[...], small[...])
     for n in range(hidden // 256):
@@ -883,12 +1053,27 @@
             ]
     d_small_low[...] = d_small[...].astype(bf16)
     move_small(d_small_low, last_sems.at[1], False)
-    pltpu.make_async_copy(stage, stage, last_sems.at[0]).wait()
-    out_to_stage(enc_hid, all_rows)
-    move_out(0, last_sems.at[0], False)
-    wait_head(g1, g2, None, store_sems)
+    scatter_ticks(done + 3, done + 4)
+    out_to_stage(enc_hid, all_rows, w1)
+    move_out(0, w1, last_sems.at[0], False)
     pltpu.make_async_copy(d_small_low, d_small_low, last_sems.at[1]).wait()
-    pltpu.make_async_copy(stage, stage, last_sems.at[0]).wait()
+    wait_out(w1, last_sems.at[0])
+    scatter_ticks(done + 4, scatter.ticks)
+
+    batch, lat = lax.axis_index("batch"), lax.axis_index("lat")
+    action_rows = []
+    for k in range(heads):
+        tail = sum_ref[pl.ds(at.head_at(k) + at.task_at, at.tail_rows), :].astype(f32)
+        action_rows.append(tail[at.task_rows : at.task_rows + 1])
+        if k > 0:
+            value = pl.ds(at.head_at(k) + at.value_at, at.value_rows)
+            lat_ref[lat, (k - 1) * at.value_rows : k * at.value_rows, :] = sum_ref[value, :]
+    batch_ref[batch, : at.value_rows, :] = sum_ref[
+        pl.ds(at.head_at(0) + at.value_at, at.value_rows), :
+    ]
+    action_rows.append(jnp.zeros((16 - heads, at.cols), f32))
+    batch_ref[batch, at.value_rows :, :] = jnp.concatenate(action_rows, 0).astype(bf16)
+    share(place, batch_ref, lat_ref, share_send_sems, share_recv_sems)
 
 
 def train(at, depth, side, dims, obs, extra, info, bias, mine):
@@ -915,19 +1100,19 @@
             jax.ShapeDtypeStruct((2, side, side, depth, *mine.shape), bf16),
             jax.ShapeDtypeStruct((2, side, side, depth, *mine.shape), bf16),
             jax.ShapeDtypeStruct((all_rows, 128), f32),
+            jax.ShapeDtypeStruct(mine.shape, bf16),
+            jax.ShapeDtypeStruct((at.batches, at.value_rows + 16, at.cols), bf16),
+            jax.ShapeDtypeStruct((at.lats, (at.heads - 1) * at.value_rows, at.cols), bf16),
         ],
-        in_specs=[vmem, vmem, vmem, vmem, hbm],
-        out_specs=[hbm, hbm, vmem],
+        in_specs=[vmem] * 5,
+        out_specs=[hbm, hbm] + [vmem] * 4,
         scratch_shapes=[
             pltpu.VMEM((128, hidden), bf16),
             pltpu.VMEM((128, hidden), f32),
             pltpu.VMEM((8, latent), f32),
             pltpu.VMEM((rows, wide), bf16),
             pltpu.VMEM((wide, rows), bf16),
-            pltpu.VMEM((wide, hidden), bf16),
-            pltpu.VMEM((hidden, hidden), bf16),
             pltpu.VMEM((2, hidden, latent), bf16),
-            pltpu.VMEM((at.batches * at.lats, at.out_rows, at.cols), bf16),
         ]
         + saved(all_rows)
         + saved(rows)
@@ -935,9 +1120,9 @@
         + [
             pltpu.VMEM((all_rows, latent), f32),
             pltpu.VMEM((rows, latent), f32),
-            pltpu.VMEM((2, wide, hidden), bf16),
-            pltpu.VMEM((2, hidden, hidden), bf16),
-            pltpu.VMEM((2, hidden, 128), bf16),
+            pltpu.VMEM((wide, hidden), bf16),
+            pltpu.VMEM((hidden, hidden), bf16),
+            pltpu.VMEM((hidden, 128), bf16),
         ]
         + saved(rows)
         + saved(rows)
@@ -953,19 +1138,22 @@
             pltpu.VMEM((128, hidden), f32),
             pltpu.VMEM((128, hidden), bf16),
             pltpu.VMEM((8, 128), f32),
-            pltpu.SemaphoreType.DMA((2, 3)),
             pltpu.SemaphoreType.DMA((3,)),
-            pltpu.SemaphoreType.DMA((5,)),
+            pltpu.SemaphoreType.DMA((3,)),
+            pltpu.SemaphoreType.DMA((3,)),
             pltpu.SemaphoreType.DMA((2,)),
             pltpu.SemaphoreType.DMA,
             pltpu.SemaphoreType.DMA((gather_count, 2, at.total // at.chunk_rows)),
             pltpu.SemaphoreType.DMA((gather_count, 2, at.total // at.chunk_rows)),
-        ],
+            pltpu.SemaphoreType.DMA((2, depth + side, 2)),
+            pltpu.SemaphoreType.DMA((2, depth + side, 2)),
+        ]
+        + scatter_scratch(depth, side, at.total // at.chunk_rows, at.chunk_rows, at.cols, bf16),
         compiler_params=pltpu.CompilerParams(
-            collective_id=1, has_side_effects=True, vmem_limit_bytes=62 * 2**20
+            collective_id=1, has_side_effects=True, vmem_limit_bytes=VMEM_LIMIT
         ),
         name="train",
-    )(obs, extra, info, bias, mine)[1:]
+    )(obs, extra, info, bias, mine)[2:]
 
 
 def round_up(n, to):
@@ -1071,18 +1259,16 @@
     return jnp.concatenate([heads[0], tail[1], tail[0], heads[1:].reshape(-1, at.cols)], 0)
 
 
-def unpack_own(at, total, dims):
+def unpack_own(at, total, over_batch, over_lat, dims):
     split = at.head_at(1)
     heads = jnp.concatenate([total[: at.head_rows], total[split:]], 0)
-    heads = heads.reshape(at.heads, at.head_rows, at.cols)
-    outs = total[at.head_rows : split].reshape(2, at.out_rows, at.cols)[::-1]
-    part = heads[:, at.value_at : at.value_at + at.value_rows].astype(jnp.bfloat16)
-    action = heads[:, at.task_at + at.task_rows].astype(jnp.bfloat16)
-    split_over_lat = lax.all_gather(jnp.concatenate([part[0], action], 0), "batch", axis=0)
-    split_over_lat = split_over_lat.astype(jnp.float32)
+    heads = heads.reshape(at.heads, at.head_rows, at.cols).astype(jnp.float32)
+    outs = total.astype(jnp.float32)[at.head_rows : split].reshape(2, at.out_rows, at.cols)[::-1]
+    split_over_lat = over_batch.astype(jnp.float32)
     small = split_over_lat[:, : at.value_rows].reshape(-1, at.cols)
-    action = split_over_lat[: at.acts, at.value_rows :].transpose(1, 0, 2)[: at.heads - 1]
-    out = widen(at, lax.all_gather(part[1:], "lat", axis=0).astype(jnp.float32))
+    action = split_over_lat[: at.acts, at.value_rows : at.value_rows + at.heads].transpose(1, 0, 2)[: at.heads - 1]
+    out = over_lat.reshape(at.lats, at.heads - 1, at.value_rows, at.cols)
+    out = widen(at, out.astype(jnp.float32))
     out = out.transpose(1, 0, 2, 3).reshape(at.heads - 1, at.middle_rows, 128)
     tr, tc = at.table_shape
     table = small[TABLE_AT : TABLE_AT + 16].reshape(16, at.pieces, 128).transpose(1, 0, 2)
@@ -1155,10 +1341,9 @@
         ],
         0,
     )
-    parts, d_obs = train(at, depth, side, dims, obs, extra, info, bias, mine)
-    total = scatter_sum(parts, depth, side, at.total // at.chunk_rows)
+    d_obs, total, over_batch, over_lat = train(at, depth, side, dims, obs, extra, info, bias, mine)
     grad_observations = d_obs[:, :obs_dim].reshape(horizon + 1, seqs, obs_dim).transpose(1, 0, 2)
-    return (grad_observations,) + unpack_own(at, total, dims)
+    return (grad_observations,) + unpack_own(at, total, over_batch, over_lat, dims)
 
 
 def solution(mesh):

time: 702 us -> 470 us (0.67)
  Pallas kernels: 621 us -> 427 us
  blocking collectives: 36.2 us -> 0 us
    pallas_call x1 -> x0, Pallas kernels: 174 us -> none  [scatter_sum(): pl.pallas_call(functools.partial(scatter_kernel, depth, side, chunks, chu...]
    all_gather x2 -> x0, blocking collectives: 36.2 us -> none  [the longest x1 30.5 us: unpack_own(): lax.all_gather(jnp.concatenate([part[0], action], 0), 'batch', axis=0)]
    pallas_call x1, Pallas kernels: 447 us -> 427 us  [train(): pl.pallas_call(functools.partial(train_kernel, at, depth, side, dims['hor...]
where the time goes in v4:
time: 470 us; the launch traced here: 463 us
  Pallas kernels  427 us (91%)
  local copies, waits for them, and re-layouts  24.9 us (5%)
  other arithmetic  9.55 us (2%)
    pallas_call x1, Pallas kernels, train(): pl.pallas_call(functools.partial(train_kernel, at, depth, side, dims['hor...  427 us

profile of v4, /device:TPU:0, one launch (start us, length us, event | category | flops | bytes accessed | tf_op | source)
XLA Modules:
  0.0 463.0 jit_solution(10894123154481421376)
XLA Ops:
  0.7 0.7 convert_element_type.112
  1.4 0.8 select_reduce_fusion
  2.3 0.8 remainder_convert_fusion
  3.4 0.7 convert_bitcast_fusion.1
  4.2 0.7 convert_bitcast_fusion
  4.9 1.3 fusion.21.bias_ref
  6.2 0.8 reshape.165
  7.1 0.7 fusion.17
  7.8 0.7 copy.126
  8.7 0.7 bitcast_convert_fusion
  9.6 0.7 copy.132
  10.4 0.8 copy.131
  11.2 0.8 copy.133
  12.0 1.0 fusion.27
  13.5 1.0 fusion.26
  14.9 0.8 copy.140.extra_ref
  15.9 0.7 pad.57.clone
  17.0 0.7 pad.59.info_ref
  18.2 1.1 pad_maximum_fusion.mine_ref
  19.3 427.3 %train.1 = (bf16[2,2,2,4,2240,256]{5,4,3,2,1,0:T(8,128)(2,1)}, bf16[2,2,2,4,2240,256]{5,4,3,2,1,0:T(8,128)(2,1)}, f32[768,128]{1,0:T(8,128)}, bf16[2240,256]{1,0...) custom-call(bf16[768,128]{1,0:T(8,128)(2,1)} %bitcast.66, bf16[576,128]{1,0:T(8,128)(2,1)} %copy.140.extra_ref, ...), custom_call_target="tpu_custom_call" | custom-call | tf_op jit(solution)/shard_map/train/pallas_call | solution.py:1097
  446.6 2.0 copy.141
  448.5 0.7 slice.214
  449.3 0.7 copy.155
  450.0 0.9 slice.159
  450.9 0.8 slice.197
  454.1 0.9 convert_element_type.122
  455.7 0.9 slice.172
  456.8 0.7 copy.152
  458.2 0.8 maximum_maximum_fusion
  459.2 0.9 copy.153
  460.8 1.0 slice.205
  461.8 1.1 slice.209
  (86 shorter events, 7.5 us)
Async XLA Ops:
  0.6 16.0 %copy-start.4 = (bf16[6,128,101]{1,2,0:T(8,128)(2,1)S(1)}, bf16[6,128,101]{1,2,0:T(8,128)(2,1)}, u32[]{:S(2)}) copy-start(bf16[6,128,101]{1,2,0:T(8,128)(2,1)} %param.32) | copy-start | bytes 465412
  0.7 15.0 %copy-start.5 = (bf16[192,4,39]{0,1,2:T(4,128)(2,1)S(1)}, bf16[192,4,39]{0,1,2:T(4,128)(2,1)}, u32[]{:S(2)}) copy-start(bf16[192,4,39]{0,1,2:T(4,128)(2,1)} %param.20) | copy-start | bytes 179716
  13.1 4.7 %copy-start.2 = (bf16[8,128,256]{2,1,0:T(8,128)(2,1)S(1)}, bf16[8,128,256]{2,1,0:T(8,128)(2,1)}, u32[]{:S(2)}) copy-start(bf16[8,128,256]{2,1,0:T(8,128)(2,1)} %param.31) | copy-start | bytes 1572868
  13.1 4.7 %copy-start.3 = (bf16[8,96,256]{2,1,0:T(8,128)(2,1)S(1)}, bf16[8,96,256]{2,1,0:T(8,128)(2,1)}, u32[]{:S(2)}) copy-start(bf16[8,96,256]{2,1,0:T(8,128)(2,1)} %param.28) | copy-start | bytes 1179652
  446.6 10.0 %copy-start = (bf16[2240,256]{1,0:T(8,128)(2,1)S(1)}, bf16[2240,256]{1,0:T(8,128)(2,1)}, u32[]{:S(2)}) copy-start(bf16[2240,256]{1,0:T(8,128)(2,1)} %get-tuple-element.21) | copy-start | bytes 3440644
  452.4 4.4 copy-start.6
  456.8 2.3 copy-start.1

commit v5 on v4

--- a/solution.py
+++ b/solution.py
@@ -12,7 +12,7 @@
 HIGHEST = lax.Precision.HIGHEST
 NORM_ROWS = 192
 SOFT_ROWS = 192
-LOSS_ROWS = 192
+LOSS_ROWS = 576
 GAIN_AT = 40
 SHIFT_AT = 64
 BIAS_AT = 88
@@ -24,9 +24,10 @@
 ID_AT = 15
 HIGH_AT = 16
 LOW_AT = 17
-ENTRY_TICKS = 10
-HEAD_TICKS = 6
-LAG = 2
+PROLOGUE_TICKS = 2
+ENTRY_SITES = (0, 1, 2, 4, 6, 8)
+HEAD_TICKS = 3
+LAG = 1
 SCATTER_LAG = 2
 VMEM_LIMIT = 62 * 2**20
 
@@ -96,14 +97,17 @@
 
 
 class Gather:
-    def __init__(self, place, chunks, chunk_rows, mine_ref, all_ref, own_sem, send_sems, recv_sems):
-        self.place, self.chunks, self.chunk_rows = place, chunks, chunk_rows
+    def __init__(
+        self, place, base, chunks, chunk_rows, lag, mine_ref, all_ref, own, send_sems, recv_sems, order=None
+    ):
+        self.order = order or (lambda t: t)
+        self.place, self.base, self.chunks, self.chunk_rows, self.lag = place, base, chunks, chunk_rows, lag
         self.mine_ref, self.all_ref = mine_ref, all_ref
         self.send_sems, self.recv_sems = send_sems, recv_sems
         self.steps = gather_steps(place.depth, place.side)
-        self.ticks = chunks + LAG * len(self.steps)
+        self.ticks = chunks + lag * len(self.steps)
         self.dims = {name: (pos, size, at) for name, pos, size, at in place.dims()}
-        self.own = pltpu.make_async_copy(mine_ref, all_ref.at[place.c, place.i, place.j, place.z], own_sem)
+        self.own = own
 
     def block(self, name, owner, rows):
         place = self.place
@@ -126,7 +130,7 @@
     def each(self, which, t, act, sending):
         name, s = self.steps[which]
         place = self.place
-        rows = pl.ds(pl.multiple_of(t * self.chunk_rows, 16), self.chunk_rows)
+        rows = pl.ds(pl.multiple_of(self.base + self.order(t) * self.chunk_rows, 16), self.chunk_rows)
         if name == "c":
             core = place.c if sending else 1 - place.c
             ref = self.all_ref.at[core, :, :, :, rows]
@@ -156,17 +160,17 @@
                 source = self.mine_ref.at[rows] if sending and name == "z" and s == 0 else ref
                 act(self.copy(which, t, way, source, ref, at(target)))
 
-    def tick(self, t, first, last, lag):
+    def tick(self, t):
         for which in range(len(self.steps) + 1):
-            self.one(t - lag * which, which, first, last)
-
-    def one(self, at, which, first, last):
-        @pl.when((at >= first) & (at < last))
+            self.one(t - self.lag * which, which)
+
+    def one(self, at, which):
+        @pl.when((at >= 0) & (at < self.chunks))
         def _():
             if which > 0:
                 self.each(which - 1, at, lambda c: c.wait_recv(), False)
             if which < len(self.steps):
-                if which == self.place.depth - 1:
+                if which == self.place.depth - 1 and self.own is not None:
 
                     @pl.when(at == 0)
                     def _():
@@ -758,24 +762,49 @@
 
     place = Place(depth, side)
     chunk_rows = at.chunk_rows
+    own = pltpu.make_async_copy(mine_ref, all_ref.at[place.c, place.i, place.j, place.z], own_sem)
+    before = at.head_at(1) // chunk_rows
+
+    def encoder_first(t):
+        late = jnp.where(t == 6, 4, t - 3)
+        return jnp.where(t == 0, 3, jnp.where(t < 3, t + 4, late))
+
+    first_part = Gather(
+        place, 0, before, chunk_rows, 1, mine_ref, all_ref, own,
+        gather_send_sems.at[:, :, pl.ds(0, before)], gather_recv_sems.at[:, :, pl.ds(0, before)],
+        encoder_first,
+    )
     gather = Gather(
-        place, at.total // chunk_rows, chunk_rows, mine_ref, all_ref, own_sem, gather_send_sems, gather_recv_sems
+        place, at.head_at(1), (at.heads - 1) * 2, head_rows // 2, LAG, mine_ref, all_ref, None,
+        gather_send_sems.at[:, :, pl.ds(before, (at.heads - 1) * 2)],
+        gather_recv_sems.at[:, :, pl.ds(before, (at.heads - 1) * 2)],
     )
-    gather.own.start()
+    own.start()
     place.barrier()
-    before = at.head_at(1) // chunk_rows
-    entry = before + len(gather.steps)
-    ticks = iter(range(entry, entry + ENTRY_TICKS))
+    early = PROLOGUE_TICKS
+    opening = 3 + len(first_part.steps)
 
     def tick_body(t, carry):
-        gather.tick(t, 0, before, 1)
-        gather.tick(t, before, gather.chunks, LAG)
+        first_part.tick(t)
+        back = t - (opening - 2 * early)
+
+        @pl.when((back >= 0) & (lax.rem(back, 2) == 0))
+        def _():
+            gather.tick(lax.div(back, 2))
+
         return carry
 
-    lax.fori_loop(0, entry, tick_body, 0)
+    lax.fori_loop(0, opening, tick_body, 0)
+    sites = iter(range(100))
+    ticks = iter(range(early, early + len(ENTRY_SITES)))
+    first_ticks = iter(range(opening, first_part.ticks))
 
     def tick():
-        gather.tick(next(ticks), before, gather.chunks, LAG)
+        n = next(first_ticks, None)
+        if n is not None:
+            first_part.tick(n)
+        if next(sites) in ENTRY_SITES:
+            gather.tick(next(ticks))
 
     chunks = at.total // chunk_rows
     head_chunks = head_rows // chunk_rows
@@ -797,18 +826,11 @@
 
     move_small(small, first_sems.at[0], True)
     move_out(0, g2, first_sems.at[1], True)
-    move_out(1, g1, first_sems.at[2], True)
-    move_head(0, w1, w2, vo, load_sems, True)
     d_small[...] = jnp.zeros_like(d_small)
     dx[...] = jnp.zeros_like(dx)
     ids = info_ref[:seqs, ID_AT : ID_AT + 1]
     lanes = lax.broadcasted_iota(jnp.int32, (seqs, 128), 1).astype(f32)
     task_hot = (lanes == ids).astype(f32)
-    wait_head(w1, w2, vo, load_sems)
-    embedded = task_rows(info_ref, w1)
-    for t in range(horizon):
-        part = slice(t * seqs, (t + 1) * seqs)
-        xa[part, latent:] = (embedded + extra_ref[part, :].astype(f32)).astype(bf16)
     pltpu.make_async_copy(small, small, first_sems.at[0]).wait()
     small32[...] = small[...].astype(f32)
     for l in range(at.lats):
@@ -829,6 +851,14 @@
     simnorm_forward(all_rows, 0, encoded)
     tick()
     xa[:seqs, :latent] = encoded[:seqs, :].astype(bf16)
+    assert next(first_ticks, None) is None
+    move_head(0, w1, w2, vo, load_sems, True)
+    move_out(1, g1, first_sems.at[2], True)
+    wait_head(w1, w2, vo, load_sems)
+    embedded = task_rows(info_ref, w1)
+    for t in range(horizon):
+        part = slice(t * seqs, (t + 1) * seqs)
+        xa[part, latent:] = (embedded + extra_ref[part, :].astype(f32)).astype(bf16)
     wait_out(g1, first_sems.at[2])
     stage_to_out(1, g1)
 
@@ -847,6 +877,9 @@
         simnorm_forward(seqs, t * seqs, predicted)
         if t + 1 < horizon:
             xa[(t + 1) * seqs : (t + 2) * seqs, :latent] = predicted[part, :].astype(bf16)
+    ready = max(early + len(ENTRY_SITES), 2 + LAG * len(gather.steps))
+    for n in range(early + len(ENTRY_SITES), ready):
+        gather.tick(n)
     for which in range(3):
         move_head(1, w1, w2, vo, load_sems, True, which)
     for n in range(xa.shape[1] // 128):
@@ -859,12 +892,14 @@
     def head(k):
         wait_head(w1, w2, vo, load_sems)
         following = lax.rem(k + 1, heads)
-        first_tick = entry + ENTRY_TICKS + (k - 1) * HEAD_TICKS
+        first_tick = ready + (k - 1) * HEAD_TICKS
 
         def tick(n):
-            @pl.when(first_tick + n < gather.ticks)
-            def _():
-                gather.tick(first_tick + n, before, gather.chunks, LAG)
+            if n % 2 == 0 and n // 2 < HEAD_TICKS:
+
+                @pl.when(first_tick + n // 2 < gather.ticks)
+                def _():
+                    gather.tick(first_tick + n // 2)
 
             if n > 1:
 
@@ -966,6 +1001,7 @@
     lax.fori_loop(1, heads, heads_body, 0)
 
     assert next(ticks, None) is None
+    first_part.drain()
     gather.drain()
     wait_head(g1, g2, gv, store_sems)
     wait_head(w1, w2, vo, load_sems)
@@ -1259,39 +1295,80 @@
     return jnp.concatenate([heads[0], tail[1], tail[0], heads[1:].reshape(-1, at.cols)], 0)
 
 
+def unpack_kernel(
+    at, bins, lin, total_ref, batch_ref, lat_ref, enc_ref, out_ref, latent_ref, action_ref, task_ref,
+    middle_ref, value_ref, policy_ref, gain_ref, shift_ref, bias_ref, rest_ref,
+):
+    f32 = jnp.float32
+    half, quarter, unit = at.middle_rows // 2, at.middle_rows // 4, at.cols // 4
+    for k in range(at.heads):
+        base = at.head_at(k)
+        latent_ref[k] = total_ref[base : base + at.latent_rows, :].astype(f32)
+        middle_ref[k] = total_ref[base + at.middle_at : base + at.value_at, :].astype(f32)
+        tail = total_ref[base + at.task_at : base + at.head_rows, :].astype(f32)
+        task_ref[k] = tail[: at.task_rows]
+    for n in range(2):
+        values = total_ref[at.out_at(n) : at.out_at(n) + at.out_rows, :].astype(f32)
+        left = jnp.concatenate([values[:half, : 2 * unit], values[:half, 2 * unit :]], 0)
+        right = jnp.concatenate([values[half:, m * unit : (m + 1) * unit] for m in range(4)], 0)
+        out_ref[n] = jnp.concatenate([left, right], 1)
+    for k in range(at.heads - 1):
+        for l in range(at.lats):
+            values = lat_ref[l, k * at.value_rows : (k + 1) * at.value_rows, :].astype(f32)
+            for n in range(at.pieces):
+                rows = slice(l * at.share + n * at.value_rows, l * at.share + (n + 1) * at.value_rows)
+                if k < at.heads - 2:
+                    value_ref[k, rows, :] = values[:, n * 128 : n * 128 + bins]
+                else:
+                    policy_ref[rows, :] = values[:, n * 128 : n * 128 + lin]
+    small = jnp.concatenate(
+        [batch_ref[b].astype(f32)[: at.value_rows] for b in range(at.batches)], 0
+    )
+    enc_ref[...] = small[: at.obs]
+    gain_ref[...] = small[GAIN_AT : GAIN_AT + at.norms]
+    shift_ref[...] = small[SHIFT_AT : SHIFT_AT + at.norms]
+    bias_ref[...] = small[BIAS_AT : BIAS_AT + 2, : at.latent_cols]
+    rest_ref[...] = small[TABLE_AT:]
+    for b in range(at.acts):
+        block = batch_ref[b].astype(f32)[at.value_rows : at.value_rows + at.heads]
+        for k in range(at.heads - 1):
+            action_ref[k, b : b + 1, :] = block[k : k + 1]
+
+
 def unpack_own(at, total, over_batch, over_lat, dims):
-    split = at.head_at(1)
-    heads = jnp.concatenate([total[: at.head_rows], total[split:]], 0)
-    heads = heads.reshape(at.heads, at.head_rows, at.cols).astype(jnp.float32)
-    outs = total.astype(jnp.float32)[at.head_rows : split].reshape(2, at.out_rows, at.cols)[::-1]
-    split_over_lat = over_batch.astype(jnp.float32)
-    small = split_over_lat[:, : at.value_rows].reshape(-1, at.cols)
-    action = split_over_lat[: at.acts, at.value_rows : at.value_rows + at.heads].transpose(1, 0, 2)[: at.heads - 1]
-    out = over_lat.reshape(at.lats, at.heads - 1, at.value_rows, at.cols)
-    out = widen(at, out.astype(jnp.float32))
-    out = out.transpose(1, 0, 2, 3).reshape(at.heads - 1, at.middle_rows, 128)
+    bins, lin = dims["bins"], dims["lin"]
+    shapes = [
+        (at.obs, at.cols),
+        (2, at.middle_rows, at.latent_cols),
+        (at.heads, at.latent_rows, at.cols),
+        (at.heads - 1, at.acts, at.cols),
+        (at.heads, at.task_rows, at.cols),
+        (at.heads, at.middle_rows, at.cols),
+        (at.heads - 2, at.middle_rows, bins),
+        (at.middle_rows, lin),
+        (at.norms, at.cols),
+        (at.norms, at.cols),
+        (2, at.latent_cols),
+        (128 - TABLE_AT, at.cols),
+    ]
+    vmem = pl.BlockSpec(memory_space=pltpu.VMEM)
+    outs = pl.pallas_call(
+        functools.partial(unpack_kernel, at, bins, lin),
+        out_shape=[jax.ShapeDtypeStruct(shape, jnp.float32) for shape in shapes],
+        in_specs=[vmem] * 3,
+        out_specs=[vmem] * len(shapes),
+        compiler_params=pltpu.CompilerParams(vmem_limit_bytes=24 * 2**20),
+        name="unpack",
+    )(total, over_batch, over_lat)
+    rest = outs[-1]
     tr, tc = at.table_shape
-    table = small[TABLE_AT : TABLE_AT + 16].reshape(16, at.pieces, 128).transpose(1, 0, 2)
+    table = rest[:16].reshape(16, at.pieces, 128).transpose(1, 0, 2)
     table = table.reshape(tc // at.task_rows, at.tail_rows, 128)[:, : at.task_rows].reshape(tc, 128)
     table = lax.dynamic_slice_in_dim(table, lax.axis_index("batch") * tr, tr, 1).T
-    wide = small[WIDE_AT : WIDE_AT + at.wide_rows].reshape(at.wide_rows, at.pieces, 128)
+    first = WIDE_AT - TABLE_AT
+    wide = rest[first : first + at.wide_rows].reshape(at.wide_rows, at.pieces, 128)
     wide = wide.transpose(1, 0, 2).reshape(8, 128)
-    return (
-        small[: at.obs],
-        out_unpack(at, outs),
-        heads[:, : at.latent_rows],
-        action,
-        heads[:, at.task_at : at.task_at + at.task_rows],
-        heads[:, at.middle_at : at.value_at],
-        out[:-1, :, : dims["bins"]],
-        out[-1, :, : dims["lin"]],
-        table,
-        small[GAIN_AT : GAIN_AT + at.norms],
-        small[SHIFT_AT : SHIFT_AT + at.norms],
-        small[BIAS_AT : BIAS_AT + 2, : at.latent_cols],
-        wide[: at.heads - 2, : dims["bins"]],
-        wide[at.heads - 2, : dims["lin"]],
-    )
+    return (*outs[:8], table, *outs[8:11], wide[: at.heads - 2, :bins], wide[at.heads - 2, :lin])
 
 
 def local(

time: 470 us -> 460 us (0.979)
    slice x22 -> x1, local copies, waits for them, and re-layouts: 7.46 us -> 0.01 us  [unpack_own(): rest[first:first + at.wide_rows].reshape(at.wide_rows, at.pieces, 128)]
    pallas_call x1, Pallas kernels: 427 us -> 421 us  [train(): pl.pallas_call(functools.partial(train_kernel, at, depth, side, dims['hor...]
    unnamed x35 -> x33, local copies, waits for them, and re-layouts: 6.83 us -> 10.9 us
where the time goes in v5:
time: 460 us; the launch traced here: 452 us
  Pallas kernels  423 us (92%)
  local copies, waits for them, and re-layouts  20.8 us (5%)
  other arithmetic  7.67 us (2%)
    pallas_call x1, Pallas kernels, train(): pl.pallas_call(functools.partial(train_kernel, at, depth, side, dims['hor...  421 us
    unnamed x33, local copies, waits for them, and re-layouts  10.9 us

profile of v5, /device:TPU:0, one launch (start us, length us, event | category | flops | bytes accessed | tf_op | source)
XLA Modules:
  0.0 452.3 jit_solution(8923130626550179606)
XLA Ops:
  0.7 0.7 convert_element_type.96
  1.4 0.8 select_reduce_fusion
  2.3 0.8 remainder_convert_fusion
  3.4 0.7 convert_bitcast_fusion.1
  4.2 0.7 convert_bitcast_fusion
  4.9 1.3 fusion.21.bias_ref
  6.2 0.8 reshape.145
  7.1 0.7 fusion.17
  7.8 0.7 copy.111
  8.7 0.7 bitcast_convert_fusion
  9.6 0.7 copy.117
  10.4 0.9 copy.116
  11.3 0.8 copy.118
  12.1 1.0 fusion.23
  13.6 1.0 fusion.22
  14.9 0.8 copy.125.extra_ref
  15.9 0.7 pad.57.clone
  17.1 0.7 pad.59.info_ref
  18.3 1.1 pad_maximum_fusion.mine_ref
  19.3 421.4 %train.1 = (bf16[2,2,2,4,2240,256]{5,4,3,2,1,0:T(8,128)(2,1)}, bf16[2,2,2,4,2240,256]{5,4,3,2,1,0:T(8,128)(2,1)}, f32[768,128]{1,0:T(8,128)}, bf16[2240,256]{1,0...) custom-call(bf16[768,128]{1,0:T(8,128)(2,1)} %bitcast.44, bf16[576,128]{1,0:T(8,128)(2,1)} %copy.125.extra_ref, ...), custom_call_target="tpu_custom_call" | custom-call | tf_op jit(solution)/shard_map/train/pallas_call | solution.py:1133
  440.7 1.9 copy.126
  442.6 1.3 copy-done
  443.9 0.9 copy-done.1
  444.8 0.9 copy-done.2
  445.7 1.3 unpack.1
  447.1 0.7 copy.134
  447.8 0.5 slice_bitcast_fusion.4
  448.3 0.7 copy.133
  449.0 0.6 copy.130
  449.6 0.7 copy.131
  450.3 0.8 copy.129
  451.1 0.9 copy.132
  (58 shorter events, 2.9 us)
Async XLA Ops:
  0.6 16.0 %copy-start.5 = (bf16[6,128,101]{1,2,0:T(8,128)(2,1)S(1)}, bf16[6,128,101]{1,2,0:T(8,128)(2,1)}, u32[]{:S(2)}) copy-start(bf16[6,128,101]{1,2,0:T(8,128)(2,1)} %param.32) | copy-start | bytes 465412
  0.7 15.1 %copy-start.6 = (bf16[192,4,39]{0,1,2:T(4,128)(2,1)S(1)}, bf16[192,4,39]{0,1,2:T(4,128)(2,1)}, u32[]{:S(2)}) copy-start(bf16[192,4,39]{0,1,2:T(4,128)(2,1)} %param.20) | copy-start | bytes 179716
  10.4 7.4 %copy-start.3 = (bf16[8,128,256]{2,1,0:T(8,128)(2,1)S(1)}, bf16[8,128,256]{2,1,0:T(8,128)(2,1)}, u32[]{:S(2)}) copy-start(bf16[8,128,256]{2,1,0:T(8,128)(2,1)} %param.31) | copy-start | bytes 1572868
  10.4 7.4 %copy-start.4 = (bf16[8,96,256]{2,1,0:T(8,128)(2,1)S(1)}, bf16[8,96,256]{2,1,0:T(8,128)(2,1)}, u32[]{:S(2)}) copy-start(bf16[8,96,256]{2,1,0:T(8,128)(2,1)} %param.28) | copy-start | bytes 1179652
  442.6 1.3 copy-start
  443.8 0.9 copy-start.1
  444.8 0.9 copy-start.2
  447.8 4.2 copy-start.7
